TPU v7x, 32 devices: a whole 2x2x4 slice. The times are simulated.
32 devices in a mesh: stream: 2 (over core), batch: 16 (over z, y, x).
Axes of the slice: x: 2, y: 2, z: 4, core: 2. Of those that a mesh axis runs over, the one named last changes fastest.
Arguments:
- tokens: bfloat16 [2, 16384, 768], P('stream', 'batch'), may hold values from -6 to 6
- lengths: int32 [2, 16, 8], P('stream', 'batch'), may hold values from 0 to 512, as said below
- attn_weight: float32 [4, 768, 768], P(None, 'batch', 'stream'), may hold values from -0.8660254 to 0.8660254
- attn_moment: float32 [4, 768, 768], P(None, 'batch', 'stream'), may hold values from -7168 to 7168
- attn_average: float32 [4, 768, 768], P(None, 'batch', 'stream'), may hold values from -0.21875 to 0.21875
- up_weight: float32 [768, 3072], P('batch', 'stream'), may hold values from -0.21875 to 0.21875
- up_moment: float32 [768, 3072], P('batch', 'stream'), may hold values from -3072 to 3072
- up_average: float32 [768, 3072], P('batch', 'stream'), may hold values from -0.21875 to 0.21875
- down_weight: float32 [3072, 768], P('batch', 'stream'), may hold values from -0.109375 to 0.109375
- down_moment: float32 [3072, 768], P('batch', 'stream'), may hold values from -4096 to 4096
- down_average: float32 [3072, 768], P('batch', 'stream'), may hold values from -0.109375 to 0.109375
- layer_vectors: float32 [8, 768], P('stream', 'batch'), may hold values from -0.4 to 1.4
- vector_moment: float32 [8, 768], P('stream', 'batch'), may hold values from -10240 to 10240
- vector_average: float32 [8, 768], P('stream', 'batch'), may hold values from -3 to 3
- up_bias: float32 [3072], P(('stream', 'batch')), may hold values from -0.625 to 0.625
- bias_moment: float32 [3072], P(('stream', 'batch')), may hold values from -4096 to 4096
- bias_average: float32 [3072], P(('stream', 'batch')), may hold values from -0.625 to 0.625
- pos_table: float32 [512, 768], P('stream', 'batch'), may hold values from -3 to 3
- pos_moment: float32 [512, 768], P('stream', 'batch'), may hold values from -5120 to 5120
- pos_average: float32 [512, 768], P('stream', 'batch'), may hold values from -3 to 3
Outputs:
- block_out: bfloat16 [2, 16384, 768], P('stream', 'batch')
- input_grad: float32 [2, 16384, 768], P('stream', 'batch')
- attn_grad: float32 [4, 768, 768], P(None, 'batch', 'stream')
- attn_moment_new: float32 [4, 768, 768], P(None, 'batch', 'stream')
- attn_weight_new: float32 [4, 768, 768], P(None, 'batch', 'stream')
- attn_average_new: float32 [4, 768, 768], P(None, 'batch', 'stream')
- up_grad: float32 [768, 3072], P('batch', 'stream')
- up_moment_new: float32 [768, 3072], P('batch', 'stream')
- up_weight_new: float32 [768, 3072], P('batch', 'stream')
- up_average_new: float32 [768, 3072], P('batch', 'stream')
- down_grad: float32 [3072, 768], P('batch', 'stream')
- down_moment_new: float32 [3072, 768], P('batch', 'stream')
- down_weight_new: float32 [3072, 768], P('batch', 'stream')
- down_average_new: float32 [3072, 768], P('batch', 'stream')
- vector_grad: float32 [8, 768], P('stream', 'batch')
- vector_moment_new: float32 [8, 768], P('stream', 'batch')
- vector_new: float32 [8, 768], P('stream', 'batch')
- vector_average_new: float32 [8, 768], P('stream', 'batch')
- bias_grad: float32 [3072], P(('stream', 'batch'))
- bias_moment_new: float32 [3072], P(('stream', 'batch'))
- bias_new: float32 [3072], P(('stream', 'batch'))
- bias_average_new: float32 [3072], P(('stream', 'batch'))
- pos_grad: float32 [512, 768], P('stream', 'batch')
- pos_moment_new: float32 [512, 768], P('stream', 'batch')
- pos_new: float32 [512, 768], P('stream', 'batch')
- pos_average_new: float32 [512, 768], P('stream', 'batch')
Inputs may be any that keep to these rules, and one draw needn't show every extreme that they name: `lengths`: for each pair index the two towers have the same number c of used slots, either 2 or 8; the used slots come first, the others are 0; a used slot's length lies between half of and all of 1024 // c, and one used slot of every device is full; in every draw some pair index has c = 2 and some has c = 8.
All inputs are finite; a program needn't handle non-finite values.
Results may differ from a plain program's by a relative error of at most 0.0075.
The roundings to bfloat16 on the way count: a program that leaves them out, or rounds other values in their place, can miss the bound.
Values may be sent and summed in bfloat16 or wider, within the bound.
No kernel may reach another device: no remote copies, remote signals or barrier semaphores. Data moves between devices by JAX's collectives and lax.ppermute only.
A program may use at most 192 MiB of HBM per device.

v0:
```python
import functools
import math

import jax
import jax.numpy as jnp
from jax import lax
from jax.experimental import pallas as pl
from jax.experimental.pallas import tpu as pltpu
from jax.sharding import PartitionSpec as P

HEADS = 12


EPS_NORM = 1e-06
INV_TEMP = 100.0
LOSS_WEIGHT = 256.0
MOMENTUM = 0.5
AVERAGE = 0.5
RATE = 0.0001
POS_RATE = 0.01
NEGATIVE = -1e30
ROOT_HALF = 0.7071067811865476
ROOT_TWO_PI = 2.5066282746310002
LANES = 128
SLOT_COUNT, LENGTHS = 4, 5
CHUNK, BLOCKS = 256, 3
COST = pl.CostEstimate(flops=1000, bytes_accessed=1000, transcendentals=0)
LONG_COST = pl.CostEstimate(flops=10**12, bytes_accessed=10**9, transcendentals=0)
ANYWHERE = pl.BlockSpec(memory_space=pl.ANY)
NN = (((1,), (0,)), ((), ()))
NT = (((1,), (1,)), ((), ()))
TN = (((0,), (0,)), ((), ()))


def halved(values):
    return values.astype(jnp.bfloat16)


def matmul(left, right, dims=NN):
    return lax.dot_general(left, right, dims, preferred_element_type=jnp.float32)


def stacked(*shape, dtype=jnp.float32):
    return jax.ShapeDtypeStruct(shape, dtype)


def after(value, *earlier):
    return lax.optimization_barrier((value, earlier))[0]


def exchanged(block, axis, mask):
    count = lax.axis_size(axis)
    return lax.ppermute(block, axis, [(place, place ^ mask) for place in range(count)])


def scalars(lengths_row):
    batch = lax.axis_index("batch")
    places = [lax.axis_index("stream"), batch & 1, (batch >> 1) & 1, batch >> 2]
    counted = jnp.sum((lengths_row > 0).astype(jnp.int32))
    return jnp.concatenate([jnp.stack(places + [counted]), lengths_row]).astype(jnp.int32)


class Gather:
    def __init__(self, block, cut):
        self.cut = cut
        self.bits = lax.axis_size("batch").bit_length() - 1
        self.blocks, self.masks = block[None], [0]

    def far(self, *earlier):
        bit = self.bits
        while bit > 2:
            step = min(2, bit - 2)
            bit -= step
            offsets = [d << bit for d in range(1 << step)]
            arrived = [exchanged(self.blocks, "batch", offset) for offset in offsets[1:]]
            own = after(self.blocks, *earlier) if earlier else self.blocks
            self.blocks = jnp.concatenate([own] + arrived, axis=0)
            self.masks = [offset | mask for offset in offsets for mask in self.masks]
        self.sides = [self.blocks[:, :, : self.cut], self.blocks[:, :, self.cut :]]
        self.masks = [self.masks, self.masks]

    def near(self, flips, *earlier):
        for side, flip in enumerate(flips):
            part = self.sides[side]
            own = after(part, *earlier) if earlier else part
            self.sides[side] = jnp.concatenate([own, exchanged(part, "batch", flip)], axis=0)
            self.masks[side] = self.masks[side] + [flip | mask for mask in self.masks[side]]

    def placed(self, at, pieces, shapes):
        sources, moves = [], []
        for other in range(2):
            for side, part in enumerate(self.sides):
                sources.append(exchanged(part, "stream", 1) if other else part)
                base = self.cut * side
                for start, stop, target, lead, offset, span in pieces:
                    low, high = max(start, base), min(stop, base + part.shape[2])
                    if low >= high:
                        continue
                    for entry, mask in enumerate(self.masks[side]):
                        moves.append(
                            (len(sources) - 1, entry, mask, (low - base, high - base), target, lead,
                             other, offset + low - start, span)
                        )
        return placed(at, sources, moves, shapes)


def place_kernel(moves, count, at_ref, *refs):
    sources, targets = refs[:count], refs[count:]
    stream = at_ref[0]
    batch = at_ref[1] + 2 * at_ref[2] + 4 * at_ref[3]
    for source, entry, mask, columns, target, lead, other, start, span in moves:
        core = stream ^ other
        low = pl.multiple_of(start + core * span, LANES) if span else start
        at = (batch ^ mask, slice(None), pl.ds(low, columns[1] - columns[0]))
        if lead == "relative":
            at = (other,) + at
        elif lead == "stream":
            at = (core,) + at
        targets[target][at] = sources[source][entry, :, columns[0] : columns[1]]


def placed(at, sources, moves, shapes):
    held = pl.BlockSpec(memory_space=pltpu.VMEM)
    return pl.pallas_call(
        functools.partial(place_kernel, moves, len(sources)),
        in_specs=[pl.BlockSpec(memory_space=pltpu.SMEM)] + [held] * len(sources),
        out_specs=[held] * len(shapes),
        out_shape=shapes,
        compiler_params=pltpu.CompilerParams(vmem_limit_bytes=20 << 20),
        cost_estimate=COST,
    )(at, *sources)


def two_words(values):
    half = values.shape[-1] // 2
    coarse = values.astype(jnp.bfloat16).astype(jnp.float32)
    lane = lax.broadcasted_iota(jnp.int32, values.shape, values.ndim - 1)
    rest = jnp.concatenate([(values - coarse)[..., half:], (values - coarse)[..., :half]], axis=-1)
    return jnp.where(lane < half, coarse, rest)


def one_word(block):
    half = block.shape[-1] // 2
    return block + jnp.concatenate([block[..., half:], block[..., :half]], axis=-1)


def received(block, wide):
    values = block.astype(jnp.float32)
    if not wide:
        return values
    return jnp.concatenate(
        [values[..., :-LANES], one_word(values[..., -LANES:])], axis=-1
    )


def sent(values, wide):
    if not wide:
        return halved(values)
    return jnp.concatenate(
        [halved(values[..., :-LANES]), halved(two_words(values[..., -LANES:]))], axis=-1
    )


def piece_specs(side, piece, away):
    array, arrived, rows, row_at, columns, column_at, flip = piece

    def spec(column, turn):
        def index(z, at):
            place = z ^ (turn(at[0]) * (array.shape[0] // 2)) if flip else z
            bit = at[1 + side] ^ (1 if away else 0)
            return (place, 0, bit, row_at, column) if side == 0 else (place, bit, 0, row_at, column)

        return pl.BlockSpec((1, 2, 1, rows, columns) if side == 0 else (1, 1, 2, rows, columns), index)

    return [spec(column_at, lambda core: core), spec(column_at, lambda core: 1 - core)]


def fold_call(kernel, count, at, ins, in_specs, outs, out_specs):
    size = sum(math.prod(o.shape) for o in outs) * 8
    return pl.pallas_call(
        kernel,
        grid_spec=pltpu.PrefetchScalarGridSpec(
            num_scalar_prefetch=1, grid=(count,), in_specs=in_specs, out_specs=out_specs
        ),
        out_shape=outs,
        compiler_params=pltpu.CompilerParams(vmem_limit_bytes=16 << 20),
        cost_estimate=COST,
    )(at, *ins)


class Fold:
    def __init__(self, at, sides, wide=False):
        self.at, self.sides, self.wide = at, sides, (False, wide)
        self.count = sides[0][0][0].shape[0]
        self.rows = [side[0][2] for side in sides]
        self.columns = [sum(piece[4] for piece in side) for side in sides]

    def piece_values(self, refs, side, pick):
        columns = []
        for k in range(len(self.sides[side])):
            wide = self.wide[side] and k == len(self.sides[side]) - 1
            arrived = pick(refs[2 * k + 1]).astype(jnp.float32)
            columns.append(pick(refs[2 * k]) + (one_word(arrived) if wide else arrived))
        return jnp.concatenate(columns, axis=-1)

    def first_kernel(self, at_ref, *refs):
        place = 0
        for side, pieces in enumerate(self.sides):
            out = refs[side - 2]
            for which in range(2):
                values = self.piece_values(
                    refs[place:], side, lambda r: r[0, which, 0] if side == 0 else r[0, 0, which]
                )
                out[0, which] = sent(values, self.wide[side])
            place += 2 * len(pieces)

    def first(self):
        ins, in_specs = [], []
        for side, pieces in enumerate(self.sides):
            for piece in pieces:
                ins += piece[:2]
                in_specs += piece_specs(side, piece, True)
        outs = [stacked(self.count, 2, r, c, dtype=jnp.bfloat16) for r, c in zip(self.rows, self.columns)]
        out_specs = [pl.BlockSpec((1,) + o.shape[1:], lambda z, at: (z, 0, 0, 0)) for o in outs]
        return fold_call(self.first_kernel, self.count, self.at, ins, in_specs, outs, out_specs)

    def first_sent(self, parts):
        return [exchanged(part, "batch", 1 << side) for side, part in enumerate(parts)]

    def second_kernel(self, at_ref, *refs):
        place = 0
        outs = refs[-4:]
        for side, pieces in enumerate(self.sides):
            arrays = refs[place : place + 2 * len(pieces)]
            arrived = refs[place + 2 * len(pieces)]
            place += 2 * len(pieces) + 1
            bit = at_ref[2 - side]
            for which, out in ((1 - bit, outs[2 * side]), (bit, outs[2 * side + 1])):
                values = self.piece_values(
                    arrays, side, lambda r: r[0, which, 0] if side == 0 else r[0, 0, which]
                )
                values = values + received(arrived[0, which], self.wide[side])
                out[0] = sent(values, self.wide[side]) if out.dtype == jnp.bfloat16 else values

    def second(self, arrived):
        ins, in_specs, outs = [], [], []
        for side, pieces in enumerate(self.sides):
            for piece in pieces:
                ins += piece[:2]
                in_specs += piece_specs(side, piece, False)
            ins.append(arrived[side])
            in_specs.append(pl.BlockSpec((1,) + arrived[side].shape[1:], lambda z, at: (z, 0, 0, 0)))
            shape = (self.count, self.rows[side], self.columns[side])
            outs += [stacked(*shape, dtype=jnp.bfloat16), stacked(*shape)]
        out_specs = [pl.BlockSpec((1,) + o.shape[1:], lambda z, at: (z, 0, 0)) for o in outs]
        return fold_call(self.second_kernel, self.count, self.at, ins, in_specs, outs, out_specs)

    def second_sent(self, out):
        return [exchanged(out[0], "batch", 2), exchanged(out[2], "batch", 1)], [out[1], out[3]]

    def third_kernel(self, radix, at_ref, keep0, keep1, in0, in1, *outs):
        mine = at_ref[3] % radix
        for d, out in enumerate(outs):
            which = mine ^ d
            column = 0
            for side, (keep, arrived) in enumerate(((keep0, in0), (keep1, in1))):
                wide = self.wide[side]
                values = keep[which] + received(arrived[which], wide)
                width = values.shape[-1]
                out[0, :, column : column + width] = values if d == 0 else sent(values, wide)
                column += width

    def third(self, arrived, kept):
        radix = min(4, self.count)
        ins = kept + arrived
        in_specs = [pl.BlockSpec((radix,) + a.shape[1:], lambda z, at: (z, 0, 0)) for a in ins]
        shape = (self.count // radix, self.rows[0], sum(self.columns))
        outs = [stacked(*shape)] + [stacked(*shape, dtype=jnp.bfloat16)] * (radix - 1)
        out_specs = [pl.BlockSpec((1,) + o.shape[1:], lambda z, at: (z, 0, 0)) for o in outs]
        return fold_call(
            functools.partial(self.third_kernel, radix), self.count // radix, self.at, ins, in_specs, outs, out_specs
        )

    def third_sent(self, out):
        radix = min(4, self.count)
        terms = [out[0]] + [exchanged(part, "batch", 4 * d) for d, part in enumerate(out) if d > 0]
        total = None
        for term in terms:
            value = received(term, self.wide[1]) if term.dtype == jnp.bfloat16 else term
            total = value if total is None else total + value
        bit = 2 + radix.bit_length() - 1
        while total.shape[0] > 1:
            total = total.reshape((total.shape[0] // 2, 2) + total.shape[1:])
            upper = (lax.axis_index("batch") >> bit) & 1
            away = sent(lax.dynamic_index_in_dim(total, 1 - upper, 1, keepdims=False), False)
            total = lax.dynamic_index_in_dim(total, upper, 1, keepdims=False)
            total = total + exchanged(away, "batch", 1 << bit).astype(jnp.float32)
            bit += 1
        return total[0]


def attend_kernel(at, q_ref, k_ref, v_ref, context_ref, turned_ref, prob_ref, bias):
    half = pl.program_id(1)

    @pl.when(pl.program_id(0) == 0)
    def _():
        span = q_ref.shape[0]
        key = lax.broadcasted_iota(jnp.int32, (span, 1), 0) + half * span
        query = lax.broadcasted_iota(jnp.int32, (1, span), 1) + half * span
        bits = (2 * span).bit_length() - 1
        key_slot = (key * at[SLOT_COUNT]) >> bits
        query_slot = (query * at[SLOT_COUNT]) >> bits
        length = jnp.zeros((span, 1), jnp.int32)
        for slot in range(at.shape[0] - LENGTHS):
            length += jnp.where(key_slot == slot, at[LENGTHS + slot], 0)
        present = key - key_slot * bucket_of(at, 2 * span) < length
        code = jnp.where(present, key_slot, -1)
        bias[half] = jnp.where(code == query_slot, 0.0, NEGATIVE)

    rows, lanes = q_ref.shape
    size = lanes // 2
    first = lax.broadcasted_iota(jnp.int32, (rows, lanes), 1) < size
    keys = k_ref[...]
    none = jnp.zeros_like(keys)
    masked = (jnp.where(first, keys, none), jnp.where(first, none, keys))
    values = v_ref[...].T
    queries = q_ref[...] * jnp.bfloat16(1.0 / math.sqrt(size))
    outs = []
    for h in range(2):
        scores = matmul(masked[h], queries, NT) + bias[half]
        weights = jnp.exp(scores - jnp.max(scores, axis=0, keepdims=True))
        probs = halved(weights * (1.0 / jnp.sum(weights, axis=0, keepdims=True)))
        prob_ref[0, 0, h] = probs
        outs.append(matmul(values[h * size : (h + 1) * size], probs))
    context = jnp.concatenate(outs, axis=0)
    turned_ref[...] = halved(context)
    context_ref[...] = halved(context.T)


def natural(pairs, i, at):
    return ((i // (pairs // 2)) ^ at[0]) * (pairs // 2) + i % (pairs // 2)


def attend(at, triples):
    tokens, wide = triples.shape[1:]
    width = wide // 3 * 2
    rows, pairs = tokens // 2, width // LANES
    own = pairs // 2

    def part(p):
        return pl.BlockSpec((None, rows, LANES), lambda i, j, at: (i // own, j, p * own + i % own))

    return pl.pallas_call(
        attend_kernel,
        grid_spec=pltpu.PrefetchScalarGridSpec(
            num_scalar_prefetch=1,
            grid=(pairs, 2),
            in_specs=[
                part(0),
                part(1),
                part(2),
            ],
            out_specs=[
                pl.BlockSpec((rows, LANES), lambda i, j, at: (j, natural(pairs, i, at))),
                pl.BlockSpec((LANES, rows), lambda i, j, at: (natural(pairs, i, at), j)),
                pl.BlockSpec((1, 1, 2, rows, rows), lambda i, j, at: (i, j, 0, 0, 0)),
            ],
            scratch_shapes=[pltpu.VMEM((2, rows, rows), jnp.float32)],
        ),
        out_shape=[
            stacked(tokens, width, dtype=jnp.bfloat16),
            stacked(width, tokens, dtype=jnp.bfloat16),
            stacked(pairs, 2, 2, rows, rows, dtype=jnp.bfloat16),
        ],
        compiler_params=pltpu.CompilerParams(vmem_limit_bytes=56 << 20),
        cost_estimate=COST,
    )(at, triples, triples, triples)


def attend_back_kernel(at, q_ref, k_ref, v_ref, context_ref, grad_ref, prob_ref, out_ref, sum_ref):
    rows, lanes = q_ref.shape
    size = lanes // 2
    scale = jnp.bfloat16(1.0 / math.sqrt(size))
    first = lax.broadcasted_iota(jnp.int32, (rows, lanes), 1) < size
    queries = q_ref[...] * scale
    keys = (k_ref[...] * scale).T
    values, grads = v_ref[...], grad_ref[...]
    none = jnp.zeros_like(values)
    masked = (jnp.where(first, values, none), jnp.where(first, none, values))
    products = (grads.astype(jnp.float32) * context_ref[...].astype(jnp.float32)).T
    dquery, dkey, dvalue = [], [], []
    for h in range(2):
        here = slice(h * size, (h + 1) * size)
        rowdot = jnp.sum(products[here], axis=0, keepdims=True)
        probs = prob_ref[0, 0, h]
        dprob = matmul(masked[h], grads, NT)
        dscore = halved(probs.astype(jnp.float32) * (dprob - rowdot))
        dkey.append(matmul(dscore, queries))
        dvalue.append(matmul(probs, grads))
        dquery.append(matmul(keys[here], dscore))
    dquery = jnp.concatenate(dquery, axis=0).T
    dkey = jnp.where(first, dkey[0], dkey[1])
    dvalue = jnp.where(first, dvalue[0], dvalue[1])
    pair = pl.program_id(2)
    quarter = out_ref.shape[2] // 3
    low = pl.multiple_of(pair * lanes, lanes)
    for p, part in enumerate((dquery, dkey, dvalue)):
        out_ref[0, :, pl.ds(p * quarter + low, lanes)] = halved(part)

    @pl.when((pl.program_id(1) == 0) & (pair == 0))
    def _():
        sum_ref[...] = jnp.zeros_like(sum_ref)

    sum_ref[0, 0, :, pl.ds(low, lanes)] += jnp.sum(dquery, axis=0, keepdims=True)
    sum_ref[0, 1, :, pl.ds(low, lanes)] += jnp.sum(dvalue, axis=0, keepdims=True)


def attend_back(at, triples, context, grad, probs):
    tokens, width = context.shape
    rows, pairs = tokens // 2, width // LANES
    own = pairs // 2

    def part(p):
        return pl.BlockSpec((None, rows, LANES), lambda r, j, i, at: (r, j, p * own + i))

    whole = pl.BlockSpec((rows, LANES), lambda r, j, i, at: (j, natural(pairs, r * own + i, at)))
    return pl.pallas_call(
        attend_back_kernel,
        grid_spec=pltpu.PrefetchScalarGridSpec(
            num_scalar_prefetch=1,
            grid=(2, 2, own),
            in_specs=[
                part(0),
                part(1),
                part(2),
                whole,
                whole,
                pl.BlockSpec((1, 1, 2, rows, rows), lambda r, j, i, at: (r * own + i, j, 0, 0, 0)),
            ],
            out_specs=[
                pl.BlockSpec((1, rows, triples.shape[2]), lambda r, j, i, at: (r, j, 0)),
                pl.BlockSpec((1, 2, 1, width // 2), lambda r, j, i, at: (r, 0, 0, 0)),
            ],
        ),
        out_shape=[stacked(*triples.shape, dtype=jnp.bfloat16), stacked(2, 2, 1, width // 2)],
        compiler_params=pltpu.CompilerParams(vmem_limit_bytes=56 << 20),
        cost_estimate=LONG_COST,
    )(at, triples, triples, triples, context, grad, probs)


def bucket_of(at, token_count):
    return jnp.where(at[SLOT_COUNT] == 2, token_count // 2, token_count // (at.shape[0] - LENGTHS))


def group_slot(at, group, token_count):
    slots = at.shape[0] - LENGTHS
    span = token_count // slots
    slot = (group * at[SLOT_COUNT]) // slots
    place = lax.broadcasted_iota(jnp.int32, (span, 1), 0) + group * span
    live = place - slot * bucket_of(at, token_count) < at[LENGTHS + slot]
    return slot, live.astype(jnp.float32)


def whole_block(array):
    return pl.BlockSpec(array.shape, lambda *_: (0,) * len(array.shape))


def kernel_call(kernel, grid, at, ins, in_specs, outs, out_specs, scratch=(), long=False, vmem=56):
    return pl.pallas_call(
        kernel,
        grid_spec=pltpu.PrefetchScalarGridSpec(
            num_scalar_prefetch=1, grid=grid, in_specs=in_specs, out_specs=out_specs,
            scratch_shapes=scratch,
        ),
        out_shape=outs,
        compiler_params=pltpu.CompilerParams(vmem_limit_bytes=vmem << 20),
        cost_estimate=LONG_COST if long else COST,
    )(at, *ins)


def entry_kernel(at, tokens, pos, weight, shift, hidden0, entry, triples, table):
    step = pl.program_id(0)
    rows = tokens.shape[0]

    @pl.when(step == 0)
    def _():
        long = pos[...].astype(jnp.float32).T
        count = long.shape[0]
        span = 2 * count // (at.shape[0] - LENGTHS)
        short = jnp.concatenate([long[:span]] * (count // span), axis=0)
        table[...] = jnp.where(at[SLOT_COUNT] == 2, long, short)

    half_steps = pl.num_programs(0) // 2
    here = pl.ds(pl.multiple_of((step % half_steps) * rows, rows), rows)
    values = tokens[...].astype(jnp.float32) + table[here]
    hidden0[...] = values
    values = halved(values)
    entry[...] = values.T
    for other in range(2):
        triples[other] = halved(matmul(values, weight[other]) + shift[other])


def entered(at, tokens, pos, qkv, shift):
    token_count, width = tokens.shape
    triple = qkv.shape[2]
    outs = [
        stacked(token_count, width),
        stacked(width, token_count, dtype=jnp.bfloat16),
        stacked(2, token_count, triple, dtype=jnp.bfloat16),
    ]
    return kernel_call(
        entry_kernel,
        (token_count // CHUNK,),
        at,
        [tokens, pos, qkv, shift],
        tiles(tokens) + [held(pos), held(qkv), held(shift)],
        outs,
        tiles(outs[0], outs[1]) + [pl.BlockSpec((2, CHUNK, triple), lambda i, at: (0, i, 0))],
        [pltpu.VMEM((token_count // 2, width), jnp.float32)],
    )


BO, B2, G1, E1, G2, E2 = 2, 3, 4, 5, 6, 7


def normal(values):
    center = values - jnp.mean(values, axis=-1, keepdims=True)
    inverse = lax.rsqrt(jnp.mean(center * center, axis=-1, keepdims=True) + EPS_NORM)
    return center * inverse, inverse


def held(array):
    return pl.BlockSpec(
        array.shape, lambda *_: (0,) * len(array.shape), pipeline_mode=pl.Buffered(buffer_count=1)
    )


def tiles(*arrays):
    return [
        pl.BlockSpec((CHUNK, a.shape[1]), lambda i, at: (i, 0))
        if a.shape[0] == arrays[0].shape[0]
        else pl.BlockSpec((a.shape[0], CHUNK), lambda i, at: (0, i))
        for a in arrays
    ]


def weight_copies(at, up, down, up_held, down_held, sems):
    half, quarter = down.shape[1] // 2, down.shape[2]
    copies = [pltpu.make_async_copy(up, up_held, sems.at[0])]
    for other in range(2):
        start = pl.multiple_of((other ^ at[0]) * half, half)
        for k in range(2):
            copies.append(
                pltpu.make_async_copy(
                    down.at[k, pl.ds(start, half)],
                    down_held.at[pl.ds(other * half, half), pl.ds(k * quarter, quarter)],
                    sems.at[1 + 2 * other + k],
                )
            )
    return copies[:1], copies[1:]


def weight_scratch(up, down):
    return [
        pltpu.VMEM(up.shape, jnp.bfloat16),
        pltpu.VMEM((down.shape[1], 2 * down.shape[2]), jnp.bfloat16),
        pltpu.SemaphoreType.DMA((5,)),
    ]


def at_first(copies, act):
    @pl.when(pl.program_id(0) == 0)
    def _():
        for copy in copies:
            act(copy)


def forward_kernel(
    at, hidden0, context, out_weight, vectors, up, up_bias, down,
    entry2, normed1, inverse1, active, slope, normed2, inverse2, block_out, pooled, units,
    up_held, down_held, sems, acts,
):
    step = pl.program_id(0)
    up_copies, down_copies = weight_copies(at, up, down, up_held, down_held, sems)
    at_first(up_copies + down_copies, lambda copy: copy.start())
    rows, width = hidden0.shape
    token_count = rows * pl.num_programs(0)
    resid = hidden0[...] + matmul(context[...], out_weight[...]) + vectors[BO : BO + 1]
    normed, inverse = normal(resid)
    hidden1 = normed * vectors[G1 : G1 + 1] + vectors[E1 : E1 + 1]
    normed1[...], inverse1[...] = halved(normed), inverse
    entry = halved(hidden1)
    entry2[...] = entry.T
    at_first(up_copies, lambda copy: copy.wait())
    half = up.shape[2]
    span = half // BLOCKS
    for other in range(2):
        for block in range(BLOCKS):
            here = slice(block * span, (block + 1) * span)
            there = slice(other * half + block * span, other * half + (block + 1) * span)
            values = matmul(entry, up_held[other, :, here]) + up_bias[other, :, here]
            cumulative = 0.5 + 0.5 * lax.erf(values * ROOT_HALF)
            acted = halved(values * cumulative)
            acts[:, there] = acted
            active[there] = acted.T
            density = jnp.exp(-0.5 * values * values) * (1.0 / ROOT_TWO_PI)
            slope[:, there] = halved(cumulative + values * density)
    at_first(down_copies, lambda copy: copy.wait())
    total = hidden1 + vectors[B2 : B2 + 1] + matmul(acts[...], down_held[...])
    normed, inverse = normal(total)
    hidden2 = normed * vectors[G2 : G2 + 1] + vectors[E2 : E2 + 1]
    normed2[...], inverse2[...] = halved(normed), inverse
    block_out[...] = halved(hidden2)

    @pl.when(step == 0)
    def _():
        pooled[...] = jnp.zeros_like(pooled)

    slots = pooled.shape[0]
    span = token_count // slots
    for group in range(rows // span):
        slot, live = group_slot(at, step * (rows // span) + group, token_count)
        part = hidden2[group * span : (group + 1) * span] * live
        pooled[pl.ds(slot, 1)] += jnp.sum(part, axis=0, keepdims=True)

    @pl.when(step == pl.num_programs(0) - 1)
    def _():
        row = lax.broadcasted_iota(jnp.int32, (slots, LANES), 0)
        length = jnp.zeros((slots, LANES), jnp.int32)
        for slot in range(slots):
            length += jnp.where(row == slot, at[LENGTHS + slot], 0)
        mean = pooled[...] * (1.0 / jnp.maximum(length[:, :1], 1).astype(jnp.float32))
        pooled[...] = mean
        squares = jnp.sum(mean * mean, axis=-1, keepdims=True)
        units[:, :width] = halved(mean * lax.rsqrt(squares + EPS_NORM))
        first = lax.broadcasted_iota(jnp.int32, (slots, LANES), 1) == 0
        units[:, width:] = halved(jnp.where(first & (length > 0), 1.0, 0.0))


def forward(at, hidden0, context, out_weight, vectors, up, up_bias, down):
    token_count, width = hidden0.shape
    slots = at.shape[0] - LENGTHS
    hidden = 2 * up.shape[2]
    half = functools.partial(stacked, dtype=jnp.bfloat16)
    outs = [
        half(width, token_count),
        half(token_count, width),
        stacked(token_count, 1),
        half(hidden, token_count),
        half(token_count, hidden),
        half(token_count, width),
        stacked(token_count, 1),
        half(token_count, width),
        stacked(slots, width),
        half(slots, width + LANES),
    ]
    return kernel_call(
        forward_kernel,
        (token_count // CHUNK,),
        at,
        [hidden0, context, out_weight, vectors, up, up_bias, down],
        tiles(hidden0, context)
        + [held(out_weight), held(vectors), ANYWHERE, held(up_bias), ANYWHERE],
        outs,
        tiles(hidden0, *outs[:8])[1:] + [whole_block(out) for out in outs[8:]],
        weight_scratch(up, down) + [pltpu.VMEM((CHUNK, hidden), jnp.bfloat16)],
        vmem=56,
    )


def norm_back(grad, normed, inverse, gain):
    scaled = grad * gain
    inner = (
        scaled
        - jnp.mean(scaled, axis=-1, keepdims=True)
        - normed * jnp.mean(scaled * normed, axis=-1, keepdims=True)
    )
    return inner * inverse


def loss_kernel(
    at, units, others, pooled, normed2, inverse2, vectors,
    dresid, dresid_half, sums, dpool,
):
    slots, width = pooled.shape
    count = units.shape[0]
    step = pl.program_id(0)

    @pl.when(step == 0)
    def _():
        own, own_flags = units[:, :width], units[:, width:]
        other, other_flags = others[:, :width], others[:, width:]
        lane = lax.broadcasted_iota(jnp.int32, (slots, LANES), 1)
        one_hot = halved(jnp.where(lane == 0, 1.0, 0.0))
        own_row = matmul(one_hot, own_flags, NT)[:1] > 0
        other_row = matmul(one_hot, other_flags, NT)[:1] > 0

        def shares(lines, columns, live):
            logits = matmul(lines, columns, NT) * INV_TEMP
            logits = jnp.where(live, logits, NEGATIVE)
            weights = jnp.exp(logits - jnp.max(logits, axis=-1, keepdims=True))
            return weights / jnp.sum(weights, axis=-1, keepdims=True)

        row = lax.broadcasted_iota(jnp.int32, (slots, count), 0)
        column = lax.broadcasted_iota(jnp.int32, (slots, count), 1)
        target = jnp.where(row == column, 1.0, 0.0)
        row_live = own_flags[:slots, :1].astype(jnp.float32)
        dlogit = halved(LOSS_WEIGHT * (shares(own[:slots], other, other_row) - target) * row_live)
        near = shares(other, own, own_row)[:, :LANES]
        row = lax.broadcasted_iota(jnp.int32, (count, LANES), 0)
        column = lax.broadcasted_iota(jnp.int32, (count, LANES), 1)
        target = jnp.where(row == column, 1.0, 0.0)
        other_live = other_flags[:, :1].astype(jnp.float32)
        dnear = LOSS_WEIGHT * (near - target) * other_live
        dnear = halved(jnp.where(column < slots, dnear, 0.0))
        dunit = INV_TEMP * (matmul(dlogit, other) + matmul(dnear, other, TN)[:slots])
        mean = pooled[...]
        inverse = lax.rsqrt(jnp.sum(mean * mean, axis=-1, keepdims=True) + EPS_NORM)
        along = jnp.sum(mean * dunit, axis=-1, keepdims=True)
        grad = inverse * dunit - inverse * inverse * inverse * mean * along
        slot_row = lax.broadcasted_iota(jnp.int32, (slots, 1), 0)
        length = jnp.zeros((slots, 1), jnp.int32)
        for slot in range(slots):
            length += jnp.where(slot_row == slot, at[LENGTHS + slot], 0)
        dpool[...] = grad * (1.0 / jnp.maximum(length, 1).astype(jnp.float32))
        sums[...] = jnp.zeros_like(sums)

    gain = vectors[G2 : G2 + 1]
    token_count = normed2.shape[0] * pl.num_programs(0)
    span = token_count // slots
    groups = normed2.shape[0] // span
    for group in range(groups):
        here = pl.ds(group * span, span)
        slot, live = group_slot(at, step * groups + group, token_count)
        dhidden = dpool[pl.ds(slot, 1)] * live
        normed = normed2[here].astype(jnp.float32)
        values = norm_back(dhidden, normed, inverse2[here], gain)
        dresid[here] = values
        dresid_half[here] = halved(values)
        for k, terms in enumerate((values, dhidden * normed, dhidden)):
            sums[k : k + 1] += jnp.sum(terms, axis=0, keepdims=True)


def loss_back(at, units, others, pooled, normed2, inverse2, vectors):
    token_count, width = normed2.shape
    half = functools.partial(stacked, dtype=jnp.bfloat16)
    ins = [units, others, pooled, normed2, inverse2, vectors]
    outs = [
        stacked(token_count, width),
        half(token_count, width),
        stacked(3, width),
    ]
    return kernel_call(
        loss_kernel,
        (token_count // CHUNK,),
        at,
        ins,
        [held(a) for a in ins[:3]] + tiles(*ins[3:5]) + [held(vectors)],
        outs,
        tiles(*outs[:2]) + [whole_block(outs[2])],
        [pltpu.VMEM(pooled.shape, jnp.float32)],
    )


def backward_kernel(
    at, dresid2, dresid2_half, slope, up, down, normed1, inverse1, vectors,
    dpre, dpre_sum, dresid, dresid_half, sums,
    up_held, down_held, sems,
):
    up_copies, down_copies = weight_copies(at, up, down, up_held, down_held, sems)
    at_first(down_copies + up_copies, lambda copy: copy.start())

    @pl.when(pl.program_id(0) == 0)
    def _():
        dpre_sum[...] = jnp.zeros_like(dpre_sum)
        sums[...] = jnp.zeros_like(sums)

    at_first(down_copies, lambda copy: copy.wait())
    half = up.shape[2]
    span = half // BLOCKS
    grad = dresid2_half[...]
    for block in range(2 * BLOCKS):
        here = slice(block * span, (block + 1) * span)
        dactive = matmul(grad, down_held[here], NT)
        values = dactive * slope[:, here].astype(jnp.float32)
        dpre_sum[:, here] += jnp.sum(values, axis=0, keepdims=True)
        dpre[:, here] = halved(values)
    at_first(up_copies, lambda copy: copy.wait())
    dhidden = dresid2[...]
    for other in range(2):
        dhidden += matmul(dpre[:, other * half : (other + 1) * half], up_held[other], NT)
    normed = normed1[...].astype(jnp.float32)
    values = norm_back(dhidden, normed, inverse1[...], vectors[G1 : G1 + 1])
    dresid[...] = values
    rounded = halved(values)
    dresid_half[...] = rounded
    for k, terms in enumerate((values, dhidden * normed, dhidden)):
        sums[k : k + 1] += jnp.sum(terms, axis=0, keepdims=True)


def backward(at, dresid2, dresid2_half, slope, up, down, normed1, inverse1, vectors):
    token_count, width = dresid2.shape
    hidden = 2 * up.shape[2]
    half = functools.partial(stacked, dtype=jnp.bfloat16)
    outs = [
        half(token_count, hidden),
        stacked(1, hidden),
        stacked(token_count, width),
        half(token_count, width),
        stacked(3, width),
    ]
    out_specs = tiles(outs[0], *outs[2:4])
    return kernel_call(
        backward_kernel,
        (token_count // CHUNK,),
        at,
        [dresid2, dresid2_half, slope, up, down, normed1, inverse1, vectors],
        tiles(dresid2, dresid2_half, slope) + [ANYWHERE, ANYWHERE] + tiles(normed1, inverse1)
        + [held(vectors)],
        outs,
        out_specs[:1] + [whole_block(outs[1])] + out_specs[1:] + [whole_block(outs[4])],
        weight_scratch(up, down),
        vmem=56,
        long=True,
    )


def leave_kernel(at, dresid1, dtriples, qkv, lines, input_grad, last_own, last_away, total):
    step = pl.program_id(0)
    rows = dresid1.shape[0]
    values = dresid1[...]
    for other in range(2):
        values = values + matmul(dtriples[other], qkv[other], NT)
    input_grad[...] = values
    half_steps = pl.num_programs(0) // 2
    here = pl.ds(pl.multiple_of((step % half_steps) * rows, rows), rows)

    @pl.when(step < half_steps)
    def _():
        total[here] = values

    @pl.when(step >= half_steps)
    def _():
        total[here] += values

    @pl.when(step == pl.num_programs(0) - 1)
    def _():
        count = total.shape[0]
        long = total[...]
        span = 2 * count // (at.shape[0] - LENGTHS)
        short = sum(long[k * span : (k + 1) * span] for k in range(count // span))
        short = jnp.concatenate([short, jnp.zeros((count - span, long.shape[1]), jnp.float32)], axis=0)
        columns = jnp.where(at[SLOT_COUNT] == 2, long, short).T
        left, right = columns[:, : count // 2], columns[:, count // 2 :]
        last_own[:, : count // 2] = jnp.where(at[0] == 0, left, right)
        last_away[:, : count // 2] = halved(jnp.where(at[0] == 0, right, left))
        last_own[:, count // 2 :] = lines[0].T
        last_away[:, count // 2 :] = halved(two_words(lines[1].T))


def left(at, dresid1, dtriples, qkv, lines):
    token_count, width = dresid1.shape
    triple = qkv.shape[2]
    columns = token_count // 4 + LANES
    outs = [
        stacked(token_count, width),
        stacked(width, columns),
        stacked(width, columns, dtype=jnp.bfloat16),
    ]
    return kernel_call(
        leave_kernel,
        (token_count // CHUNK,),
        at,
        [dresid1, dtriples, qkv, lines],
        tiles(dresid1)
        + [pl.BlockSpec((2, CHUNK, triple), lambda i, at: (0, i, 0)), held(qkv), held(lines)],
        outs,
        tiles(outs[0]) + [whole_block(out) for out in outs[1:]],
        [pltpu.VMEM((token_count // 2, width), jnp.float32)],
        long=True,
    )


def product_kernel(natural_order, at, left_ref, right_ref, own, away):
    values = left_ref[...]
    if len(right_ref.shape) == 3:
        first, second = matmul(values, right_ref[0]), matmul(values, right_ref[1])
    else:
        both = matmul(values, right_ref[...])
        first, second = both[:, : both.shape[1] // 2], both[:, both.shape[1] // 2 :]
    if natural_order:
        first, second = jnp.where(at[0] == 0, first, second), jnp.where(at[0] == 0, second, first)
    own[...], away[...] = first, halved(second)


def product(at, left_array, right_array, natural_order=False):
    rows, depth = left_array.shape
    columns = right_array.size // depth // 2
    tile = rows // 6 if rows > 1024 else rows // 3
    outs = [stacked(rows, columns), stacked(rows, columns, dtype=jnp.bfloat16)]
    return kernel_call(
        functools.partial(product_kernel, natural_order),
        (rows // tile,),
        at,
        [left_array, right_array],
        [pl.BlockSpec((tile, depth), lambda i, at: (i, 0)), held(right_array)],
        outs,
        [pl.BlockSpec((tile, columns), lambda i, at: (i, 0))] * 2,
        long=True,
        vmem=56,
    )


def renew(grad, moment, weight, average, rate):
    moment_new = MOMENTUM * moment + grad
    weight_new = weight - rate * (grad + MOMENTUM * moment_new)
    average_new = AVERAGE * average + (1.0 - AVERAGE) * weight_new
    return (grad, moment_new, weight_new, average_new)


def local(
    tokens,
    lengths,
    attn_weight,
    attn_moment,
    attn_average,
    up_weight,
    up_moment,
    up_average,
    down_weight,
    down_moment,
    down_average,
    layer_vectors,
    vector_moment,
    vector_average,
    up_bias,
    bias_moment,
    bias_average,
    pos_table,
    pos_moment,
    pos_average,
):
    at = scalars(lengths[0, 0])
    stream = at[0]
    upper = stream == 1
    devices = lax.axis_size("batch")
    rows, hidden_half = up_weight.shape
    quarter = attn_weight.shape[2]
    width = 2 * quarter
    pos_half = pos_table.shape[0]
    slot_count = lengths.shape[2]

    misc = jnp.concatenate([layer_vectors.T, up_bias.reshape(2, rows).T], axis=1)
    misc = jnp.pad(misc, ((0, 0), (0, LANES - misc.shape[1])))
    entry_block = halved(
        jnp.concatenate([attn_weight[0], attn_weight[1], attn_weight[2], pos_table.T, misc], axis=1)
    )
    middle_block = halved(
        jnp.concatenate([up_weight, attn_weight[3], jnp.zeros((rows, LANES), jnp.float32)], axis=1)
    )
    triple = 3 * quarter
    pos_stop = triple + pos_half
    entry_gather = Gather(entry_block, width)
    entry_gather.far()
    entry_gather.near((2, 1))
    down_both = lax.all_gather(
        after(halved(down_weight), *entry_gather.sides), ("stream", "batch"), axis=0, tiled=True
    )
    middle_gather = Gather(
        after(middle_block, *entry_gather.sides), (hidden_half + quarter + LANES) // 2
    )
    middle_gather.far()
    entry_gather.near((1, 2), middle_gather.blocks)
    qkv_blocks, pos_blocks, misc_blocks = entry_gather.placed(
        at,
        (
            (0, triple, 0, "relative", 0, 0),
            (triple, pos_stop, 1, "", 0, pos_half),
            (pos_stop, pos_stop + LANES, 2, "stream", 0, 0),
        ),
        [
            stacked(2, devices, rows, triple, dtype=jnp.bfloat16),
            stacked(devices, rows, 2 * pos_half, dtype=jnp.bfloat16),
            stacked(2, devices, rows, LANES, dtype=jnp.bfloat16),
        ],
    )
    qkv = qkv_blocks.reshape(2, width, triple)
    pos_full = pos_blocks.reshape(width, 2 * pos_half)
    misc_full = misc_blocks.reshape(2, width, LANES)[:, :, :6].astype(jnp.float32)
    vectors = misc_full[:, :, :4].transpose(0, 2, 1).reshape(8, width)
    biases = misc_full[:, :, 4:].reshape(2, devices, rows, 2).transpose(0, 1, 3, 2)
    biases = biases.reshape(2, 1, hidden_half)

    def own_first(pair):
        return jnp.where(upper, pair[::-1], pair)

    shift = own_first(vectors[:2].reshape(2, 2, quarter).transpose(1, 0, 2))
    shift = jnp.stack([shift[:, 0], jnp.zeros((2, quarter), jnp.float32), shift[:, 1]], axis=1)
    hidden0, entry, triples = entered(
        at, tokens[0], pos_full, qkv, shift.reshape(2, 1, triple)
    )
    middle_gather.near((2, 1), triples)
    context_half, context_turned, probs = attend(after(at, *middle_gather.sides), triples)
    middle_gather.near((1, 2), context_half)
    up_blocks, out_blocks = middle_gather.placed(
        after(at, context_half),
        (
            (0, hidden_half, 0, "relative", 0, 0),
            (hidden_half, hidden_half + quarter, 1, "", 0, quarter),
        ),
        [
            stacked(2, devices, rows, hidden_half, dtype=jnp.bfloat16),
            stacked(devices, rows, width, dtype=jnp.bfloat16),
        ],
    )
    up = up_blocks.reshape(2, width, hidden_half)
    out_full = out_blocks.reshape(width, width)
    down = down_both.reshape(2, 2 * hidden_half, quarter)
    (entry2, normed1, inverse1, active, slope, normed2, inverse2, block_out, pooled, units) = forward(
        at, hidden0, context_half, out_full, vectors, up, own_first(biases), down
    )

    units = units[None]
    bit = 0
    while 1 << bit < devices:
        step = min(2, devices.bit_length() - 1 - bit)
        arrived = [exchanged(units, "batch", d << bit) for d in range(1, 1 << step)]
        units = jnp.concatenate([units] + arrived, axis=0)
        bit += step
    units = units.reshape(-1, units.shape[2])
    others = exchanged(units, "stream", 1)
    dresid2, dresid2_half, sums2 = loss_back(
        at, units, others, pooled, normed2, inverse2, vectors
    )

    def blocks(values):
        return values.reshape(devices // 4, 2, 2, values.shape[0] // devices, values.shape[1])

    down_own, down_away = product(at, active, dresid2_half, True)
    down_in = exchanged(down_away, "stream", 1)
    by_rows = down_weight.shape[0] % 32 == 0
    half_rows = down_weight.shape[0] // 2
    down_pair = (blocks(down_own), blocks(down_in))
    if by_rows:
        down_sides = [[down_pair + (half_rows, k, quarter, 0, True)] for k in range(2)]
    else:
        down_sides = [
            [down_pair + (2 * half_rows, 0, LANES, k, True) for k in ks] for ks in ((0, 1), (2,))
        ]
    down_fold = Fold(at, down_sides)
    down_parts = down_fold.first()
    down_first = down_fold.first_sent(down_parts)
    dpre, dpre_sum, dresid1, dresid1_half, sums1 = backward(
        after(at, *down_parts), dresid2, dresid2_half, slope, up, down, normed1, inverse1, vectors
    )
    down_fold.at = after(at, dresid1_half, *down_first)
    down_parts = down_fold.second(down_first)
    down_second, down_kept = down_fold.second_sent(down_parts)
    up_own, up_away = product(after(at, *down_parts), entry2, dpre)
    up_in = exchanged(up_away, "stream", 1)
    out_own, out_away = product(
        after(at, up_away, *down_second), context_turned, dresid1_half, True
    )
    out_in = exchanged(out_away, "stream", 1)
    down_fold.at = after(at, out_own, *down_second)
    down_parts = down_fold.third(down_second, down_kept)
    down_sum = down_fold.third_sent(down_parts)
    third = hidden_half // 3
    up_pair = (blocks(up_own), blocks(up_in))
    out_pair = (blocks(out_own), blocks(out_in))
    middle_fold = Fold(
        after(at, *down_parts),
        [
            [up_pair + (rows, 0, third, 0, False), up_pair + (rows, 0, third, 1, False)],
            [up_pair + (rows, 0, third, 2, False), out_pair + (rows, 0, quarter, 0, False)],
        ],
    )
    middle_parts = middle_fold.first()
    middle_first = middle_fold.first_sent(middle_parts)
    dcontext_half = halved(matmul(after(dresid1_half, *middle_parts), out_full, NT))
    dtriples, dsums = attend_back(at, triples, context_half, dcontext_half, probs)
    middle_fold.at = after(at, dtriples, *middle_first)
    middle_parts = middle_fold.second(middle_first)
    middle_second, middle_kept = middle_fold.second_sent(middle_parts)
    qkv_own, qkv_away = product(after(at, *middle_parts), entry, dtriples)
    qkv_in = exchanged(qkv_away, "stream", 1)
    dsums = own_first(dsums[:, :, 0]).transpose(1, 0, 2).reshape(2, width)
    lines = own_first(
        jnp.concatenate([dsums, sums1[:1], sums2[:1], sums1[1:], sums2[1:]], axis=0).reshape(2, 4, width)
    )
    bias_lines = dpre_sum.reshape(2, devices, 2, rows).transpose(0, 2, 1, 3).reshape(2, 2, width)
    lines = jnp.concatenate(
        [lines, bias_lines, jnp.zeros((2, LANES - 6, width), jnp.float32)], axis=1
    )
    input_grad, last_own, last_away = left(
        after(at, qkv_away, *middle_second), dresid1, dtriples, qkv, lines
    )
    last_in = exchanged(last_away, "stream", 1)
    middle_fold.at = after(at, input_grad, *middle_second)
    middle_parts = middle_fold.third(middle_second, middle_kept)
    middle_sum = middle_fold.third_sent(middle_parts)
    qkv_pair = (blocks(qkv_own), blocks(qkv_in))
    last_pair = (blocks(last_own), blocks(last_in))
    entry_fold = Fold(
        after(at, *middle_parts),
        [
            [qkv_pair + (rows, 0, quarter, 0, False), qkv_pair + (rows, 0, quarter, 1, False)],
            [
                qkv_pair + (rows, 0, quarter, 2, False),
                last_pair + (rows, 0, pos_half, 0, False),
                last_pair + (rows, 0, LANES, pos_half // LANES, False),
            ],
        ],
        wide=True,
    )
    entry_first = entry_fold.first_sent(entry_fold.first())
    entry_second, entry_kept = entry_fold.second_sent(entry_fold.second(entry_first))
    entry_sum = entry_fold.third_sent(entry_fold.third(entry_second, entry_kept))

    down_grad = down_sum
    if by_rows:
        down_grad = jnp.concatenate([down_sum[:, :quarter], down_sum[:, quarter:]], axis=0)
    attn_grad = jnp.stack(
        [entry_sum[:, k * quarter : (k + 1) * quarter] for k in range(3)]
        + [middle_sum[:, hidden_half : hidden_half + quarter]]
    )
    attn_all = renew(attn_grad, attn_moment, attn_weight, attn_average, RATE)
    up_all = renew(middle_sum[:, :hidden_half], up_moment, up_weight, up_average, RATE)
    down_all = renew(down_grad, down_moment, down_weight, down_average, RATE)
    vector_grad = entry_sum[:, pos_stop : pos_stop + 4].T
    vector_all = renew(vector_grad, vector_moment, layer_vectors, vector_average, RATE)
    bias_grad = entry_sum[:, pos_stop + 4 : pos_stop + 6].T.reshape(-1)
    bias_all = renew(bias_grad, bias_moment, up_bias, bias_average, RATE)
    pos_grad = entry_sum[:, triple:pos_stop].T
    pos_all = renew(pos_grad, pos_moment, pos_table, pos_average, POS_RATE)
    return (
        block_out[None],
        input_grad[None],
        *attn_all,
        *up_all,
        *down_all,
        *vector_all,
        *bias_all,
        *pos_all,
    )


def solution(mesh):
    tokens_at, weight_at = P("stream", "batch", None), P("batch", "stream")
    attn_at, rows_at, bias_at = P(None, "batch", "stream"), P("stream", "batch"), P(("stream", "batch"))
    kinds = (attn_at, weight_at, weight_at, rows_at, bias_at, rows_at)
    in_specs = (tokens_at, tokens_at) + tuple(kind for kind in kinds for _ in range(3))
    out_specs = (tokens_at, tokens_at) + tuple(kind for kind in kinds for _ in range(4))
    return jax.shard_map(local, mesh=mesh, in_specs=in_specs, out_specs=out_specs, check_vma=False)
```

profile of v0, /device:TPU:0, one launch (start us, length us, event | category | flops | bytes accessed | tf_op | source)
XLA Modules:
  0.0 393.2 jit_solution(9408136087918997690)
XLA Ops:
  10.7 3.1 collective-permute-start
  13.8 2.6 collective-permute-start.1
  16.4 3.3 collective-permute-done
  19.6 8.1 %collective-permute-done.1 = bf16[1,48,1536]{2,1,0:T(8,128)(2,1)S(1)} collective-permute-done((bf16[1,48,1536]{2,1,0:T(8,128)(2,1)S(1)}, bf16[1,48,1536]{2,1,0:T(8,128)(2,1)S(1)}, u32[]{:S(2)}, u32[]{:S(2)}) %collective-permute-start.1) | collective-permute-done | bytes 147488 | tf_op jit(solution)/shard_map/ppermute | solution.py:53
  27.9 1.6 collective-permute-start.4
  29.5 1.5 collective-permute-start.3
  31.7 3.0 collective-permute-done.4
  34.8 1.4 collective-permute-done.3
  37.2 3.0 collective-permute-start.5
  42.8 1.5 collective-permute-start.9
  45.5 12.0 %collective-permute-done.6 = bf16[1,48,2048]{2,1,0:T(8,128)(2,1)S(1)} collective-permute-done((bf16[1,48,2048]{2,1,0:T(8,128)(2,1)S(1)}, bf16[1,48,2048]{2,1,0:T(8,128)(2,1)S(1)}, u32[]{:S(2)}, u32[]{:S(2)}) %collective-permute-start.6) | collective-permute-done | bytes 196640 | tf_op jit(solution)/shard_map/ppermute | solution.py:53
  61.9 2.1 fusion.6
  64.6 1.5 collective-permute-start.12
  66.2 1.7 shard_map.395
  67.8 1.7 copy-done.11
  73.1 9.5 %shard_map.396 = (f32[1024,768]{1,0:T(8,128)}, bf16[768,1024]{1,0:T(8,128)(2,1)}, bf16[2,1024,1152]{2,1,0:T(8,128)(2,1)}) custom-call(s32[13]{0:T(128)} %copy-done.16, bf16[1024,768]{1,0:T(8,128)(2,1)} %bitcast.135, bf16[768,512]{1,0:T(8,128)(2,1)} %bitcast.131, bf16[2,768,1152]{2,1,0:T(8,128)(2,1)} %bitcast.125, f32[2,1,1152]{2,1,0:T(1,128)} %reshape.229.shift), custom_call_target="tpu_custom_call" | custom-call | flops 1000 | bytes 1000 | tf_op jit(solution)/shard_map/pallas_call | solution.py:469
  87.3 1.4 collective-permute-start.14
  88.7 21.1 %shard_map.397 = (bf16[1024,768]{1,0:T(8,128)(2,1)}, bf16[768,1024]{1,0:T(8,128)(2,1)}, bf16[6,2,2,512,512]{4,3,2,1,0:T(8,128)(2,1)}) custom-call(s32[13]{0:T(128)} %copy-done.16, bf16[2,1024,1152]{2,1,0:T(8,128)(2,1)} %get-tuple-element.127.q_ref.k_ref.v_ref, bf16[2,1024,1152]{2,1,0:T(8,128)(2,1)} %get-tuple-element.127.q_ref.k_ref.v_ref, ...), custom_call_target="tpu_custom_call" | custom-call | flops 1000 | bytes 1000 | tf_op jit(solution)/shard_map/pallas_call | solution.py:353
  110.0 2.1 collective-permute-done.15
  112.3 2.2 collective-permute-done.14
  115.8 3.3 collective-permute-done.16.refs_2_
  119.1 2.3 shard_map.398
  121.4 2.1 copy-done.9
  124.5 27.5 %shard_map.399 = (bf16[768,1024]{1,0:T(8,128)(2,1)}, bf16[1024,768]{1,0:T(8,128)(2,1)}, f32[1024,1]{1,0:T(8,128)}, bf16[3072,1024]{1,0:T(8,128)(2,1)}, bf16[1024...) custom-call(s32[13]{0:T(128)} %copy-done.16, ...), custom_call_target="tpu_custom_call" | custom-call | flops 1000 | bytes 1000 | tf_op jit(solution)/shard_map/pallas_call | solution.py:469
  152.1 1.4 collective-permute-start.18
  154.1 1.6 collective-permute-start.20
  157.4 1.5 collective-permute-done.20
  159.6 3.0 collective-permute-start.21
  165.4 3.1 collective-permute-done.22
  168.5 1.5 collective-permute-done.23
  170.1 1.5 collective-permute-done.24.others
  172.3 7.0 %shard_map.400 = (f32[1024,768]{1,0:T(8,128)}, bf16[1024,768]{1,0:T(8,128)(2,1)}, f32[3,768]{1,0:T(4,128)}) custom-call(s32[13]{0:T(128)} %copy-done.16, bf16[128,896]{1,0:T(8,128)(2,1)} %bitcast.141, bf16[128,896]{1,0:T(8,128)(2,1)} %copy-done.36, f32[8,768]{1,0:T(8,128)} %get-tuple-element.141.pooled, bf16[1024,768]{1,0:T(8,128)(2,1)} %get-tuple-element.142.normed2, ...), custom_call_target="tpu_custom_call" | custom-call | flops 1000 | bytes 1000 | tf_op jit(solution)/shard_map/pallas_call | solution.py:469
  179.2 11.0 %shard_map.401 = (f32[3072,384]{1,0:T(8,128)}, bf16[3072,384]{1,0:T(8,128)(2,1)}) custom-call(s32[13]{0:T(128)} %copy-done.16, bf16[3072,1024]{1,0:T(8,128)(2,1)} %get-tuple-element.139.left_ref, bf16[1024,768]{1,0:T(8,128)(2,1)} %get-tuple-element.144.right_ref.dresid2_half), custom_call_target="tpu_custom_call" | custom-call | flops 999999995904 | bytes 1000000000 | tf_op jit(solution)/shard_map/pallas_call | solution.py:469
  190.4 4.6 %collective-permute-done.25 = bf16[3072,384]{1,0:T(8,128)(2,1)S(1)} collective-permute-done((bf16[3072,384]{1,0:T(8,128)(2,1)}, bf16[3072,384]{1,0:T(8,128)(2,1)S(1)}, u32[]{:S(2)}, u32[]{:S(2)}) %collective-permute-start.25) | collective-permute-done | bytes 2359328 | tf_op jit(solution)/shard_map/ppermute | solution.py:53
  195.0 3.2 copy-done.3
  198.2 2.5 shard_map.402
  202.7 22.8 %shard_map.403 = (bf16[1024,3072]{1,0:T(8,128)(2,1)}, f32[1,3072]{1,0:T(1,128)}, f32[1024,768]{1,0:T(8,128)}, bf16[1024,768]{1,0:T(8,128)(2,1)}, f32[3,768]{1,0:T(4,128)}) custom-call(s32[13]{0:T(128)} %copy-done.16, f32[1024,768]{1,0:T(8,128)} %get-tuple-element.150.dresid2, bf16[1024,768]{1,0:T(8,128)(2,1)} %get-tuple-element.144.right_ref.dresid2_half, ...), custom_call_target="tpu_custom_call" | custom-call | flops 999999995904 | bytes 1000000000 | tf_op jit(solution)/shard_map/pallas_call | solution.py:469
  225.6 2.3 copy-done.4
  227.9 1.7 copy-done.6
  229.6 4.1 %shard_map.404 = (bf16[4,96,384]{2,1,0:T(8,128)(2,1)}, f32[4,96,384]{2,1,0:T(8,128)S(1)}, bf16[4,96,384]{2,1,0:T(8,128)(2,1)}, f32[4,96,384]{2,1,0:T(8,128)S(1)}) custom-call(s32[13]{0:T(128)S(1)} %copy-done.19, f32[4,2,2,192,384]{4,3,2,1,0:T(8,128)S(1)} %bitcast.107, bf16[4,2,2,192,384]{4,3,2,1,0:T(8,128)(2,1)S(1)} %bitcast.111, ...), custom_call_target="tpu_custom_call" | custom-call | flops 1000 | bytes 1000 | tf_op jit(solution)/shard_map/pallas_call | solution.py:180
  235.7 9.9 %shard_map.405 = (f32[768,1536]{1,0:T(8,128)}, bf16[768,1536]{1,0:T(8,128)(2,1)}) custom-call(s32[13]{0:T(128)} %copy-done.16, bf16[768,1024]{1,0:T(8,128)(2,1)} %get-tuple-element.161.left_ref, bf16[1024,3072]{1,0:T(8,128)(2,1)} %get-tuple-element.162.right_ref), custom_call_target="tpu_custom_call" | custom-call | flops 999999995904 | bytes 1000000000 | tf_op jit(solution)/shard_map/pallas_call | solution.py:469
  245.7 5.6 %shard_map.406 = (f32[768,384]{1,0:T(8,128)}, bf16[768,384]{1,0:T(8,128)(2,1)}) custom-call(s32[13]{0:T(128)} %copy-done.16, bf16[768,1024]{1,0:T(8,128)(2,1)} %get-tuple-element.165.left_ref, bf16[1024,768]{1,0:T(8,128)(2,1)} %get-tuple-element.177.right_ref), custom_call_target="tpu_custom_call" | custom-call | flops 999999995904 | bytes 1000000000 | tf_op jit(solution)/shard_map/pallas_call | solution.py:469
  256.8 2.4 shard_map.407
  261.1 2.4 collective-permute-start.50
  263.6 2.3 copy-done
  265.9 4.4 %shard_map.408 = (bf16[4,2,48,1024]{3,2,1,0:T(8,128)(2,1)}, bf16[4,2,48,896]{3,2,1,0:T(8,128)(2,1)}) custom-call(s32[13]{0:T(128)S(1)} %copy-done.20, f32[4,2,2,48,1536]{4,3,2,1,0:T(8,128)S(1)} %bitcast.93, bf16[4,2,2,48,1536]{4,3,2,1,0:T(8,128)(2,1)} %bitcast.30.refs_1_.refs_3_.refs_5_.refs_6_, f32[4,2,2,48,1536]{4,3,2,1,0:T(8,128)S(1)} %bitcast.94, ...), custom_call_target="tpu_custom_call" | custom-call | flops 1000 | bytes 1000 | tf_op jit(solution)/shard_map/pallas_call | solution.py:180
  272.4 2.6 convolution_convert_fusion.grad_ref
  275.0 21.9 %shard_map.409 = (bf16[2,1024,1152]{2,1,0:T(8,128)(2,1)}, f32[2,2,1,384]{3,2,1,0:T(1,128)}) custom-call(s32[13]{0:T(128)} %copy-done.16, bf16[2,1024,1152]{2,1,0:T(8,128)(2,1)} %get-tuple-element.127.q_ref.k_ref.v_ref, bf16[2,1024,1152]{2,1,0:T(8,128)(2,1)} %get-tuple-element.127.q_ref.k_ref.v_ref, ...), custom_call_target="tpu_custom_call" | custom-call | flops 999999995904 | bytes 1000000000 | tf_op jit(solution)/shard_map/pallas_call | solution.py:427
  298.8 2.3 copy-done.1
  301.1 4.4 %shard_map.410 = (bf16[4,48,1024]{2,1,0:T(8,128)(2,1)}, f32[4,48,1024]{2,1,0:T(8,128)S(1)}, bf16[4,48,896]{2,1,0:T(8,128)(2,1)}, f32[4,48,896]{2,1,0:T(8,128)S(1)}) custom-call(s32[13]{0:T(128)S(1)} %copy-done.21, f32[4,2,2,48,1536]{4,3,2,1,0:T(8,128)S(1)} %bitcast.96, bf16[4,2,2,48,1536]{4,3,2,1,0:T(8,128)(2,1)} %bitcast.30.refs_1_.refs_3_.refs_5_.refs_6_, ...), custom_call_target="tpu_custom_call" | custom-call | flops 1000 | bytes 1000 | tf_op jit(solution)/shard_map/pallas_call | solution.py:180
  307.5 8.6 %shard_map.411 = (f32[768,1152]{1,0:T(8,128)}, bf16[768,1152]{1,0:T(8,128)(2,1)}) custom-call(s32[13]{0:T(128)} %copy-done.16, bf16[768,1024]{1,0:T(8,128)(2,1)} %get-tuple-element.186.left_ref, bf16[2,1024,1152]{2,1,0:T(8,128)(2,1)} %get-tuple-element.179.right_ref.dtriples), custom_call_target="tpu_custom_call" | custom-call | flops 999999995904 | bytes 1000000000 | tf_op jit(solution)/shard_map/pallas_call | solution.py:469
  316.2 11.8 %shard_map.412 = (f32[1024,768]{1,0:T(8,128)}, f32[768,384]{1,0:T(8,128)}, bf16[768,384]{1,0:T(8,128)(2,1)}) custom-call(s32[13]{0:T(128)} %copy-done.16, f32[1024,768]{1,0:T(8,128)} %get-tuple-element.189.dresid1, bf16[2,1024,1152]{2,1,0:T(8,128)(2,1)} %get-tuple-element.179.right_ref.dtriples, bf16[2,768,1152]{2,1,0:T(8,128)(2,1)} %bitcast.126, ...), custom_call_target="tpu_custom_call" | custom-call | flops 999999995904 | bytes 1000000000 | tf_op jit(solution)/shard_map/pallas_call | solution.py:469
  330.2 1.8 shard_map.413
  332.0 1.9 collective-permute-start.46
  333.9 2.4 collective-permute-start.47
  337.7 3.3 shard_map.414
  344.2 4.3 %collective-permute-done.46 = bf16[1,48,1920]{2,1,0:T(8,128)(2,1)S(1)} collective-permute-done((bf16[1,48,1920]{2,1,0:T(8,128)(2,1)S(1)}, bf16[1,48,1920]{2,1,0:T(8,128)(2,1)S(1)}, u32[]{:S(2)}, u32[]{:S(2)}) %collective-permute-start.46) | collective-permute-done | bytes 184352 | tf_op jit(solution)/shard_map/ppermute | solution.py:53
  348.6 6.9 %collective-permute-done.38.refs_4_ = bf16[4,2,48,768]{3,2,1,0:T(8,128)(2,1)S(1)} collective-permute-done((bf16[4,2,48,768]{3,2,1,0:T(8,128)(2,1)S(1)}, bf16[4,2,48,768]{3,2,1,0:T(8,128)(2,1)S(1)}, u32[]{:S(2)}, u32[]{:S(2)}) %collective-permute-start.38) | collective-permute-done | bytes 589856 | tf_op jit(solution)/shard_map/ppermute | solution.py:53
  355.9 3.3 shard_map.415
  363.1 3.2 collective-permute-done.40.in0
  368.1 1.4 collective-permute-start.44
  369.6 3.0 collective-permute-start.42
  372.6 3.4 collective-permute-done.44
  376.1 4.4 %collective-permute-done.43 = bf16[1,48,1536]{2,1,0:T(8,128)(2,1)S(1)} collective-permute-done((bf16[1,48,1536]{2,1,0:T(8,128)(2,1)S(1)}, bf16[1,48,1536]{2,1,0:T(8,128)(2,1)S(1)}, u32[]{:S(2)}, u32[]{:S(2)}) %collective-permute-start.43) | collective-permute-done | bytes 147488 | tf_op jit(solution)/shard_map/ppermute | solution.py:53
  (292 shorter events, 67.9 us)
Async XLA Ops:
  7.2 23.8 %copy-start.23 = (f32[192,384]{1,0:T(8,128)S(1)}, f32[192,384]{1,0:T(8,128)}, u32[]{:S(2)}) copy-start(f32[192,384]{1,0:T(8,128)} %param.28) | copy-start | bytes 884740
  7.2 117.3 %all-gather.2.cloned.1.call-start = ((), (), s32[]{:S(2)}) async-start(), calls=%async_computation | async-start | bytes 4866048 | tf_op jit(solution)/shard_map/all_gather | solution.py:966
  10.7 8.9 %collective-permute-start = (bf16[1,48,1536]{2,1,0:T(8,128)(2,1)S(1)}, bf16[1,48,1536]{2,1,0:T(8,128)(2,1)S(1)}, u32[]{:S(2)}, u32[]{:S(2)}) collective-permute-start(bf16[1,48,1536]{2,1,0:T(8,128)(2,1)S(1)} %constant_dynamic-update-slice_fusion), channel_id=1, source_target_pairs={{0,4},{1,5},{2,6},{3,7},{4,0},{5,1},{6,2},{7,3},{8,12},{9,13},{10,... | collective-permute-start | bytes 442376 | tf_op jit(solution)/shard_map/ppermute | solution.py:53
  13.8 14.0 %collective-permute-start.1 = (bf16[1,48,1536]{2,1,0:T(8,128)(2,1)S(1)}, bf16[1,48,1536]{2,1,0:T(8,128)(2,1)S(1)}, u32[]{:S(2)}, u32[]{:S(2)}) collective-permute-start(bf16[1,48,1536]{2,1,0:T(8,128)(2,1)S(1)} %constant_dynamic-update-slice_fusion), channel_id=1, source_target_pairs={{0,8},{1,9},{2,10},{3,11},{4,12},{5,13},{6,14},{7,15},{8,0},{9,1},... | collective-permute-start | bytes 442376 | tf_op jit(solution)/shard_map/ppermute | solution.py:53
  16.4 11.4 %collective-permute-start.2 = (bf16[1,48,1536]{2,1,0:T(8,128)(2,1)S(1)}, bf16[1,48,1536]{2,1,0:T(8,128)(2,1)S(1)}, u32[]{:S(2)}, u32[]{:S(2)}) collective-permute-start(bf16[1,48,1536]{2,1,0:T(8,128)(2,1)S(1)} %constant_dynamic-update-slice_fusion), channel_id=1, source_target_pairs={{0,12},{1,13},{2,14},{3,15},{4,8},{5,9},{6,10},{7,11},{8,4},{9,5},... | collective-permute-start | bytes 442376 | tf_op jit(solution)/shard_map/ppermute | solution.py:53
  27.9 6.8 %collective-permute-start.4 = (bf16[4,48,768]{2,1,0:T(8,128)(2,1)S(1)}, bf16[4,48,768]{2,1,0:T(8,128)(2,1)S(1)}, u32[]{:S(2)}, u32[]{:S(2)}) collective-permute-start(bf16[4,48,768]{2,1,0:T(8,128)(2,1)S(1)} %get-tuple-element.342), channel_id=1, source_target_pairs={{0,1},{1,0},{2,3},{3,2},{4,5},{5,4},{6,7},{7,6},{8,9},{9,8},{10,11... | collective-permute-start | bytes 884744 | tf_op jit(solution)/shard_map/ppermute | solution.py:53
  29.5 6.7 %collective-permute-start.3 = (bf16[4,48,768]{2,1,0:T(8,128)(2,1)S(1)}, bf16[4,48,768]{2,1,0:T(8,128)(2,1)S(1)}, u32[]{:S(2)}, u32[]{:S(2)}) collective-permute-start(bf16[4,48,768]{2,1,0:T(8,128)(2,1)S(1)} %get-tuple-element.343), channel_id=1, source_target_pairs={{0,2},{1,3},{2,0},{3,1},{4,6},{5,7},{6,4},{7,5},{8,10},{9,11},{10,... | collective-permute-start | bytes 884744 | tf_op jit(solution)/shard_map/ppermute | solution.py:53
  37.2 8.3 %collective-permute-start.5 = (bf16[1,48,2048]{2,1,0:T(8,128)(2,1)S(1)}, bf16[1,48,2048]{2,1,0:T(8,128)(2,1)S(1)}, u32[]{:S(2)}, u32[]{:S(2)}) collective-permute-start(bf16[1,48,2048]{2,1,0:T(8,128)(2,1)S(1)} %bitcast.136), channel_id=1, source_target_pairs={{0,4},{1,5},{2,6},{3,7},{4,0},{5,1},{6,2},{7,3},{8,12},{9,13},{10,... | collective-permute-start | bytes 589832 | tf_op jit(solution)/shard_map/ppermute | solution.py:53
  40.2 17.4 %collective-permute-start.6 = (bf16[1,48,2048]{2,1,0:T(8,128)(2,1)S(1)}, bf16[1,48,2048]{2,1,0:T(8,128)(2,1)S(1)}, u32[]{:S(2)}, u32[]{:S(2)}) collective-permute-start(bf16[1,48,2048]{2,1,0:T(8,128)(2,1)S(1)} %bitcast.137), channel_id=1, source_target_pairs={{0,8},{1,9},{2,10},{3,11},{4,12},{5,13},{6,14},{7,15},{8,0},{9,1},... | collective-permute-start | bytes 589832 | tf_op jit(solution)/shard_map/ppermute | solution.py:53
  41.5 16.1 %collective-permute-start.7 = (bf16[1,48,2048]{2,1,0:T(8,128)(2,1)S(1)}, bf16[1,48,2048]{2,1,0:T(8,128)(2,1)S(1)}, u32[]{:S(2)}, u32[]{:S(2)}) collective-permute-start(bf16[1,48,2048]{2,1,0:T(8,128)(2,1)S(1)} %bitcast.138), channel_id=1, source_target_pairs={{0,12},{1,13},{2,14},{3,15},{4,8},{5,9},{6,10},{7,11},{8,4},{9,5},... | collective-permute-start | bytes 589832 | tf_op jit(solution)/shard_map/ppermute | solution.py:53
  42.8 16.9 %collective-permute-start.9 = (bf16[8,48,768]{2,1,0:T(8,128)(2,1)S(1)}, bf16[8,48,768]{2,1,0:T(8,128)(2,1)S(1)}, u32[]{:S(2)}, u32[]{:S(2)}) collective-permute-start(bf16[8,48,768]{2,1,0:T(8,128)(2,1)S(1)} %pad_maximum_fusion.3), channel_id=1, source_target_pairs={{0,2},{1,3},{2,0},{3,1},{4,6},{5,7},{6,4},{7,5},{8,10},{9,11},{10,... | collective-permute-start | bytes 1769480 | tf_op jit(solution)/shard_map/ppermute | solution.py:53
  44.4 15.5 %collective-permute-start.8 = (bf16[8,48,768]{2,1,0:T(8,128)(2,1)}, bf16[8,48,768]{2,1,0:T(8,128)(2,1)S(1)}, u32[]{:S(2)}, u32[]{:S(2)}) collective-permute-start(bf16[8,48,768]{2,1,0:T(8,128)(2,1)} %pad_maximum_fusion.2), channel_id=1, source_target_pairs={{0,1},{1,0},{2,3},{3,2},{4,5},{5,4},{6,7},{7,6},{8,9},{9,8},{10,11... | collective-permute-start | bytes 1769480 | tf_op jit(solution)/shard_map/ppermute | solution.py:53
  59.7 6.4 %collective-permute-start.11 = (bf16[16,48,768]{2,1,0:T(8,128)(2,1)S(1)}, bf16[16,48,768]{2,1,0:T(8,128)(2,1)S(1)}, u32[]{:S(2)}, u32[]{:S(2)}) collective-permute-start(bf16[16,48,768]{2,1,0:T(8,128)(2,1)S(1)} %constant_dynamic-update-slice_fusion.7.refs_1_), channel_id=1, source_target_pairs={{0,16},{16,0},{1,17},{17,1},{2,18},{18,2},{3,19},{19,3},{4,20},{20... | collective-permute-start | bytes 3538952 | tf_op jit(solution)/shard_map/ppermute | solution.py:53
  59.9 6.3 %collective-permute-start.10 = (bf16[16,48,768]{2,1,0:T(8,128)(2,1)S(1)}, bf16[16,48,768]{2,1,0:T(8,128)(2,1)}, u32[]{:S(2)}, u32[]{:S(2)}) collective-permute-start(bf16[16,48,768]{2,1,0:T(8,128)(2,1)S(1)} %constant_dynamic-update-slice_fusion.5.refs_0_), channel_id=1, source_target_pairs={{0,16},{16,0},{1,17},{17,1},{2,18},{18,2},{3,19},{19,3},{4,20},{20... | collective-permute-start | bytes 3538952 | tf_op jit(solution)/shard_map/ppermute | solution.py:53
  63.9 19.7 %collective-permute-start.13 = (bf16[4,48,1024]{2,1,0:T(8,128)(2,1)}, bf16[4,48,1024]{2,1,0:T(8,128)(2,1)}, u32[]{:S(2)}, u32[]{:S(2)}) collective-permute-start(bf16[4,48,1024]{2,1,0:T(8,128)(2,1)} %get-tuple-element.129), channel_id=1, source_target_pairs={{0,1},{1,0},{2,3},{3,2},{4,5},{5,4},{6,7},{7,6},{8,9},{9,8},{10,11... | collective-permute-start | bytes 1179656 | tf_op jit(solution)/shard_map/ppermute | solution.py:53
  64.6 21.7 %collective-permute-start.12 = (bf16[4,48,1024]{2,1,0:T(8,128)(2,1)}, bf16[4,48,1024]{2,1,0:T(8,128)(2,1)}, u32[]{:S(2)}, u32[]{:S(2)}) collective-permute-start(bf16[4,48,1024]{2,1,0:T(8,128)(2,1)} %get-tuple-element.128), channel_id=1, source_target_pairs={{0,2},{1,3},{2,0},{3,1},{4,6},{5,7},{6,4},{7,5},{8,10},{9,11},{10,... | collective-permute-start | bytes 1179656 | tf_op jit(solution)/shard_map/ppermute | solution.py:53
  84.7 27.4 %collective-permute-start.15 = (bf16[8,48,1024]{2,1,0:T(8,128)(2,1)S(1)}, bf16[8,48,1024]{2,1,0:T(8,128)(2,1)S(1)}, u32[]{:S(2)}, u32[]{:S(2)}) collective-permute-start(bf16[8,48,1024]{2,1,0:T(8,128)(2,1)S(1)} %constant_dynamic-update-slice_fusion.11), channel_id=1, source_target_pairs={{0,2},{1,3},{2,0},{3,1},{4,6},{5,7},{6,4},{7,5},{8,10},{9,11},{10,... | collective-permute-start | bytes 2359304 | tf_op jit(solution)/shard_map/ppermute | solution.py:53
  87.3 27.2 %collective-permute-start.14 = (bf16[8,48,1024]{2,1,0:T(8,128)(2,1)S(1)}, bf16[8,48,1024]{2,1,0:T(8,128)(2,1)S(1)}, u32[]{:S(2)}, u32[]{:S(2)}) collective-permute-start(bf16[8,48,1024]{2,1,0:T(8,128)(2,1)S(1)} %constant_dynamic-update-slice_fusion.9), channel_id=1, source_target_pairs={{0,1},{1,0},{2,3},{3,2},{4,5},{5,4},{6,7},{7,6},{8,9},{9,8},{10,11... | collective-permute-start | bytes 2359304 | tf_op jit(solution)/shard_map/ppermute | solution.py:53
  112.2 3.6 collective-permute-start.17
  114.6 4.5 %collective-permute-start.16 = (bf16[16,48,1024]{2,1,0:T(8,128)(2,1)S(1)}, bf16[16,48,1024]{2,1,0:T(8,128)(2,1)}, u32[]{:S(2)}, u32[]{:S(2)}) collective-permute-start(bf16[16,48,1024]{2,1,0:T(8,128)(2,1)S(1)} %constant_dynamic-update-slice_fusion.13.refs_0_), channel_id=1, source_target_pairs={{0,16},{16,0},{1,17},{17,1},{2,18},{18,2},{3,19},{19,3},{4,20},{20... | collective-permute-start | bytes 4718600 | tf_op jit(solution)/shard_map/ppermute | solution.py:53
  152.1 4.3 %collective-permute-start.18 = (bf16[1,8,896]{2,1,0:T(8,128)(2,1)}, bf16[1,8,896]{2,1,0:T(8,128)(2,1)S(1)}, u32[]{:S(2)}, u32[]{:S(2)}) collective-permute-start(bf16[1,8,896]{2,1,0:T(8,128)(2,1)} %bitcast.144), channel_id=1, source_target_pairs={{0,1},{1,0},{2,3},{3,2},{4,5},{5,4},{6,7},{7,6},{8,9},{9,8},{10,11... | collective-permute-start | bytes 43016 | tf_op jit(solution)/shard_map/ppermute | solution.py:53
  153.5 3.9 collective-permute-start.19
  154.1 4.8 %collective-permute-start.20 = (bf16[1,8,896]{2,1,0:T(8,128)(2,1)}, bf16[1,8,896]{2,1,0:T(8,128)(2,1)S(1)}, u32[]{:S(2)}, u32[]{:S(2)}) collective-permute-start(bf16[1,8,896]{2,1,0:T(8,128)(2,1)} %bitcast.146), channel_id=1, source_target_pairs={{0,3},{1,2},{2,1},{3,0},{4,7},{5,6},{6,5},{7,4},{8,11},{9,10},{10,... | collective-permute-start | bytes 43016 | tf_op jit(solution)/shard_map/ppermute | solution.py:53
  159.6 5.7 %collective-permute-start.21 = (bf16[4,8,896]{2,1,0:T(8,128)(2,1)S(1)}, bf16[4,8,896]{2,1,0:T(8,128)(2,1)S(1)}, u32[]{:S(2)}, u32[]{:S(2)}) collective-permute-start(bf16[4,8,896]{2,1,0:T(8,128)(2,1)S(1)} %pad_maximum_fusion.6), channel_id=1, source_target_pairs={{0,4},{1,5},{2,6},{3,7},{4,0},{5,1},{6,2},{7,3},{8,12},{9,13},{10,... | collective-permute-start | bytes 172040 | tf_op jit(solution)/shard_map/ppermute | solution.py:53
  162.6 5.9 %collective-permute-start.22 = (bf16[4,8,896]{2,1,0:T(8,128)(2,1)S(1)}, bf16[4,8,896]{2,1,0:T(8,128)(2,1)S(1)}, u32[]{:S(2)}, u32[]{:S(2)}) collective-permute-start(bf16[4,8,896]{2,1,0:T(8,128)(2,1)S(1)} %pad_maximum_fusion.6), channel_id=1, source_target_pairs={{0,8},{1,9},{2,10},{3,11},{4,12},{5,13},{6,14},{7,15},{8,0},{9,1},... | collective-permute-start | bytes 172040 | tf_op jit(solution)/shard_map/ppermute | solution.py:53
  163.9 6.1 %collective-permute-start.23 = (bf16[4,8,896]{2,1,0:T(8,128)(2,1)S(1)}, bf16[4,8,896]{2,1,0:T(8,128)(2,1)S(1)}, u32[]{:S(2)}, u32[]{:S(2)}) collective-permute-start(bf16[4,8,896]{2,1,0:T(8,128)(2,1)S(1)} %pad_maximum_fusion.6), channel_id=1, source_target_pairs={{0,12},{1,13},{2,14},{3,15},{4,8},{5,9},{6,10},{7,11},{8,4},{9,5},... | collective-permute-start | bytes 172040 | tf_op jit(solution)/shard_map/ppermute | solution.py:53
  170.0 1.6 collective-permute-start.24
  179.2 15.8 %copy-start.18 = (s32[13]{0:T(128)S(1)}, s32[13]{0:T(128)}, u32[]{:S(2)}) copy-start(s32[13]{0:T(128)} %copy-done.16) | copy-start | bytes 160
  190.2 4.7 %collective-permute-start.25 = (bf16[3072,384]{1,0:T(8,128)(2,1)}, bf16[3072,384]{1,0:T(8,128)(2,1)S(1)}, u32[]{:S(2)}, u32[]{:S(2)}) collective-permute-start(bf16[3072,384]{1,0:T(8,128)(2,1)} %get-tuple-element.146), channel_id=1, source_target_pairs={{0,16},{16,0},{1,17},{17,1},{2,18},{18,2},{3,19},{19,3},{4,20},{20... | collective-permute-start | bytes 7077896 | tf_op jit(solution)/shard_map/ppermute | solution.py:53
  200.7 24.9 %collective-permute-start.26 = (bf16[4,2,96,384]{3,2,1,0:T(8,128)(2,1)}, bf16[4,2,96,384]{3,2,1,0:T(8,128)(2,1)}, u32[]{:S(2)}, u32[]{:S(2)}) collective-permute-start(bf16[4,2,96,384]{3,2,1,0:T(8,128)(2,1)} %get-tuple-element.147), channel_id=1, source_target_pairs={{0,1},{1,0},{2,3},{3,2},{4,5},{5,4},{6,7},{7,6},{8,9},{9,8},{10,11... | collective-permute-start | bytes 1769480 | tf_op jit(solution)/shard_map/ppermute | solution.py:53
  201.4 24.1 %collective-permute-start.27 = (bf16[4,2,96,384]{3,2,1,0:T(8,128)(2,1)}, bf16[4,2,96,384]{3,2,1,0:T(8,128)(2,1)}, u32[]{:S(2)}, u32[]{:S(2)}) collective-permute-start(bf16[4,2,96,384]{3,2,1,0:T(8,128)(2,1)} %get-tuple-element.148), channel_id=1, source_target_pairs={{0,2},{1,3},{2,0},{3,1},{4,6},{5,7},{6,4},{7,5},{8,10},{9,11},{10,... | collective-permute-start | bytes 1769480 | tf_op jit(solution)/shard_map/ppermute | solution.py:53
  202.7 22.8 %copy-start.19 = (s32[13]{0:T(128)S(1)}, s32[13]{0:T(128)}, u32[]{:S(2)}) copy-start(s32[13]{0:T(128)} %copy-done.16) | copy-start | bytes 160
  233.7 11.9 %collective-permute-start.28 = (bf16[4,96,384]{2,1,0:T(8,128)(2,1)}, bf16[4,96,384]{2,1,0:T(8,128)(2,1)}, u32[]{:S(2)}, u32[]{:S(2)}) collective-permute-start(bf16[4,96,384]{2,1,0:T(8,128)(2,1)} %get-tuple-element.156), channel_id=1, source_target_pairs={{0,2},{1,3},{2,0},{3,1},{4,6},{5,7},{6,4},{7,5},{8,10},{9,11},{10,... | collective-permute-start | bytes 884744 | tf_op jit(solution)/shard_map/ppermute | solution.py:53
  234.4 11.2 %collective-permute-start.29 = (bf16[4,96,384]{2,1,0:T(8,128)(2,1)}, bf16[4,96,384]{2,1,0:T(8,128)(2,1)}, u32[]{:S(2)}, u32[]{:S(2)}) collective-permute-start(bf16[4,96,384]{2,1,0:T(8,128)(2,1)} %get-tuple-element.158), channel_id=1, source_target_pairs={{0,1},{1,0},{2,3},{3,2},{4,5},{5,4},{6,7},{7,6},{8,9},{9,8},{10,11... | collective-permute-start | bytes 884744 | tf_op jit(solution)/shard_map/ppermute | solution.py:53
  245.6 18.0 %collective-permute-start.30 = (bf16[768,1536]{1,0:T(8,128)(2,1)}, bf16[768,1536]{1,0:T(8,128)(2,1)}, u32[]{:S(2)}, u32[]{:S(2)}) collective-permute-start(bf16[768,1536]{1,0:T(8,128)(2,1)} %get-tuple-element.163), channel_id=1, source_target_pairs={{0,16},{16,0},{1,17},{17,1},{2,18},{18,2},{3,19},{19,3},{4,20},{20... | collective-permute-start | bytes 7077896 | tf_op jit(solution)/shard_map/ppermute | solution.py:53
  251.3 12.3 %collective-permute-start.31 = (bf16[768,384]{1,0:T(8,128)(2,1)}, bf16[768,384]{1,0:T(8,128)(2,1)S(1)}, u32[]{:S(2)}, u32[]{:S(2)}) collective-permute-start(bf16[768,384]{1,0:T(8,128)(2,1)} %get-tuple-element.174), channel_id=1, source_target_pairs={{0,16},{16,0},{1,17},{17,1},{2,18},{18,2},{3,19},{19,3},{4,20},{20... | collective-permute-start | bytes 1769480 | tf_op jit(solution)/shard_map/ppermute | solution.py:53
  259.2 69.6 %collective-permute-start.48 = (bf16[1,96,768]{2,1,0:T(8,128)(2,1)}, bf16[1,96,768]{2,1,0:T(8,128)(2,1)}, u32[]{:S(2)}, u32[]{:S(2)}) collective-permute-start(bf16[1,96,768]{2,1,0:T(8,128)(2,1)} %get-tuple-element.169), channel_id=1, source_target_pairs={{0,4},{1,5},{2,6},{3,7},{4,0},{5,1},{6,2},{7,3},{8,12},{9,13},{10,... | collective-permute-start | bytes 442376 | tf_op jit(solution)/shard_map/ppermute | solution.py:53
  259.8 69.0 %collective-permute-start.49 = (bf16[1,96,768]{2,1,0:T(8,128)(2,1)}, bf16[1,96,768]{2,1,0:T(8,128)(2,1)}, u32[]{:S(2)}, u32[]{:S(2)}) collective-permute-start(bf16[1,96,768]{2,1,0:T(8,128)(2,1)} %get-tuple-element.170), channel_id=1, source_target_pairs={{0,8},{1,9},{2,10},{3,11},{4,12},{5,13},{6,14},{7,15},{8,0},{9,1},... | collective-permute-start | bytes 442376 | tf_op jit(solution)/shard_map/ppermute | solution.py:53
  261.1 67.7 %collective-permute-start.50 = (bf16[1,96,768]{2,1,0:T(8,128)(2,1)}, bf16[1,96,768]{2,1,0:T(8,128)(2,1)}, u32[]{:S(2)}, u32[]{:S(2)}) collective-permute-start(bf16[1,96,768]{2,1,0:T(8,128)(2,1)} %get-tuple-element.171), channel_id=1, source_target_pairs={{0,12},{1,13},{2,14},{3,15},{4,8},{5,9},{6,10},{7,11},{8,4},{9,5},... | collective-permute-start | bytes 442376 | tf_op jit(solution)/shard_map/ppermute | solution.py:53
  270.4 28.4 %collective-permute-start.32 = (bf16[4,2,48,1024]{3,2,1,0:T(8,128)(2,1)}, bf16[4,2,48,1024]{3,2,1,0:T(8,128)(2,1)}, u32[]{:S(2)}, u32[]{:S(2)}) collective-permute-start(bf16[4,2,48,1024]{3,2,1,0:T(8,128)(2,1)} %get-tuple-element.175), channel_id=1, source_target_pairs={{0,1},{1,0},{2,3},{3,2},{4,5},{5,4},{6,7},{7,6},{8,9},{9,8},{10,11... | collective-permute-start | bytes 2359304 | tf_op jit(solution)/shard_map/ppermute | solution.py:53
  271.1 27.7 %collective-permute-start.33 = (bf16[4,2,48,896]{3,2,1,0:T(8,128)(2,1)}, bf16[4,2,48,896]{3,2,1,0:T(8,128)(2,1)}, u32[]{:S(2)}, u32[]{:S(2)}) collective-permute-start(bf16[4,2,48,896]{3,2,1,0:T(8,128)(2,1)} %get-tuple-element.176), channel_id=1, source_target_pairs={{0,2},{1,3},{2,0},{3,1},{4,6},{5,7},{6,4},{7,5},{8,10},{9,11},{10,... | collective-permute-start | bytes 2064392 | tf_op jit(solution)/shard_map/ppermute | solution.py:53
  275.0 22.7 %copy-start.41 = (f32[2,768]{1,0:T(2,128)S(1)}, f32[2,768]{1,0:T(2,128)}, u32[]{:S(2)}) copy-start(f32[2,768]{1,0:T(2,128)} %slice.147) | copy-start | bytes 18436
  275.0 22.7 %copy-start.42 = (f32[2,768]{1,0:T(2,128)S(1)}, f32[2,768]{1,0:T(2,128)}, u32[]{:S(2)}) copy-start(f32[2,768]{1,0:T(2,128)} %slice.146) | copy-start | bytes 18436
  275.0 22.7 %copy-start.43 = (f32[1,768]{1,0:T(1,128)S(1)}, f32[1,768]{1,0:T(1,128)}, u32[]{:S(2)}) copy-start(f32[1,768]{1,0:T(1,128)} %slice.145) | copy-start | bytes 9220
  275.0 22.7 %copy-start.44 = (f32[1,768]{1,0:T(1,128)S(1)}, f32[1,768]{1,0:T(1,128)}, u32[]{:S(2)}) copy-start(f32[1,768]{1,0:T(1,128)} %slice.144) | copy-start | bytes 9220
  275.0 22.8 %copy-start.40 = (f32[2,2,768]{2,1,0:T(2,128)S(1)}, f32[2,2,768]{2,1,0:T(2,128)}, u32[]{:S(2)}) copy-start(f32[2,2,768]{2,1,0:T(2,128)} %reshape.223) | copy-start | bytes 36868
  275.0 22.8 %copy-start.56 = (f32[128]{0:T(128)S(1)}, f32[128]{0:T(128)}, u32[]{:S(2)}) copy-start(f32[128]{0:T(128)} %pad.26.clone) | copy-start | bytes 1540
  275.0 23.8 %copy-start.21 = (s32[13]{0:T(128)S(1)}, s32[13]{0:T(128)}, u32[]{:S(2)}) copy-start(s32[13]{0:T(128)} %copy-done.16) | copy-start | bytes 160
  305.5 10.6 %collective-permute-start.34 = (bf16[4,48,1024]{2,1,0:T(8,128)(2,1)}, bf16[4,48,1024]{2,1,0:T(8,128)(2,1)}, u32[]{:S(2)}, u32[]{:S(2)}) collective-permute-start(bf16[4,48,1024]{2,1,0:T(8,128)(2,1)} %get-tuple-element.181), channel_id=1, source_target_pairs={{0,2},{1,3},{2,0},{3,1},{4,6},{5,7},{6,4},{7,5},{8,10},{9,11},{10,... | collective-permute-start | bytes 1179656 | tf_op jit(solution)/shard_map/ppermute | solution.py:53
  306.3 9.9 %collective-permute-start.35 = (bf16[4,48,896]{2,1,0:T(8,128)(2,1)}, bf16[4,48,896]{2,1,0:T(8,128)(2,1)}, u32[]{:S(2)}, u32[]{:S(2)}) collective-permute-start(bf16[4,48,896]{2,1,0:T(8,128)(2,1)} %get-tuple-element.183), channel_id=1, source_target_pairs={{0,1},{1,0},{2,3},{3,2},{4,5},{5,4},{6,7},{7,6},{8,9},{9,8},{10,11... | collective-permute-start | bytes 1032200 | tf_op jit(solution)/shard_map/ppermute | solution.py:53
  316.1 20.2 %collective-permute-start.36 = (bf16[768,1152]{1,0:T(8,128)(2,1)}, bf16[768,1152]{1,0:T(8,128)(2,1)}, u32[]{:S(2)}, u32[]{:S(2)}) collective-permute-start(bf16[768,1152]{1,0:T(8,128)(2,1)} %get-tuple-element.187), channel_id=1, source_target_pairs={{0,16},{16,0},{1,17},{17,1},{2,18},{18,2},{3,19},{19,3},{4,20},{20... | collective-permute-start | bytes 5308424 | tf_op jit(solution)/shard_map/ppermute | solution.py:53
  328.0 8.4 %collective-permute-start.37 = (bf16[768,384]{1,0:T(8,128)(2,1)}, bf16[768,384]{1,0:T(8,128)(2,1)S(1)}, u32[]{:S(2)}, u32[]{:S(2)}) collective-permute-start(bf16[768,384]{1,0:T(8,128)(2,1)} %get-tuple-element.203), channel_id=1, source_target_pairs={{0,16},{16,0},{1,17},{17,1},{2,18},{18,2},{3,19},{19,3},{4,20},{20... | collective-permute-start | bytes 1769480 | tf_op jit(solution)/shard_map/ppermute | solution.py:53
  331.9 12.2 %collective-permute-start.45 = (bf16[1,48,1920]{2,1,0:T(8,128)(2,1)S(1)}, bf16[1,48,1920]{2,1,0:T(8,128)(2,1)S(1)}, u32[]{:S(2)}, u32[]{:S(2)}) collective-permute-start(bf16[1,48,1920]{2,1,0:T(8,128)(2,1)S(1)} %get-tuple-element.197), channel_id=1, source_target_pairs={{0,4},{1,5},{2,6},{3,7},{4,0},{5,1},{6,2},{7,3},{8,12},{9,13},{10,... | collective-permute-start | bytes 552968 | tf_op jit(solution)/shard_map/ppermute | solution.py:53
  332.0 16.4 %collective-permute-start.46 = (bf16[1,48,1920]{2,1,0:T(8,128)(2,1)S(1)}, bf16[1,48,1920]{2,1,0:T(8,128)(2,1)S(1)}, u32[]{:S(2)}, u32[]{:S(2)}) collective-permute-start(bf16[1,48,1920]{2,1,0:T(8,128)(2,1)S(1)} %get-tuple-element.198), channel_id=1, source_target_pairs={{0,8},{1,9},{2,10},{3,11},{4,12},{5,13},{6,14},{7,15},{8,0},{9,1},... | collective-permute-start | bytes 552968 | tf_op jit(solution)/shard_map/ppermute | solution.py:53
  333.9 14.5 %collective-permute-start.47 = (bf16[1,48,1920]{2,1,0:T(8,128)(2,1)S(1)}, bf16[1,48,1920]{2,1,0:T(8,128)(2,1)S(1)}, u32[]{:S(2)}, u32[]{:S(2)}) collective-permute-start(bf16[1,48,1920]{2,1,0:T(8,128)(2,1)S(1)} %get-tuple-element.199), channel_id=1, source_target_pairs={{0,12},{1,13},{2,14},{3,15},{4,8},{5,9},{6,10},{7,11},{8,4},{9,5},... | collective-permute-start | bytes 552968 | tf_op jit(solution)/shard_map/ppermute | solution.py:53
  341.0 14.5 %collective-permute-start.38 = (bf16[4,2,48,768]{3,2,1,0:T(8,128)(2,1)S(1)}, bf16[4,2,48,768]{3,2,1,0:T(8,128)(2,1)S(1)}, u32[]{:S(2)}, u32[]{:S(2)}) collective-permute-start(bf16[4,2,48,768]{3,2,1,0:T(8,128)(2,1)S(1)} %get-tuple-element.204), channel_id=1, source_target_pairs={{0,1},{1,0},{2,3},{3,2},{4,5},{5,4},{6,7},{7,6},{8,9},{9,8},{10,11... | collective-permute-start | bytes 1769480 | tf_op jit(solution)/shard_map/ppermute | solution.py:53
  341.8 14.2 %collective-permute-start.39 = (bf16[4,2,48,768]{3,2,1,0:T(8,128)(2,1)S(1)}, bf16[4,2,48,768]{3,2,1,0:T(8,128)(2,1)S(1)}, u32[]{:S(2)}, u32[]{:S(2)}) collective-permute-start(bf16[4,2,48,768]{3,2,1,0:T(8,128)(2,1)S(1)} %get-tuple-element.205), channel_id=1, source_target_pairs={{0,2},{1,3},{2,0},{3,1},{4,6},{5,7},{6,4},{7,5},{8,10},{9,11},{10,... | collective-permute-start | bytes 1769480 | tf_op jit(solution)/shard_map/ppermute | solution.py:53
  348.5 13.5 %copy-start.26 = (f32[48,1536]{1,0:T(8,128)S(1)}, f32[48,1536]{1,0:T(8,128)}, u32[]{:S(2)}) copy-start(f32[48,1536]{1,0:T(8,128)} %param.25) | copy-start | bytes 884740
  348.5 13.5 %copy-start.30 = (f32[48,1536]{1,0:T(8,128)S(1)}, f32[48,1536]{1,0:T(8,128)}, u32[]{:S(2)}) copy-start(f32[48,1536]{1,0:T(8,128)} %param.27) | copy-start | bytes 884740
  359.3 7.0 %collective-permute-start.40 = (bf16[4,48,768]{2,1,0:T(8,128)(2,1)S(1)}, bf16[4,48,768]{2,1,0:T(8,128)(2,1)S(1)}, u32[]{:S(2)}, u32[]{:S(2)}) collective-permute-start(bf16[4,48,768]{2,1,0:T(8,128)(2,1)S(1)} %get-tuple-element.208), channel_id=1, source_target_pairs={{0,2},{1,3},{2,0},{3,1},{4,6},{5,7},{6,4},{7,5},{8,10},{9,11},{10,... | collective-permute-start | bytes 884744 | tf_op jit(solution)/shard_map/ppermute | solution.py:53
  360.6 6.7 %collective-permute-start.41 = (bf16[4,48,768]{2,1,0:T(8,128)(2,1)S(1)}, bf16[4,48,768]{2,1,0:T(8,128)(2,1)S(1)}, u32[]{:S(2)}, u32[]{:S(2)}) collective-permute-start(bf16[4,48,768]{2,1,0:T(8,128)(2,1)S(1)} %get-tuple-element.209), channel_id=1, source_target_pairs={{0,1},{1,0},{2,3},{3,2},{4,5},{5,4},{6,7},{7,6},{8,9},{9,8},{10,11... | collective-permute-start | bytes 884744 | tf_op jit(solution)/shard_map/ppermute | solution.py:53
  368.1 7.8 %collective-permute-start.44 = (bf16[1,48,1536]{2,1,0:T(8,128)(2,1)S(1)}, bf16[1,48,1536]{2,1,0:T(8,128)(2,1)S(1)}, u32[]{:S(2)}, u32[]{:S(2)}) collective-permute-start(bf16[1,48,1536]{2,1,0:T(8,128)(2,1)S(1)} %get-tuple-element.213), channel_id=1, source_target_pairs={{0,12},{1,13},{2,14},{3,15},{4,8},{5,9},{6,10},{7,11},{8,4},{9,5},... | collective-permute-start | bytes 442376 | tf_op jit(solution)/shard_map/ppermute | solution.py:53
  369.6 10.9 %collective-permute-start.43 = (bf16[1,48,1536]{2,1,0:T(8,128)(2,1)S(1)}, bf16[1,48,1536]{2,1,0:T(8,128)(2,1)S(1)}, u32[]{:S(2)}, u32[]{:S(2)}) collective-permute-start(bf16[1,48,1536]{2,1,0:T(8,128)(2,1)S(1)} %get-tuple-element.212), channel_id=1, source_target_pairs={{0,8},{1,9},{2,10},{3,11},{4,12},{5,13},{6,14},{7,15},{8,0},{9,1},... | collective-permute-start | bytes 442376 | tf_op jit(solution)/shard_map/ppermute | solution.py:53
  369.6 11.1 %collective-permute-start.42 = (bf16[1,48,1536]{2,1,0:T(8,128)(2,1)S(1)}, bf16[1,48,1536]{2,1,0:T(8,128)(2,1)S(1)}, u32[]{:S(2)}, u32[]{:S(2)}) collective-permute-start(bf16[1,48,1536]{2,1,0:T(8,128)(2,1)S(1)} %get-tuple-element.211), channel_id=1, source_target_pairs={{0,4},{1,5},{2,6},{3,7},{4,0},{5,1},{6,2},{7,3},{8,12},{9,13},{10,... | collective-permute-start | bytes 442376 | tf_op jit(solution)/shard_map/ppermute | solution.py:53
  (46 other events, 250.8 us)
Sparse Core Ops, SparseCore 0:
  37.2 81.0 all-gather.1
where the time goes:
time: 395 us; the launch traced here: 393 us
  Pallas kernels  188 us (48%)
  waiting for transfers between devices  73.3 us (19%)
  starting transfers between devices  58.1 us (15%)
  local copies, waits for them, and re-layouts  40.6 us (10%)
  other arithmetic  15.8 us (4%)
  between operations  15 us (4%)
    pallas_call x9, Pallas kernels, kernel_call(): pl.pallas_call(kernel, grid_spec=pltpu.PrefetchScalarGridSpec(num_scalar_...  114 us
    ppermute x51, waiting for transfers between devices, exchanged(): lax.ppermute(block, axis, [(place, place ^ mask) for place in range(count)])  73.3 us
    ppermute x51, starting transfers between devices, exchanged(): lax.ppermute(block, axis, [(place, place ^ mask) for place in range(count)])  58.1 us
    unnamed x138, local copies, waits for them, and re-layouts  29.3 us
    pallas_call x9, Pallas kernels, fold_call(): pl.pallas_call(kernel, grid_spec=pltpu.PrefetchScalarGridSpec(num_scalar_...  27 us
    pallas_call x1, Pallas kernels, attend_back(): pl.pallas_call(attend_back_kernel, grid_spec=pltpu.PrefetchScalarGridSpec...  21.9 us
    pallas_call x1, Pallas kernels, attend(): pl.pallas_call(attend_kernel, grid_spec=pltpu.PrefetchScalarGridSpec(num_...  21.1 us
  transfers between devices with their start and end apart: 52, of which 23 were waited for; matrix products, arithmetic and copies ran while one was open for 7% of the time, Pallas kernels for 33%

commit v1 on v0

--- a/solution.py
+++ b/solution.py
@@ -27,6 +27,8 @@
 COST = pl.CostEstimate(flops=1000, bytes_accessed=1000, transcendentals=0)
 LONG_COST = pl.CostEstimate(flops=10**12, bytes_accessed=10**9, transcendentals=0)
 ANYWHERE = pl.BlockSpec(memory_space=pl.ANY)
+HERE = pl.BlockSpec(memory_space=pltpu.VMEM)
+FORWARD_VMEM, BACKWARD_VMEM, PRODUCT_VMEM, OTHER_VMEM = 22, 20, 14, 20
 NN = (((1,), (0,)), ((), ()))
 NT = (((1,), (1,)), ((), ()))
 TN = (((0,), (0,)), ((), ()))
@@ -42,6 +44,10 @@
 
 def stacked(*shape, dtype=jnp.float32):
     return jax.ShapeDtypeStruct(shape, dtype)
+
+
+def far_off(*shape, dtype=jnp.bfloat16):
+    return pltpu.HBM(shape, dtype)
 
 
 def after(value, *earlier):
@@ -86,7 +92,7 @@
             self.sides[side] = jnp.concatenate([own, exchanged(part, "batch", flip)], axis=0)
             self.masks[side] = self.masks[side] + [flip | mask for mask in self.masks[side]]
 
-    def placed(self, at, pieces, shapes):
+    def placed(self, at, pieces, shapes, down=None):
         sources, moves = [], []
         for other in range(2):
             for side, part in enumerate(self.sides):
@@ -101,12 +107,38 @@
                             (len(sources) - 1, entry, mask, (low - base, high - base), target, lead,
                              other, offset + low - start, span)
                         )
-        return placed(at, sources, moves, shapes)
-
-
-def place_kernel(moves, count, at_ref, *refs):
-    sources, targets = refs[:count], refs[count:]
+        return placed(at, sources, moves, shapes, down)
+
+
+def far_away(array):
+    return pltpu.with_memory_space_constraint(array, pltpu.HBM)
+
+
+def near_by(array):
+    return pltpu.with_memory_space_constraint(array, pltpu.VMEM)
+
+
+def place_kernel(moves, count, with_down, at_ref, *refs):
+    sources, rest = refs[:count], refs[count:]
     stream = at_ref[0]
+    copies = []
+    if with_down:
+        down, targets, down_held, sems = rest[0], rest[1:-2], rest[-2], rest[-1]
+        half, quarter = down.shape[1] // 2, down.shape[2]
+        for other in range(2):
+            start = pl.multiple_of((other ^ stream) * half, half)
+            for k in range(2):
+                copies.append(
+                    pltpu.make_async_copy(
+                        down.at[k, pl.ds(start, half)],
+                        down_held.at[pl.ds(other * half, half), pl.ds(k * quarter, quarter)],
+                        sems.at[2 * other + k],
+                    )
+                )
+        for copy in copies:
+            copy.start()
+    else:
+        targets = rest
     batch = at_ref[1] + 2 * at_ref[2] + 4 * at_ref[3]
     for source, entry, mask, columns, target, lead, other, start, span in moves:
         core = stream ^ other
@@ -117,18 +149,29 @@
         elif lead == "stream":
             at = (core,) + at
         targets[target][at] = sources[source][entry, :, columns[0] : columns[1]]
-
-
-def placed(at, sources, moves, shapes):
-    held = pl.BlockSpec(memory_space=pltpu.VMEM)
+    for copy in copies:
+        copy.wait()
+
+
+def placed(at, sources, moves, shapes, down=None):
+    held_here = pl.BlockSpec(memory_space=pltpu.VMEM)
+    ins, in_specs, out_specs = list(sources), [held_here] * len(sources), [held_here] * len(shapes)
+    scratch = []
+    if down is not None:
+        ins.append(far_away(down))
+        in_specs.append(ANYWHERE)
+        shapes = list(shapes) + [pltpu.VMEM((down.shape[1], 2 * down.shape[2]), down.dtype)]
+        out_specs.append(held_here)
+        scratch.append(pltpu.SemaphoreType.DMA((4,)))
     return pl.pallas_call(
-        functools.partial(place_kernel, moves, len(sources)),
-        in_specs=[pl.BlockSpec(memory_space=pltpu.SMEM)] + [held] * len(sources),
-        out_specs=[held] * len(shapes),
+        functools.partial(place_kernel, moves, len(sources), down is not None),
+        in_specs=[pl.BlockSpec(memory_space=pltpu.SMEM)] + in_specs,
+        out_specs=out_specs,
         out_shape=shapes,
-        compiler_params=pltpu.CompilerParams(vmem_limit_bytes=20 << 20),
+        scratch_shapes=scratch,
+        compiler_params=pltpu.CompilerParams(vmem_limit_bytes=24 << 20),
         cost_estimate=COST,
-    )(at, *sources)
+    )(at, *ins)
 
 
 def two_words(values):
@@ -161,21 +204,16 @@
     )
 
 
-def piece_specs(side, piece, away):
-    array, arrived, rows, row_at, columns, column_at, flip = piece
-
-    def spec(column, turn):
-        def index(z, at):
-            place = z ^ (turn(at[0]) * (array.shape[0] // 2)) if flip else z
-            bit = at[1 + side] ^ (1 if away else 0)
-            return (place, 0, bit, row_at, column) if side == 0 else (place, bit, 0, row_at, column)
-
-        return pl.BlockSpec((1, 2, 1, rows, columns) if side == 0 else (1, 1, 2, rows, columns), index)
-
-    return [spec(column_at, lambda core: core), spec(column_at, lambda core: 1 - core)]
-
-
-def fold_call(kernel, count, at, ins, in_specs, outs, out_specs):
+def piece_spec(piece):
+    array, _, rows, row_at, columns, column_at, _ = piece
+    return pl.BlockSpec(
+        (array.shape[0], 2, 2, rows, columns),
+        lambda _, at: (0, 0, 0, row_at, column_at),
+        pipeline_mode=pl.Buffered(buffer_count=1),
+    )
+
+
+def fold_call(kernel, count, at, ins, in_specs, outs, out_specs, long=False):
     size = sum(math.prod(o.shape) for o in outs) * 8
     return pl.pallas_call(
         kernel,
@@ -183,8 +221,8 @@
             num_scalar_prefetch=1, grid=(count,), in_specs=in_specs, out_specs=out_specs
         ),
         out_shape=outs,
-        compiler_params=pltpu.CompilerParams(vmem_limit_bytes=16 << 20),
-        cost_estimate=COST,
+        compiler_params=pltpu.CompilerParams(vmem_limit_bytes=26 << 20),
+        cost_estimate=LONG_COST if long else COST,
     )(at, *ins)
 
 
@@ -195,65 +233,66 @@
         self.rows = [side[0][2] for side in sides]
         self.columns = [sum(piece[4] for piece in side) for side in sides]
 
-    def piece_values(self, refs, side, pick):
+    def piece_values(self, refs, side, z, bit, which, core):
         columns = []
-        for k in range(len(self.sides[side])):
+        for k, piece in enumerate(self.sides[side]):
+            values = []
+            for turn, ref in ((core, refs[2 * k]), (1 - core, refs[2 * k + 1])):
+                place = z ^ (turn * (self.count // 2)) if piece[6] else z
+                entry = ref[place, which, bit] if side == 0 else ref[place, bit, which]
+                values.append(entry.astype(jnp.float32))
             wide = self.wide[side] and k == len(self.sides[side]) - 1
-            arrived = pick(refs[2 * k + 1]).astype(jnp.float32)
-            columns.append(pick(refs[2 * k]) + (one_word(arrived) if wide else arrived))
+            columns.append(values[0] + (one_word(values[1]) if wide else values[1]))
         return jnp.concatenate(columns, axis=-1)
 
     def first_kernel(self, at_ref, *refs):
         place = 0
         for side, pieces in enumerate(self.sides):
-            out = refs[side - 2]
-            for which in range(2):
-                values = self.piece_values(
-                    refs[place:], side, lambda r: r[0, which, 0] if side == 0 else r[0, 0, which]
-                )
-                out[0, which] = sent(values, self.wide[side])
+            goes, stays = refs[2 * side - 4], refs[2 * side - 3]
+            bit = at_ref[1 + side]
+            for z in range(self.count):
+                for which in range(2):
+                    values = self.piece_values(refs[place:], side, z, 1 - bit, which, at_ref[0])
+                    goes[z, which] = sent(values, self.wide[side])
+                    stays[z, which] = self.piece_values(
+                        refs[place:], side, z, bit, which, at_ref[0]
+                    )
             place += 2 * len(pieces)
 
     def first(self):
-        ins, in_specs = [], []
-        for side, pieces in enumerate(self.sides):
-            for piece in pieces:
-                ins += piece[:2]
-                in_specs += piece_specs(side, piece, True)
-        outs = [stacked(self.count, 2, r, c, dtype=jnp.bfloat16) for r, c in zip(self.rows, self.columns)]
-        out_specs = [pl.BlockSpec((1,) + o.shape[1:], lambda z, at: (z, 0, 0, 0)) for o in outs]
-        return fold_call(self.first_kernel, self.count, self.at, ins, in_specs, outs, out_specs)
-
-    def first_sent(self, parts):
-        return [exchanged(part, "batch", 1 << side) for side, part in enumerate(parts)]
-
-    def second_kernel(self, at_ref, *refs):
-        place = 0
-        outs = refs[-4:]
-        for side, pieces in enumerate(self.sides):
-            arrays = refs[place : place + 2 * len(pieces)]
-            arrived = refs[place + 2 * len(pieces)]
-            place += 2 * len(pieces) + 1
-            bit = at_ref[2 - side]
-            for which, out in ((1 - bit, outs[2 * side]), (bit, outs[2 * side + 1])):
-                values = self.piece_values(
-                    arrays, side, lambda r: r[0, which, 0] if side == 0 else r[0, 0, which]
-                )
-                values = values + received(arrived[0, which], self.wide[side])
-                out[0] = sent(values, self.wide[side]) if out.dtype == jnp.bfloat16 else values
-
-    def second(self, arrived):
         ins, in_specs, outs = [], [], []
         for side, pieces in enumerate(self.sides):
             for piece in pieces:
                 ins += piece[:2]
-                in_specs += piece_specs(side, piece, False)
-            ins.append(arrived[side])
-            in_specs.append(pl.BlockSpec((1,) + arrived[side].shape[1:], lambda z, at: (z, 0, 0, 0)))
+                in_specs += [piece_spec(piece)] * 2
+            shape = (self.count, 2, self.rows[side], self.columns[side])
+            outs += [stacked(*shape, dtype=jnp.bfloat16), far_off(*shape, dtype=jnp.float32)]
+        return fold_call(self.first_kernel, 1, self.at, ins, in_specs, outs, [whole_block(o) for o in outs])
+
+    def first_sent(self, parts):
+        self.stays = parts[1::2]
+        return [exchanged(part, "batch", 1 << side) for side, part in enumerate(parts[::2])]
+
+    def second_kernel(self, at_ref, *refs):
+        outs = refs[-4:]
+        for side in range(2):
+            stays, arrived = refs[2 * side], refs[2 * side + 1]
+            bit = at_ref[2 - side]
+            for z in range(self.count):
+                for which, out in ((1 - bit, outs[2 * side]), (bit, outs[2 * side + 1])):
+                    values = stays[z, which] + received(arrived[z, which], self.wide[side])
+                    out[z] = sent(values, self.wide[side]) if out.dtype == jnp.bfloat16 else values
+
+    def second(self, arrived):
+        ins, outs = [], []
+        for side in range(2):
+            ins += [far_away(self.stays[side]), arrived[side]]
             shape = (self.count, self.rows[side], self.columns[side])
-            outs += [stacked(*shape, dtype=jnp.bfloat16), stacked(*shape)]
-        out_specs = [pl.BlockSpec((1,) + o.shape[1:], lambda z, at: (z, 0, 0)) for o in outs]
-        return fold_call(self.second_kernel, self.count, self.at, ins, in_specs, outs, out_specs)
+            outs += [stacked(*shape, dtype=jnp.bfloat16), far_off(*shape, dtype=jnp.float32)]
+        return fold_call(
+            self.second_kernel, 1, self.at, ins, [whole_block(a) for a in ins], outs,
+            [whole_block(out) for out in outs],
+        )
 
     def second_sent(self, out):
         return [exchanged(out[0], "batch", 2), exchanged(out[2], "batch", 1)], [out[1], out[3]]
@@ -272,18 +311,19 @@
 
     def third(self, arrived, kept):
         radix = min(4, self.count)
-        ins = kept + arrived
+        ins = [far_away(part) for part in kept] + arrived
         in_specs = [pl.BlockSpec((radix,) + a.shape[1:], lambda z, at: (z, 0, 0)) for a in ins]
         shape = (self.count // radix, self.rows[0], sum(self.columns))
-        outs = [stacked(*shape)] + [stacked(*shape, dtype=jnp.bfloat16)] * (radix - 1)
+        outs = [far_off(*shape, dtype=jnp.float32)] + [stacked(*shape, dtype=jnp.bfloat16)] * (radix - 1)
         out_specs = [pl.BlockSpec((1,) + o.shape[1:], lambda z, at: (z, 0, 0)) for o in outs]
         return fold_call(
-            functools.partial(self.third_kernel, radix), self.count // radix, self.at, ins, in_specs, outs, out_specs
+            functools.partial(self.third_kernel, radix), self.count // radix, self.at, ins, in_specs, outs, out_specs, True
         )
 
-    def third_sent(self, out):
+    def third_sent(self, out, *earlier):
         radix = min(4, self.count)
-        terms = [out[0]] + [exchanged(part, "batch", 4 * d) for d, part in enumerate(out) if d > 0]
+        arrived = [exchanged(part, "batch", 4 * d) for d, part in enumerate(out) if d > 0]
+        terms = [out[0]] + [after(part, *earlier) if earlier else part for part in arrived]
         total = None
         for term in terms:
             value = received(term, self.wide[1]) if term.dtype == jnp.bfloat16 else term
@@ -325,13 +365,14 @@
     masked = (jnp.where(first, keys, none), jnp.where(first, none, keys))
     values = v_ref[...].T
     queries = q_ref[...] * jnp.bfloat16(1.0 / math.sqrt(size))
-    outs = []
+    products = [matmul(masked[h], queries, NT) for h in range(2)]
+    probs = []
     for h in range(2):
-        scores = matmul(masked[h], queries, NT) + bias[half]
+        scores = products[h] + bias[half]
         weights = jnp.exp(scores - jnp.max(scores, axis=0, keepdims=True))
-        probs = halved(weights * (1.0 / jnp.sum(weights, axis=0, keepdims=True)))
-        prob_ref[0, 0, h] = probs
-        outs.append(matmul(values[h * size : (h + 1) * size], probs))
+        probs.append(halved(weights * (1.0 / jnp.sum(weights, axis=0, keepdims=True))))
+        prob_ref[0, 0, h] = probs[h]
+    outs = [matmul(values[h * size : (h + 1) * size], probs[h]) for h in range(2)]
     context = jnp.concatenate(outs, axis=0)
     turned_ref[...] = halved(context)
     context_ref[...] = halved(context.T)
@@ -368,13 +409,13 @@
             scratch_shapes=[pltpu.VMEM((2, rows, rows), jnp.float32)],
         ),
         out_shape=[
-            stacked(tokens, width, dtype=jnp.bfloat16),
-            stacked(width, tokens, dtype=jnp.bfloat16),
-            stacked(pairs, 2, 2, rows, rows, dtype=jnp.bfloat16),
+            far_off(tokens, width),
+            far_off(width, tokens),
+            far_off(pairs, 2, 2, rows, rows),
         ],
-        compiler_params=pltpu.CompilerParams(vmem_limit_bytes=56 << 20),
+        compiler_params=pltpu.CompilerParams(vmem_limit_bytes=24 << 20),
         cost_estimate=COST,
-    )(at, triples, triples, triples)
+    )(at, *[far_away(triples)] * 3)
 
 
 def attend_back_kernel(at, q_ref, k_ref, v_ref, context_ref, grad_ref, prob_ref, out_ref, sum_ref):
@@ -442,10 +483,10 @@
                 pl.BlockSpec((1, 2, 1, width // 2), lambda r, j, i, at: (r, 0, 0, 0)),
             ],
         ),
-        out_shape=[stacked(*triples.shape, dtype=jnp.bfloat16), stacked(2, 2, 1, width // 2)],
-        compiler_params=pltpu.CompilerParams(vmem_limit_bytes=56 << 20),
+        out_shape=[pltpu.VMEM(triples.shape, jnp.bfloat16), stacked(2, 2, 1, width // 2)],
+        compiler_params=pltpu.CompilerParams(vmem_limit_bytes=24 << 20),
         cost_estimate=LONG_COST,
-    )(at, triples, triples, triples, context, grad, probs)
+    )(at, *[far_away(triples)] * 3, context, grad, probs)
 
 
 def bucket_of(at, token_count):
@@ -465,7 +506,7 @@
     return pl.BlockSpec(array.shape, lambda *_: (0,) * len(array.shape))
 
 
-def kernel_call(kernel, grid, at, ins, in_specs, outs, out_specs, scratch=(), long=False, vmem=56):
+def kernel_call(kernel, grid, at, ins, in_specs, outs, out_specs, scratch=(), long=False, vmem=OTHER_VMEM):
     return pl.pallas_call(
         kernel,
         grid_spec=pltpu.PrefetchScalarGridSpec(
@@ -478,9 +519,12 @@
     )(at, *ins)
 
 
-def entry_kernel(at, tokens, pos, weight, shift, hidden0, entry, triples, table):
+def entry_kernel(
+    at, tokens, pos, weight, misc, hidden0, entry, triples, vectors, bias_lines, table, shift
+):
     step = pl.program_id(0)
-    rows = tokens.shape[0]
+    rows, width = tokens.shape
+    quarter = width // 2
 
     @pl.when(step == 0)
     def _():
@@ -489,6 +533,15 @@
         span = 2 * count // (at.shape[0] - LENGTHS)
         short = jnp.concatenate([long[:span]] * (count // span), axis=0)
         table[...] = jnp.where(at[SLOT_COUNT] == 2, long, short)
+        for core in range(2):
+            lines = misc[core].astype(jnp.float32).T
+            vectors[4 * core : 4 * core + 4] = lines[:4]
+            bias_lines[2 * core : 2 * core + 2] = lines[4:6]
+        shift[...] = jnp.zeros_like(shift)
+        for other in range(2):
+            here = pl.ds(pl.multiple_of((other ^ at[0]) * quarter, quarter), quarter)
+            shift[other, :, :quarter] = vectors[BQ : BQ + 1, here]
+            shift[other, :, 2 * quarter :] = vectors[BV : BV + 1, here]
 
     half_steps = pl.num_programs(0) // 2
     here = pl.ds(pl.multiple_of((step % half_steps) * rows, rows), rows)
@@ -500,27 +553,34 @@
         triples[other] = halved(matmul(values, weight[other]) + shift[other])
 
 
-def entered(at, tokens, pos, qkv, shift):
+def entered(at, tokens, pos, qkv, misc):
     token_count, width = tokens.shape
     triple = qkv.shape[2]
     outs = [
-        stacked(token_count, width),
-        stacked(width, token_count, dtype=jnp.bfloat16),
-        stacked(2, token_count, triple, dtype=jnp.bfloat16),
+        far_off(token_count, width, dtype=jnp.float32),
+        far_off(width, token_count),
+        far_off(2, token_count, triple),
+        stacked(8, width),
+        stacked(4, width),
     ]
     return kernel_call(
         entry_kernel,
         (token_count // CHUNK,),
         at,
-        [tokens, pos, qkv, shift],
-        tiles(tokens) + [held(pos), held(qkv), held(shift)],
+        [far_away(tokens), near_by(pos), near_by(qkv), near_by(misc)],
+        tiles(tokens) + [HERE, HERE, HERE],
         outs,
-        tiles(outs[0], outs[1]) + [pl.BlockSpec((2, CHUNK, triple), lambda i, at: (0, i, 0))],
-        [pltpu.VMEM((token_count // 2, width), jnp.float32)],
-    )
-
-
-BO, B2, G1, E1, G2, E2 = 2, 3, 4, 5, 6, 7
+        tiles(outs[0], outs[1])
+        + [pl.BlockSpec((2, CHUNK, triple), lambda i, at: (0, i, 0))]
+        + [whole_block(out) for out in outs[3:]],
+        [
+            pltpu.VMEM((token_count // 2, width), jnp.float32),
+            pltpu.VMEM((2, 1, triple), jnp.float32),
+        ],
+    )
+
+
+BQ, BV, BO, B2, G1, E1, G2, E2 = range(8)
 
 
 def normal(values):
@@ -544,45 +604,11 @@
     ]
 
 
-def weight_copies(at, up, down, up_held, down_held, sems):
-    half, quarter = down.shape[1] // 2, down.shape[2]
-    copies = [pltpu.make_async_copy(up, up_held, sems.at[0])]
-    for other in range(2):
-        start = pl.multiple_of((other ^ at[0]) * half, half)
-        for k in range(2):
-            copies.append(
-                pltpu.make_async_copy(
-                    down.at[k, pl.ds(start, half)],
-                    down_held.at[pl.ds(other * half, half), pl.ds(k * quarter, quarter)],
-                    sems.at[1 + 2 * other + k],
-                )
-            )
-    return copies[:1], copies[1:]
-
-
-def weight_scratch(up, down):
-    return [
-        pltpu.VMEM(up.shape, jnp.bfloat16),
-        pltpu.VMEM((down.shape[1], 2 * down.shape[2]), jnp.bfloat16),
-        pltpu.SemaphoreType.DMA((5,)),
-    ]
-
-
-def at_first(copies, act):
-    @pl.when(pl.program_id(0) == 0)
-    def _():
-        for copy in copies:
-            act(copy)
-
-
 def forward_kernel(
     at, hidden0, context, out_weight, vectors, up, up_bias, down,
-    entry2, normed1, inverse1, active, slope, normed2, inverse2, block_out, pooled, units,
-    up_held, down_held, sems, acts,
+    entry2, normed1, inverse1, active, slope, normed2, inverse2, block_out, pooled, units, acts,
 ):
     step = pl.program_id(0)
-    up_copies, down_copies = weight_copies(at, up, down, up_held, down_held, sems)
-    at_first(up_copies + down_copies, lambda copy: copy.start())
     rows, width = hidden0.shape
     token_count = rows * pl.num_programs(0)
     resid = hidden0[...] + matmul(context[...], out_weight[...]) + vectors[BO : BO + 1]
@@ -591,22 +617,20 @@
     normed1[...], inverse1[...] = halved(normed), inverse
     entry = halved(hidden1)
     entry2[...] = entry.T
-    at_first(up_copies, lambda copy: copy.wait())
     half = up.shape[2]
     span = half // BLOCKS
     for other in range(2):
         for block in range(BLOCKS):
             here = slice(block * span, (block + 1) * span)
             there = slice(other * half + block * span, other * half + (block + 1) * span)
-            values = matmul(entry, up_held[other, :, here]) + up_bias[other, :, here]
+            values = matmul(entry, up[other, :, here]) + up_bias[other, :, here]
             cumulative = 0.5 + 0.5 * lax.erf(values * ROOT_HALF)
             acted = halved(values * cumulative)
             acts[:, there] = acted
             active[there] = acted.T
             density = jnp.exp(-0.5 * values * values) * (1.0 / ROOT_TWO_PI)
             slope[:, there] = halved(cumulative + values * density)
-    at_first(down_copies, lambda copy: copy.wait())
-    total = hidden1 + vectors[B2 : B2 + 1] + matmul(acts[...], down_held[...])
+    total = hidden1 + vectors[B2 : B2 + 1] + matmul(acts[...], down[...])
     normed, inverse = normal(total)
     hidden2 = normed * vectors[G2 : G2 + 1] + vectors[E2 : E2 + 1]
     normed2[...], inverse2[...] = halved(normed), inverse
@@ -643,14 +667,14 @@
     hidden = 2 * up.shape[2]
     half = functools.partial(stacked, dtype=jnp.bfloat16)
     outs = [
-        half(width, token_count),
-        half(token_count, width),
+        far_off(width, token_count),
+        far_off(token_count, width),
         stacked(token_count, 1),
-        half(hidden, token_count),
-        half(token_count, hidden),
-        half(token_count, width),
+        pltpu.VMEM((hidden, token_count), jnp.bfloat16),
+        pltpu.VMEM((token_count, hidden), jnp.bfloat16),
+        far_off(token_count, width),
         stacked(token_count, 1),
-        half(token_count, width),
+        far_off(token_count, width),
         stacked(slots, width),
         half(slots, width + LANES),
     ]
@@ -658,13 +682,13 @@
         forward_kernel,
         (token_count // CHUNK,),
         at,
-        [hidden0, context, out_weight, vectors, up, up_bias, down],
+        [far_away(hidden0), far_away(context), out_weight, vectors, near_by(up), up_bias, near_by(down)],
         tiles(hidden0, context)
-        + [held(out_weight), held(vectors), ANYWHERE, held(up_bias), ANYWHERE],
+        + [held(out_weight), held(vectors), HERE, held(up_bias), HERE],
         outs,
         tiles(hidden0, *outs[:8])[1:] + [whole_block(out) for out in outs[8:]],
-        weight_scratch(up, down) + [pltpu.VMEM((CHUNK, hidden), jnp.bfloat16)],
-        vmem=56,
+        [pltpu.VMEM((CHUNK, hidden), jnp.bfloat16)],
+        vmem=FORWARD_VMEM,
     )
 
 
@@ -744,9 +768,9 @@
 def loss_back(at, units, others, pooled, normed2, inverse2, vectors):
     token_count, width = normed2.shape
     half = functools.partial(stacked, dtype=jnp.bfloat16)
-    ins = [units, others, pooled, normed2, inverse2, vectors]
+    ins = [units, others, pooled, far_away(normed2), inverse2, vectors]
     outs = [
-        stacked(token_count, width),
+        far_off(token_count, width, dtype=jnp.float32),
         half(token_count, width),
         stacked(3, width),
     ]
@@ -765,30 +789,24 @@
 def backward_kernel(
     at, dresid2, dresid2_half, slope, up, down, normed1, inverse1, vectors,
     dpre, dpre_sum, dresid, dresid_half, sums,
-    up_held, down_held, sems,
 ):
-    up_copies, down_copies = weight_copies(at, up, down, up_held, down_held, sems)
-    at_first(down_copies + up_copies, lambda copy: copy.start())
-
     @pl.when(pl.program_id(0) == 0)
     def _():
         dpre_sum[...] = jnp.zeros_like(dpre_sum)
         sums[...] = jnp.zeros_like(sums)
 
-    at_first(down_copies, lambda copy: copy.wait())
     half = up.shape[2]
     span = half // BLOCKS
     grad = dresid2_half[...]
     for block in range(2 * BLOCKS):
         here = slice(block * span, (block + 1) * span)
-        dactive = matmul(grad, down_held[here], NT)
+        dactive = matmul(grad, down[here], NT)
         values = dactive * slope[:, here].astype(jnp.float32)
         dpre_sum[:, here] += jnp.sum(values, axis=0, keepdims=True)
         dpre[:, here] = halved(values)
-    at_first(up_copies, lambda copy: copy.wait())
     dhidden = dresid2[...]
     for other in range(2):
-        dhidden += matmul(dpre[:, other * half : (other + 1) * half], up_held[other], NT)
+        dhidden += matmul(dpre[:, other * half : (other + 1) * half], up[other], NT)
     normed = normed1[...].astype(jnp.float32)
     values = norm_back(dhidden, normed, inverse1[...], vectors[G1 : G1 + 1])
     dresid[...] = values
@@ -803,9 +821,9 @@
     hidden = 2 * up.shape[2]
     half = functools.partial(stacked, dtype=jnp.bfloat16)
     outs = [
-        half(token_count, hidden),
+        pltpu.VMEM((token_count, hidden), jnp.bfloat16),
         stacked(1, hidden),
-        stacked(token_count, width),
+        far_off(token_count, width, dtype=jnp.float32),
         half(token_count, width),
         stacked(3, width),
     ]
@@ -814,18 +832,19 @@
         backward_kernel,
         (token_count // CHUNK,),
         at,
-        [dresid2, dresid2_half, slope, up, down, normed1, inverse1, vectors],
-        tiles(dresid2, dresid2_half, slope) + [ANYWHERE, ANYWHERE] + tiles(normed1, inverse1)
+        [far_away(dresid2), dresid2_half, near_by(slope), near_by(up), near_by(down), far_away(normed1), inverse1, vectors],
+        tiles(dresid2, dresid2_half, slope) + [HERE, HERE] + tiles(normed1, inverse1)
         + [held(vectors)],
         outs,
         out_specs[:1] + [whole_block(outs[1])] + out_specs[1:] + [whole_block(outs[4])],
-        weight_scratch(up, down),
-        vmem=56,
+        vmem=BACKWARD_VMEM,
         long=True,
     )
 
 
-def leave_kernel(at, dresid1, dtriples, qkv, lines, input_grad, last_own, last_away, total):
+def leave_kernel(
+    at, dresid1, dtriples, qkv, dsums, sums1, sums2, dpre_sum, input_grad, last_own, last_away, total, turned,
+):
     step = pl.program_id(0)
     rows = dresid1.shape[0]
     values = dresid1[...]
@@ -854,14 +873,28 @@
         left, right = columns[:, : count // 2], columns[:, count // 2 :]
         last_own[:, : count // 2] = jnp.where(at[0] == 0, left, right)
         last_away[:, : count // 2] = halved(jnp.where(at[0] == 0, right, left))
-        last_own[:, count // 2 :] = lines[0].T
-        last_away[:, count // 2 :] = halved(two_words(lines[1].T))
-
-
-def left(at, dresid1, dtriples, qkv, lines):
+        width = long.shape[1]
+        first = [jnp.concatenate([dsums[0, k], dsums[1, k]], axis=1) for k in range(2)]
+        swapped = [jnp.concatenate([dsums[1, k], dsums[0, k]], axis=1) for k in range(2)]
+        heads = [jnp.where(at[0] == 0, a, b) for a, b in zip(first, swapped)]
+        vectors = [heads + [sums1[:1], sums2[:1]], [sums1[1:2], sums1[2:3], sums2[1:2], sums2[2:3]]]
+        blank = jnp.zeros((LANES - 4, width), jnp.float32)
+        vectors = [jnp.concatenate(rows + [blank], axis=0).T for rows in vectors]
+        lane = lax.broadcasted_iota(jnp.int32, (width, LANES), 1)
+        for other, (out, words) in enumerate(((last_own, False), (last_away, True))):
+            row = dpre_sum[:, other * 2 * width : (other + 1) * 2 * width]
+            turned[...] = jnp.broadcast_to(row, (LANES, 2 * width)).T
+            lines = jnp.where(at[0] == other, vectors[0], vectors[1])
+            for k in range(2):
+                lines = jnp.where(lane == 4 + k, turned[pl.ds(k, width, 2)], lines)
+            out[:, count // 2 :] = halved(two_words(lines)) if words else lines
+
+
+def left(at, dresid1, dtriples, qkv, dsums, sums1, sums2, dpre_sum):
     token_count, width = dresid1.shape
     triple = qkv.shape[2]
     columns = token_count // 4 + LANES
+    small = [dsums, sums1, sums2, dpre_sum]
     outs = [
         stacked(token_count, width),
         stacked(width, columns),
@@ -871,12 +904,16 @@
         leave_kernel,
         (token_count // CHUNK,),
         at,
-        [dresid1, dtriples, qkv, lines],
+        [far_away(dresid1), near_by(dtriples), qkv] + small,
         tiles(dresid1)
-        + [pl.BlockSpec((2, CHUNK, triple), lambda i, at: (0, i, 0)), held(qkv), held(lines)],
+        + [pl.BlockSpec((2, CHUNK, triple), lambda i, at: (0, i, 0)), held(qkv)]
+        + [held(a) for a in small],
         outs,
         tiles(outs[0]) + [whole_block(out) for out in outs[1:]],
-        [pltpu.VMEM((token_count // 2, width), jnp.float32)],
+        [
+            pltpu.VMEM((token_count // 2, width), jnp.float32),
+            pltpu.VMEM((2 * width, LANES), jnp.float32),
+        ],
         long=True,
     )
 
@@ -888,26 +925,27 @@
     else:
         both = matmul(values, right_ref[...])
         first, second = both[:, : both.shape[1] // 2], both[:, both.shape[1] // 2 :]
+    first, second = halved(first), halved(second)
     if natural_order:
         first, second = jnp.where(at[0] == 0, first, second), jnp.where(at[0] == 0, second, first)
-    own[...], away[...] = first, halved(second)
-
-
-def product(at, left_array, right_array, natural_order=False):
+    own[...], away[...] = first, second
+
+
+def product(at, left_array, right_array, natural_order=False, near=None):
     rows, depth = left_array.shape
     columns = right_array.size // depth // 2
     tile = rows // 6 if rows > 1024 else rows // 3
-    outs = [stacked(rows, columns), stacked(rows, columns, dtype=jnp.bfloat16)]
+    outs = [stacked(rows, columns, dtype=jnp.bfloat16)] * 2
     return kernel_call(
         functools.partial(product_kernel, natural_order),
         (rows // tile,),
         at,
-        [left_array, right_array],
-        [pl.BlockSpec((tile, depth), lambda i, at: (i, 0)), held(right_array)],
+        [near_by(left_array) if near == 0 else left_array, near_by(right_array) if near == 1 else right_array],
+        [pl.BlockSpec((tile, depth), lambda i, at: (i, 0)), HERE if near == 1 else held(right_array)],
         outs,
         [pl.BlockSpec((tile, columns), lambda i, at: (i, 0))] * 2,
         long=True,
-        vmem=56,
+        vmem=PRODUCT_VMEM,
     )
 
 
@@ -950,7 +988,7 @@
     pos_half = pos_table.shape[0]
     slot_count = lengths.shape[2]
 
-    misc = jnp.concatenate([layer_vectors.T, up_bias.reshape(2, rows).T], axis=1)
+    misc = jnp.concatenate([layer_vectors.T, up_bias.reshape(rows, 2)], axis=1)
     misc = jnp.pad(misc, ((0, 0), (0, LANES - misc.shape[1])))
     entry_block = halved(
         jnp.concatenate([attn_weight[0], attn_weight[1], attn_weight[2], pos_table.T, misc], axis=1)
@@ -962,10 +1000,10 @@
     pos_stop = triple + pos_half
     entry_gather = Gather(entry_block, width)
     entry_gather.far()
+    down_both = lax.all_gather(
+        after(halved(down_weight), entry_gather.blocks), ("stream", "batch"), axis=0, tiled=True
+    )
     entry_gather.near((2, 1))
-    down_both = lax.all_gather(
-        after(halved(down_weight), *entry_gather.sides), ("stream", "batch"), axis=0, tiled=True
-    )
     middle_gather = Gather(
         after(middle_block, *entry_gather.sides), (hidden_half + quarter + LANES) // 2
     )
@@ -979,43 +1017,37 @@
             (pos_stop, pos_stop + LANES, 2, "stream", 0, 0),
         ),
         [
-            stacked(2, devices, rows, triple, dtype=jnp.bfloat16),
-            stacked(devices, rows, 2 * pos_half, dtype=jnp.bfloat16),
-            stacked(2, devices, rows, LANES, dtype=jnp.bfloat16),
+            pltpu.VMEM((2, devices, rows, triple), jnp.bfloat16),
+            pltpu.VMEM((devices, rows, 2 * pos_half), jnp.bfloat16),
+            pltpu.VMEM((2, devices, rows, LANES), jnp.bfloat16),
         ],
     )
     qkv = qkv_blocks.reshape(2, width, triple)
     pos_full = pos_blocks.reshape(width, 2 * pos_half)
-    misc_full = misc_blocks.reshape(2, width, LANES)[:, :, :6].astype(jnp.float32)
-    vectors = misc_full[:, :, :4].transpose(0, 2, 1).reshape(8, width)
-    biases = misc_full[:, :, 4:].reshape(2, devices, rows, 2).transpose(0, 1, 3, 2)
-    biases = biases.reshape(2, 1, hidden_half)
-
     def own_first(pair):
         return jnp.where(upper, pair[::-1], pair)
 
-    shift = own_first(vectors[:2].reshape(2, 2, quarter).transpose(1, 0, 2))
-    shift = jnp.stack([shift[:, 0], jnp.zeros((2, quarter), jnp.float32), shift[:, 1]], axis=1)
-    hidden0, entry, triples = entered(
-        at, tokens[0], pos_full, qkv, shift.reshape(2, 1, triple)
-    )
+    hidden0, entry, triples, vectors, bias_lines = entered(
+        at, tokens[0], pos_full, qkv, misc_blocks.reshape(2, width, LANES)
+    )
+    biases = bias_lines.reshape(2, 2, width).transpose(0, 2, 1).reshape(2, 1, hidden_half)
     middle_gather.near((2, 1), triples)
     context_half, context_turned, probs = attend(after(at, *middle_gather.sides), triples)
     middle_gather.near((1, 2), context_half)
-    up_blocks, out_blocks = middle_gather.placed(
+    up_blocks, out_blocks, down = middle_gather.placed(
         after(at, context_half),
         (
             (0, hidden_half, 0, "relative", 0, 0),
             (hidden_half, hidden_half + quarter, 1, "", 0, quarter),
         ),
         [
-            stacked(2, devices, rows, hidden_half, dtype=jnp.bfloat16),
+            pltpu.VMEM((2, devices, rows, hidden_half), jnp.bfloat16),
             stacked(devices, rows, width, dtype=jnp.bfloat16),
         ],
+        down_both.reshape(2, 2 * hidden_half, quarter),
     )
     up = up_blocks.reshape(2, width, hidden_half)
     out_full = out_blocks.reshape(width, width)
-    down = down_both.reshape(2, 2 * hidden_half, quarter)
     (entry2, normed1, inverse1, active, slope, normed2, inverse2, block_out, pooled, units) = forward(
         at, hidden0, context_half, out_full, vectors, up, own_first(biases), down
     )
@@ -1036,7 +1068,7 @@
     def blocks(values):
         return values.reshape(devices // 4, 2, 2, values.shape[0] // devices, values.shape[1])
 
-    down_own, down_away = product(at, active, dresid2_half, True)
+    down_own, down_away = product(at, active, dresid2_half, True, near=0)
     down_in = exchanged(down_away, "stream", 1)
     by_rows = down_weight.shape[0] % 32 == 0
     half_rows = down_weight.shape[0] // 2
@@ -1056,7 +1088,7 @@
     down_fold.at = after(at, dresid1_half, *down_first)
     down_parts = down_fold.second(down_first)
     down_second, down_kept = down_fold.second_sent(down_parts)
-    up_own, up_away = product(after(at, *down_parts), entry2, dpre)
+    up_own, up_away = product(after(at, *down_parts), entry2, dpre, near=1)
     up_in = exchanged(up_away, "stream", 1)
     out_own, out_away = product(
         after(at, up_away, *down_second), context_turned, dresid1_half, True
@@ -1064,7 +1096,6 @@
     out_in = exchanged(out_away, "stream", 1)
     down_fold.at = after(at, out_own, *down_second)
     down_parts = down_fold.third(down_second, down_kept)
-    down_sum = down_fold.third_sent(down_parts)
     third = hidden_half // 3
     up_pair = (blocks(up_own), blocks(up_in))
     out_pair = (blocks(out_own), blocks(out_in))
@@ -1079,30 +1110,20 @@
     middle_first = middle_fold.first_sent(middle_parts)
     dcontext_half = halved(matmul(after(dresid1_half, *middle_parts), out_full, NT))
     dtriples, dsums = attend_back(at, triples, context_half, dcontext_half, probs)
-    middle_fold.at = after(at, dtriples, *middle_first)
+    qkv_own, qkv_away = product(at, entry, dtriples, near=1)
+    down_sum = down_fold.third_sent(down_parts, qkv_away)
+    qkv_in = exchanged(qkv_away, "stream", 1)
+    middle_fold.at = after(at, qkv_away, *middle_first)
     middle_parts = middle_fold.second(middle_first)
     middle_second, middle_kept = middle_fold.second_sent(middle_parts)
-    qkv_own, qkv_away = product(after(at, *middle_parts), entry, dtriples)
-    qkv_in = exchanged(qkv_away, "stream", 1)
-    dsums = own_first(dsums[:, :, 0]).transpose(1, 0, 2).reshape(2, width)
-    lines = own_first(
-        jnp.concatenate([dsums, sums1[:1], sums2[:1], sums1[1:], sums2[1:]], axis=0).reshape(2, 4, width)
-    )
-    bias_lines = dpre_sum.reshape(2, devices, 2, rows).transpose(0, 2, 1, 3).reshape(2, 2, width)
-    lines = jnp.concatenate(
-        [lines, bias_lines, jnp.zeros((2, LANES - 6, width), jnp.float32)], axis=1
-    )
     input_grad, last_own, last_away = left(
-        after(at, qkv_away, *middle_second), dresid1, dtriples, qkv, lines
+        after(at, qkv_away, *middle_parts), dresid1, dtriples, qkv, dsums, sums1, sums2, dpre_sum
     )
     last_in = exchanged(last_away, "stream", 1)
-    middle_fold.at = after(at, input_grad, *middle_second)
-    middle_parts = middle_fold.third(middle_second, middle_kept)
-    middle_sum = middle_fold.third_sent(middle_parts)
     qkv_pair = (blocks(qkv_own), blocks(qkv_in))
     last_pair = (blocks(last_own), blocks(last_in))
     entry_fold = Fold(
-        after(at, *middle_parts),
+        at,
         [
             [qkv_pair + (rows, 0, quarter, 0, False), qkv_pair + (rows, 0, quarter, 1, False)],
             [
@@ -1113,8 +1134,14 @@
         ],
         wide=True,
     )
-    entry_first = entry_fold.first_sent(entry_fold.first())
-    entry_second, entry_kept = entry_fold.second_sent(entry_fold.second(entry_first))
+    entry_parts = entry_fold.first()
+    entry_first = entry_fold.first_sent(entry_parts)
+    middle_fold.at = after(at, *entry_parts, *middle_second)
+    middle_parts = middle_fold.third(middle_second, middle_kept)
+    entry_fold.at = after(at, *middle_parts)
+    entry_parts = entry_fold.second(entry_first)
+    middle_sum = middle_fold.third_sent(middle_parts, *entry_parts)
+    entry_second, entry_kept = entry_fold.second_sent(entry_parts)
     entry_sum = entry_fold.third_sent(entry_fold.third(entry_second, entry_kept))
 
     down_grad = down_sum
@@ -1129,7 +1156,7 @@
     down_all = renew(down_grad, down_moment, down_weight, down_average, RATE)
     vector_grad = entry_sum[:, pos_stop : pos_stop + 4].T
     vector_all = renew(vector_grad, vector_moment, layer_vectors, vector_average, RATE)
-    bias_grad = entry_sum[:, pos_stop + 4 : pos_stop + 6].T.reshape(-1)
+    bias_grad = entry_sum[:, pos_stop + 4 : pos_stop + 6].reshape(-1)
     bias_all = renew(bias_grad, bias_moment, up_bias, bias_average, RATE)
     pos_grad = entry_sum[:, triple:pos_stop].T
     pos_all = renew(pos_grad, pos_moment, pos_table, pos_average, POS_RATE)

time: 395 us -> 337 us (0.85)
  Pallas kernels: 188 us -> 162 us
  local copies, waits for them, and re-layouts: 40.6 us -> 16.7 us
    pallas_call x9, Pallas kernels: 114 us -> 84.5 us  [kernel_call(): pl.pallas_call(kernel, grid_spec=pltpu.PrefetchScalarGridSpec(num_scalar_...]
    unnamed x138 -> x108, local copies, waits for them, and re-layouts: 29.3 us -> 7.73 us
    pallas_call x9, Pallas kernels: 27 us -> 32.6 us  [fold_call(): pl.pallas_call(kernel, grid_spec=pltpu.PrefetchScalarGridSpec(num_scalar_...]
  transfers between devices with their start and end apart: 52 -> 52, of which waited for: 23 -> 28; matrix products, arithmetic and copies ran while one was open for 7% -> 6% of each run, Pallas kernels for 33% -> 33%
where the time goes in v1:
time: 337 us; the launch traced here: 336 us
  Pallas kernels  162 us (48%)
  waiting for transfers between devices  72.4 us (21%)
  starting transfers between devices  55.4 us (16%)
  local copies, waits for them, and re-layouts  16.7 us (5%)
  between operations  14.8 us (4%)
  other arithmetic  12.8 us (4%)
    pallas_call x9, Pallas kernels, kernel_call(): pl.pallas_call(kernel, grid_spec=pltpu.PrefetchScalarGridSpec(num_scalar_...  84.5 us
    ppermute x51, waiting for transfers between devices, exchanged(): lax.ppermute(block, axis, [(place, place ^ mask) for place in range(count)])  71.3 us
    ppermute x51, starting transfers between devices, exchanged(): lax.ppermute(block, axis, [(place, place ^ mask) for place in range(count)])  55.3 us
    pallas_call x9, Pallas kernels, fold_call(): pl.pallas_call(kernel, grid_spec=pltpu.PrefetchScalarGridSpec(num_scalar_...  32.6 us
    pallas_call x1, Pallas kernels, attend_back(): pl.pallas_call(attend_back_kernel, grid_spec=pltpu.PrefetchScalarGridSpec...  19.7 us
    pallas_call x1, Pallas kernels, attend(): pl.pallas_call(attend_kernel, grid_spec=pltpu.PrefetchScalarGridSpec(num_...  19 us
    unnamed x108, local copies, waits for them, and re-layouts  7.73 us
  transfers between devices with their start and end apart: 52, of which 28 were waited for; matrix products, arithmetic and copies ran while one was open for 6% of the time, Pallas kernels for 33%

profile of v1, /device:TPU:0, one launch (start us, length us, event | category | flops | bytes accessed | tf_op | source)
XLA Modules:
  0.0 335.6 jit_solution(3741280770561188374)
XLA Ops:
  10.8 5.1 %collective-permute-start.2 = (bf16[1,48,1536]{2,1,0:T(8,128)(2,1)S(1)}, bf16[1,48,1536]{2,1,0:T(8,128)(2,1)S(1)}, u32[]{:S(2)}, u32[]{:S(2)}) collective-permute-start(bf16[1,48,1536]{2,1,0:T(8,128)(2,1)S(1)} %constant_dynamic-update-slice_fusion), channel_id=1, source_target_pairs={{0,12},{1,13},{2,14},{3,15},{4,8},{5,9},{6,10},{7,11},{8,4},{9,5},... | collective-permute-start | bytes 442376 | tf_op jit(solution)/shard_map/ppermute | solution.py:59
  16.6 1.6 convert_element_type.48
  18.2 2.5 collective-permute-done.2
  20.7 7.7 %collective-permute-done.1 = bf16[1,48,1536]{2,1,0:T(8,128)(2,1)S(1)} collective-permute-done((bf16[1,48,1536]{2,1,0:T(8,128)(2,1)S(1)}, bf16[1,48,1536]{2,1,0:T(8,128)(2,1)S(1)}, u32[]{:S(2)}, u32[]{:S(2)}) %collective-permute-start.1) | collective-permute-done | bytes 147488 | tf_op jit(solution)/shard_map/ppermute | solution.py:59
  28.6 1.6 collective-permute-start.3
  30.2 1.5 collective-permute-start.4
  31.7 5.0 %collective-permute-done.3 = bf16[4,48,768]{2,1,0:T(8,128)(2,1)S(1)} collective-permute-done((bf16[4,48,768]{2,1,0:T(8,128)(2,1)S(1)}, bf16[4,48,768]{2,1,0:T(8,128)(2,1)S(1)}, u32[]{:S(2)}, u32[]{:S(2)}) %collective-permute-start.3) | collective-permute-done | bytes 294944 | tf_op jit(solution)/shard_map/ppermute | solution.py:59
  38.0 2.4 collective-permute-start.7
  40.4 2.1 collective-permute-start.5
  42.5 1.5 collective-permute-start.8
  44.5 3.6 %collective-permute-done.7 = bf16[1,48,2048]{2,1,0:T(8,128)(2,1)S(1)} collective-permute-done((bf16[1,48,2048]{2,1,0:T(8,128)(2,1)S(1)}, bf16[1,48,2048]{2,1,0:T(8,128)(2,1)S(1)}, u32[]{:S(2)}, u32[]{:S(2)}) %collective-permute-start.7) | collective-permute-done | bytes 196640 | tf_op jit(solution)/shard_map/ppermute | solution.py:59
  48.1 10.2 %collective-permute-done.6 = bf16[1,48,2048]{2,1,0:T(8,128)(2,1)S(1)} collective-permute-done((bf16[1,48,2048]{2,1,0:T(8,128)(2,1)S(1)}, bf16[1,48,2048]{2,1,0:T(8,128)(2,1)S(1)}, u32[]{:S(2)}, u32[]{:S(2)}) %collective-permute-start.6) | collective-permute-done | bytes 196640 | tf_op jit(solution)/shard_map/ppermute | solution.py:59
  60.9 1.5 collective-permute-start.13
  63.7 1.7 shard_map.395
  65.4 8.4 %shard_map.396 = (f32[1024,768]{1,0:T(8,128)}, bf16[768,1024]{1,0:T(8,128)(2,1)}, bf16[2,1024,1152]{2,1,0:T(8,128)(2,1)}, f32[8,768]{1,0:T(8,128)S(1)}, f32[4,768]{1,0:T(4,128)S(1)}) custom-call(s32[13]{0:T(128)S(1)} %concatenate.84.at_ref.at, bf16[1024,768]{1,0:T(8,128)(2,1)} %bitcast.102, bf16[768,512]{1,0:T(8,128)(2,1)S(1)} %bitcast.89, ...), custom_call_target="tpu_custom_call" | custom-call | flops 1000 | bytes 1000 | tf_op jit(solution)/shard_map/pallas_call | solution.py:510
  80.0 19.0 %shard_map.397 = (bf16[1024,768]{1,0:T(8,128)(2,1)}, bf16[768,1024]{1,0:T(8,128)(2,1)}, bf16[6,2,2,512,512]{4,3,2,1,0:T(8,128)(2,1)}) custom-call(s32[13]{0:T(128)S(1)} %concatenate.84.at_ref.at, bf16[2,1024,1152]{2,1,0:T(8,128)(2,1)} %get-tuple-element.141.q_ref.k_ref.v_ref, bf16[2,1024,1152]{2,1,0:T(8,128)(2,1)} %get-tuple-element.141.q_ref.k_ref.v_ref, ...), custom_call_target="tpu_custom_call" | custom-call | flops 1000 | bytes 1000 | tf_op jit(solution)/shard_map/pallas_call | solution.py:394
  99.1 4.4 %collective-permute-done.14 = bf16[8,48,1024]{2,1,0:T(8,128)(2,1)S(1)} collective-permute-done((bf16[8,48,1024]{2,1,0:T(8,128)(2,1)S(1)}, bf16[8,48,1024]{2,1,0:T(8,128)(2,1)S(1)}, u32[]{:S(2)}, u32[]{:S(2)}) %collective-permute-start.14) | collective-permute-done | bytes 786464 | tf_op jit(solution)/shard_map/ppermute | solution.py:59
  103.7 3.2 collective-permute-done.15
  108.2 1.6 reshape.201
  109.8 1.3 collective-permute-done.17.refs_3_
  112.3 4.6 %shard_map.398 = (bf16[2,16,48,1536]{3,2,1,0:T(8,128)(2,1)S(1)}, bf16[16,48,768]{2,1,0:T(8,128)(2,1)S(1)}, bf16[3072,768]{1,0:T(8,128)(2,1)S(1)}) custom-call(s32[13]{0:T(128)S(1)} %concatenate.84.at_ref.at, bf16[16,48,1024]{2,1,0:T(8,128)(2,1)S(1)} %constant_dynamic-update-slice_fusion.13.refs_0_, ...), custom_call_target="tpu_custom_call" | custom-call | flops 1000 | bytes 1000 | tf_op jit(solution)/shard_map/pallas_call | solution.py:166
  116.8 22.8 %shard_map.399 = (bf16[768,1024]{1,0:T(8,128)(2,1)}, bf16[1024,768]{1,0:T(8,128)(2,1)}, f32[1024,1]{1,0:T(8,128)S(1)}, bf16[3072,1024]{1,0:T(8,128)(2,1)S(1)}, b...) custom-call(s32[13]{0:T(128)S(1)} %concatenate.84.at_ref.at, ...), custom_call_target="tpu_custom_call" | custom-call | flops 1000 | bytes 1000 | tf_op jit(solution)/shard_map/pallas_call | solution.py:510
  141.2 2.0 collective-permute-start.20
  144.3 1.5 collective-permute-done.20
  145.8 2.5 collective-permute-start.21
  148.7 2.1 collective-permute-start.23
  150.8 3.0 collective-permute-done.22
  154.8 1.5 collective-permute-done.24.others
  156.3 6.3 %shard_map.400 = (f32[1024,768]{1,0:T(8,128)}, bf16[1024,768]{1,0:T(8,128)(2,1)S(1)}, f32[3,768]{1,0:T(4,128)S(1)}) custom-call(s32[13]{0:T(128)S(1)} %concatenate.84.at_ref.at, bf16[128,896]{1,0:T(8,128)(2,1)S(1)} %bitcast.93, bf16[128,896]{1,0:T(8,128)(2,1)S(1)} %collective-permute-done.24.others, f32[8,768]{1,0:T(8,128)S(1)} %get-tuple-element.159.pooled, ...), custom_call_target="tpu_custom_call" | custom-call | flops 1000 | bytes 1000 | tf_op jit(solution)/shard_map/pallas_call | solution.py:510
  162.6 6.7 %shard_map.401 = (bf16[3072,384]{1,0:T(8,128)(2,1)S(1)}, bf16[3072,384]{1,0:T(8,128)(2,1)S(1)}) custom-call(s32[13]{0:T(128)S(1)} %concatenate.84.at_ref.at, bf16[3072,1024]{1,0:T(8,128)(2,1)S(1)} %get-tuple-element.157.left_ref, bf16[1024,768]{1,0:T(8,128)(2,1)S(1)} %get-tuple-element.162.right_ref.dresid2_half), custom_call_target="tpu_custom_call" | custom-call | flops 999999995904 | bytes 1000000000 | tf_op jit(solution)/shard_map/pallas_call | solution.py:510
  169.5 4.4 %collective-permute-done.25 = bf16[3072,384]{1,0:T(8,128)(2,1)S(1)} collective-permute-done((bf16[3072,384]{1,0:T(8,128)(2,1)S(1)}, bf16[3072,384]{1,0:T(8,128)(2,1)S(1)}, u32[]{:S(2)}, u32[]{:S(2)}) %collective-permute-start.25) | collective-permute-done | bytes 2359328 | tf_op jit(solution)/shard_map/ppermute | solution.py:59
  174.0 2.8 shard_map.402
  177.7 1.6 collective-permute-start.27
  179.4 14.6 %shard_map.403 = (bf16[1024,3072]{1,0:T(8,128)(2,1)S(1)}, f32[1,3072]{1,0:T(1,128)S(1)}, f32[1024,768]{1,0:T(8,128)}, bf16[1024,768]{1,0:T(8,128)(2,1)S(1)}, f32[3,768]{1,0:T(4,128)S(1)}) custom-call(s32[13]{0:T(128)S(1)} %concatenate.84.at_ref.at, f32[1024,768]{1,0:T(8,128)} %get-tuple-element.170.dresid2, bf16[1024,768]{1,0:T(8,128)(2,1)S(1)} %copy-done.9, ...), custom_call_target="tpu_custom_call" | custom-call | flops 999999995904 | bytes 1000000000 | tf_op jit(solution)/shard_map/pallas_call | solution.py:510
  194.0 3.9 %shard_map.404 = (bf16[4,96,384]{2,1,0:T(8,128)(2,1)}, f32[4,96,384]{2,1,0:T(8,128)}, bf16[4,96,384]{2,1,0:T(8,128)(2,1)}, f32[4,96,384]{2,1,0:T(8,128)}) custom-call(s32[13]{0:T(128)S(1)} %concatenate.84.at_ref.at, f32[4,2,96,384]{3,2,1,0:T(8,128)} %get-tuple-element.166.refs_0_, bf16[4,2,96,384]{3,2,1,0:T(8,128)(2,1)} %collective-permute-done.26.refs_1_, ...), custom_call_target="tpu_custom_call" | custom-call | flops 1000 | bytes 1000 | tf_op jit(solution)/shard_map/pallas_call | solution.py:218
  199.4 6.9 %shard_map.405 = (bf16[768,1536]{1,0:T(8,128)(2,1)S(1)}, bf16[768,1536]{1,0:T(8,128)(2,1)}) custom-call(s32[13]{0:T(128)S(1)} %concatenate.84.at_ref.at, bf16[768,1024]{1,0:T(8,128)(2,1)S(1)} %copy-done.7, bf16[1024,3072]{1,0:T(8,128)(2,1)S(1)} %get-tuple-element.182.right_ref), custom_call_target="tpu_custom_call" | custom-call | flops 999999995904 | bytes 1000000000 | tf_op jit(solution)/shard_map/pallas_call | solution.py:510
  206.8 3.1 shard_map.406
  209.9 2.9 shard_map.407
  212.8 2.2 collective-permute-start.50
  215.1 2.1 collective-permute-start.48
  217.2 5.2 %shard_map.408 = (bf16[4,2,48,1024]{3,2,1,0:T(8,128)(2,1)}, f32[4,2,48,1024]{3,2,1,0:T(8,128)}, bf16[4,2,48,896]{3,2,1,0:T(8,128)(2,1)}, f32[4,2,48,896]{3,2,1,0:T(8,128)}) custom-call(s32[13]{0:T(128)S(1)} %concatenate.84.at_ref.at, bf16[4,2,2,48,1536]{4,3,2,1,0:T(8,128)(2,1)S(1)} %bitcast.69, bf16[4,2,2,48,1536]{4,3,2,1,0:T(8,128)(2,1)} %bitcast.26.refs_1_.refs_3_.refs_5_, ...), custom_call_target="tpu_custom_call" | custom-call | flops 1000 | bytes 1000 | tf_op jit(solution)/shard_map/pallas_call | solution.py:218
  222.4 1.3 collective-permute-start.32
  223.7 1.2 collective-permute-start.33
  224.9 1.4 convolution_convert_fusion.grad_ref
  227.6 19.7 %shard_map.409 = (bf16[2,1024,1152]{2,1,0:T(8,128)(2,1)S(1)}, f32[2,2,1,384]{3,2,1,0:T(1,128)S(1)}) custom-call(s32[13]{0:T(128)S(1)} %concatenate.84.at_ref.at, bf16[2,1024,1152]{2,1,0:T(8,128)(2,1)} %get-tuple-element.141.q_ref.k_ref.v_ref, bf16[2,1024,1152]{2,1,0:T(8,128)(2,1)} %get-tuple-element.141.q_ref.k_ref.v_ref, ...), custom_call_target="tpu_custom_call" | custom-call | flops 999999995904 | bytes 1000000000 | tf_op jit(solution)/shard_map/pallas_call | solution.py:468
  247.3 6.0 %shard_map.410 = (bf16[768,1152]{1,0:T(8,128)(2,1)S(1)}, bf16[768,1152]{1,0:T(8,128)(2,1)}) custom-call(s32[13]{0:T(128)S(1)} %concatenate.84.at_ref.at, bf16[768,1024]{1,0:T(8,128)(2,1)S(1)} %copy-done.5, bf16[2,1024,1152]{2,1,0:T(8,128)(2,1)S(1)} %get-tuple-element.201.right_ref.dtriples), custom_call_target="tpu_custom_call" | custom-call | flops 999999995904 | bytes 1000000000 | tf_op jit(solution)/shard_map/pallas_call | solution.py:510
  253.4 4.4 %shard_map.411 = (bf16[4,48,1024]{2,1,0:T(8,128)(2,1)S(1)}, f32[4,48,1024]{2,1,0:T(8,128)}, bf16[4,48,896]{2,1,0:T(8,128)(2,1)S(1)}, f32[4,48,896]{2,1,0:T(8,128)}) custom-call(s32[13]{0:T(128)S(1)} %concatenate.84.at_ref.at, f32[4,2,48,1024]{3,2,1,0:T(8,128)} %get-tuple-element.196.refs_0_, bf16[4,2,48,1024]{3,2,1,0:T(8,128)(2,1)} %collective-permute-done.32.refs_1_, ...), custom_call_target="tpu_custom_call" | custom-call | flops 1000 | bytes 1000 | tf_op jit(solution)/shard_map/pallas_call | solution.py:218
  257.9 9.7 %shard_map.412 = (f32[1024,768]{1,0:T(8,128)}, f32[768,384]{1,0:T(8,128)S(1)}, bf16[768,384]{1,0:T(8,128)(2,1)}) custom-call(s32[13]{0:T(128)S(1)} %concatenate.84.at_ref.at, f32[1024,768]{1,0:T(8,128)} %get-tuple-element.209.dresid1, bf16[2,1024,1152]{2,1,0:T(8,128)(2,1)S(1)} %get-tuple-element.201.right_ref.dtriples, bf16[2,768,1152]{2,1,0:T(8,128)(2,1)S(1)} %bitcast.84, ...), custom_call_target="tpu_custom_call" | custom-call | flops 999999995904 | bytes 1000000000 | tf_op jit(solution)/shard_map/pallas_call | solution.py:510
  271.6 1.2 add_bitcast_fusion.1
  273.6 4.2 %shard_map.413 = (bf16[4,2,48,768]{3,2,1,0:T(8,128)(2,1)}, f32[4,2,48,768]{3,2,1,0:T(8,128)}, bf16[4,2,48,768]{3,2,1,0:T(8,128)(2,1)}, f32[4,2,48,768]{3,2,1,0:T(8,128)}) custom-call(s32[13]{0:T(128)S(1)} %concatenate.84.at_ref.at, bf16[4,2,2,48,1152]{4,3,2,1,0:T(8,128)(2,1)S(1)} %bitcast.72, bf16[4,2,2,48,1152]{4,3,2,1,0:T(8,128)(2,1)} %bitcast.31.refs_1_.refs_3_.refs_5_, ...), custom_call_target="tpu_custom_call" | custom-call | flops 1000 | bytes 1000 | tf_op jit(solution)/shard_map/pallas_call | solution.py:218
  277.8 1.3 collective-permute-start.38
  279.1 1.2 collective-permute-start.39
  280.3 1.4 collective-permute-done.37.in1
  281.8 2.8 shard_map.414
  284.6 2.1 collective-permute-start.47
  286.7 2.2 collective-permute-start.45
  290.1 3.7 %collective-permute-done.38.refs_1_ = bf16[4,2,48,768]{3,2,1,0:T(8,128)(2,1)} collective-permute-done((bf16[4,2,48,768]{3,2,1,0:T(8,128)(2,1)}, bf16[4,2,48,768]{3,2,1,0:T(8,128)(2,1)}, u32[]{:S(2)}, u32[]{:S(2)}) %collective-permute-start.38) | collective-permute-done | bytes 589856 | tf_op jit(solution)/shard_map/ppermute | solution.py:59
  294.4 3.8 %shard_map.415 = (bf16[4,48,768]{2,1,0:T(8,128)(2,1)S(1)}, f32[4,48,768]{2,1,0:T(8,128)}, bf16[4,48,768]{2,1,0:T(8,128)(2,1)S(1)}, f32[4,48,768]{2,1,0:T(8,128)}) custom-call(s32[13]{0:T(128)S(1)} %concatenate.84.at_ref.at, f32[4,2,48,768]{3,2,1,0:T(8,128)} %get-tuple-element.219.refs_0_, bf16[4,2,48,768]{3,2,1,0:T(8,128)(2,1)} %collective-permute-done.38.refs_1_, ...), custom_call_target="tpu_custom_call" | custom-call | flops 1000 | bytes 1000 | tf_op jit(solution)/shard_map/pallas_call | solution.py:218
  300.2 1.5 collective-permute-done.46
  302.5 3.4 %collective-permute-done.40.in0 = bf16[4,48,768]{2,1,0:T(8,128)(2,1)S(1)} collective-permute-done((bf16[4,48,768]{2,1,0:T(8,128)(2,1)S(1)}, bf16[4,48,768]{2,1,0:T(8,128)(2,1)S(1)}, u32[]{:S(2)}, u32[]{:S(2)}) %collective-permute-start.40) | collective-permute-done | bytes 294944 | tf_op jit(solution)/shard_map/ppermute | solution.py:59
  306.7 2.7 shard_map.416
  310.5 2.7 collective-permute-start.43
  313.2 1.6 collective-permute-start.44
  315.1 7.7 %collective-permute-done.43 = bf16[1,48,1536]{2,1,0:T(8,128)(2,1)S(1)} collective-permute-done((bf16[1,48,1536]{2,1,0:T(8,128)(2,1)S(1)}, bf16[1,48,1536]{2,1,0:T(8,128)(2,1)S(1)}, u32[]{:S(2)}, u32[]{:S(2)}) %collective-permute-start.43) | collective-permute-done | bytes 147488 | tf_op jit(solution)/shard_map/ppermute | solution.py:59
  (234 shorter events, 44.7 us)
Async XLA Ops:
  7.2 21.3 %copy-start.14 = (f32[48,1536]{1,0:T(8,128)S(1)}, f32[48,1536]{1,0:T(8,128)}, u32[]{:S(2)}) copy-start(f32[48,1536]{1,0:T(8,128)} %param.25) | copy-start | bytes 884740
  7.2 105.1 %all-gather.2.cloned.1.call-start = ((), (), s32[]{:S(2)}) async-start(), calls=%async_computation | async-start | bytes 4866048 | tf_op jit(solution)/shard_map/all_gather | solution.py:1003
  10.8 9.9 %collective-permute-start.2 = (bf16[1,48,1536]{2,1,0:T(8,128)(2,1)S(1)}, bf16[1,48,1536]{2,1,0:T(8,128)(2,1)S(1)}, u32[]{:S(2)}, u32[]{:S(2)}) collective-permute-start(bf16[1,48,1536]{2,1,0:T(8,128)(2,1)S(1)} %constant_dynamic-update-slice_fusion), channel_id=1, source_target_pairs={{0,12},{1,13},{2,14},{3,15},{4,8},{5,9},{6,10},{7,11},{8,4},{9,5},... | collective-permute-start | bytes 442376 | tf_op jit(solution)/shard_map/ppermute | solution.py:59
  15.9 12.5 %collective-permute-start.1 = (bf16[1,48,1536]{2,1,0:T(8,128)(2,1)S(1)}, bf16[1,48,1536]{2,1,0:T(8,128)(2,1)S(1)}, u32[]{:S(2)}, u32[]{:S(2)}) collective-permute-start(bf16[1,48,1536]{2,1,0:T(8,128)(2,1)S(1)} %constant_dynamic-update-slice_fusion), channel_id=1, source_target_pairs={{0,8},{1,9},{2,10},{3,11},{4,12},{5,13},{6,14},{7,15},{8,0},{9,1},... | collective-permute-start | bytes 442376 | tf_op jit(solution)/shard_map/ppermute | solution.py:59
  15.9 12.5 %collective-permute-start = (bf16[1,48,1536]{2,1,0:T(8,128)(2,1)S(1)}, bf16[1,48,1536]{2,1,0:T(8,128)(2,1)S(1)}, u32[]{:S(2)}, u32[]{:S(2)}) collective-permute-start(bf16[1,48,1536]{2,1,0:T(8,128)(2,1)S(1)} %constant_dynamic-update-slice_fusion), channel_id=1, source_target_pairs={{0,4},{1,5},{2,6},{3,7},{4,0},{5,1},{6,2},{7,3},{8,12},{9,13},{10,... | collective-permute-start | bytes 442376 | tf_op jit(solution)/shard_map/ppermute | solution.py:59
  28.6 8.1 %collective-permute-start.3 = (bf16[4,48,768]{2,1,0:T(8,128)(2,1)S(1)}, bf16[4,48,768]{2,1,0:T(8,128)(2,1)S(1)}, u32[]{:S(2)}, u32[]{:S(2)}) collective-permute-start(bf16[4,48,768]{2,1,0:T(8,128)(2,1)S(1)} %get-tuple-element.397), channel_id=1, source_target_pairs={{0,2},{1,3},{2,0},{3,1},{4,6},{5,7},{6,4},{7,5},{8,10},{9,11},{10,... | collective-permute-start | bytes 884744 | tf_op jit(solution)/shard_map/ppermute | solution.py:59
  30.2 7.8 %collective-permute-start.4 = (bf16[4,48,768]{2,1,0:T(8,128)(2,1)S(1)}, bf16[4,48,768]{2,1,0:T(8,128)(2,1)S(1)}, u32[]{:S(2)}, u32[]{:S(2)}) collective-permute-start(bf16[4,48,768]{2,1,0:T(8,128)(2,1)S(1)} %get-tuple-element.396), channel_id=1, source_target_pairs={{0,1},{1,0},{2,3},{3,2},{4,5},{5,4},{6,7},{7,6},{8,9},{9,8},{10,11... | collective-permute-start | bytes 884744 | tf_op jit(solution)/shard_map/ppermute | solution.py:59
  38.0 10.1 %collective-permute-start.7 = (bf16[1,48,2048]{2,1,0:T(8,128)(2,1)S(1)}, bf16[1,48,2048]{2,1,0:T(8,128)(2,1)S(1)}, u32[]{:S(2)}, u32[]{:S(2)}) collective-permute-start(bf16[1,48,2048]{2,1,0:T(8,128)(2,1)S(1)} %bitcast.103), channel_id=1, source_target_pairs={{0,12},{1,13},{2,14},{3,15},{4,8},{5,9},{6,10},{7,11},{8,4},{9,5},... | collective-permute-start | bytes 589832 | tf_op jit(solution)/shard_map/ppermute | solution.py:59
  40.4 17.9 %collective-permute-start.6 = (bf16[1,48,2048]{2,1,0:T(8,128)(2,1)S(1)}, bf16[1,48,2048]{2,1,0:T(8,128)(2,1)S(1)}, u32[]{:S(2)}, u32[]{:S(2)}) collective-permute-start(bf16[1,48,2048]{2,1,0:T(8,128)(2,1)S(1)} %bitcast.104), channel_id=1, source_target_pairs={{0,8},{1,9},{2,10},{3,11},{4,12},{5,13},{6,14},{7,15},{8,0},{9,1},... | collective-permute-start | bytes 589832 | tf_op jit(solution)/shard_map/ppermute | solution.py:59
  40.4 17.9 %collective-permute-start.5 = (bf16[1,48,2048]{2,1,0:T(8,128)(2,1)S(1)}, bf16[1,48,2048]{2,1,0:T(8,128)(2,1)S(1)}, u32[]{:S(2)}, u32[]{:S(2)}) collective-permute-start(bf16[1,48,2048]{2,1,0:T(8,128)(2,1)S(1)} %bitcast.105), channel_id=1, source_target_pairs={{0,4},{1,5},{2,6},{3,7},{4,0},{5,1},{6,2},{7,3},{8,12},{9,13},{10,... | collective-permute-start | bytes 589832 | tf_op jit(solution)/shard_map/ppermute | solution.py:59
  42.5 16.1 %collective-permute-start.8 = (bf16[8,48,768]{2,1,0:T(8,128)(2,1)S(1)}, bf16[8,48,768]{2,1,0:T(8,128)(2,1)S(1)}, u32[]{:S(2)}, u32[]{:S(2)}) collective-permute-start(bf16[8,48,768]{2,1,0:T(8,128)(2,1)S(1)} %pad_maximum_fusion.2), channel_id=1, source_target_pairs={{0,1},{1,0},{2,3},{3,2},{4,5},{5,4},{6,7},{7,6},{8,9},{9,8},{10,11... | collective-permute-start | bytes 1769480 | tf_op jit(solution)/shard_map/ppermute | solution.py:59
  44.0 14.7 %collective-permute-start.9 = (bf16[8,48,768]{2,1,0:T(8,128)(2,1)S(1)}, bf16[8,48,768]{2,1,0:T(8,128)(2,1)S(1)}, u32[]{:S(2)}, u32[]{:S(2)}) collective-permute-start(bf16[8,48,768]{2,1,0:T(8,128)(2,1)S(1)} %pad_maximum_fusion.3), channel_id=1, source_target_pairs={{0,2},{1,3},{2,0},{3,1},{4,6},{5,7},{6,4},{7,5},{8,10},{9,11},{10,... | collective-permute-start | bytes 1769480 | tf_op jit(solution)/shard_map/ppermute | solution.py:59
  58.6 5.1 %collective-permute-start.10 = (bf16[16,48,768]{2,1,0:T(8,128)(2,1)S(1)}, bf16[16,48,768]{2,1,0:T(8,128)(2,1)S(1)}, u32[]{:S(2)}, u32[]{:S(2)}) collective-permute-start(bf16[16,48,768]{2,1,0:T(8,128)(2,1)S(1)} %constant_dynamic-update-slice_fusion.5.refs_0_), channel_id=1, source_target_pairs={{0,16},{16,0},{1,17},{17,1},{2,18},{18,2},{3,19},{19,3},{4,20},{20... | collective-permute-start | bytes 3538952 | tf_op jit(solution)/shard_map/ppermute | solution.py:59
  58.8 5.0 %collective-permute-start.11 = (bf16[16,48,768]{2,1,0:T(8,128)(2,1)S(1)}, bf16[16,48,768]{2,1,0:T(8,128)(2,1)}, u32[]{:S(2)}, u32[]{:S(2)}) collective-permute-start(bf16[16,48,768]{2,1,0:T(8,128)(2,1)S(1)} %constant_dynamic-update-slice_fusion.7.refs_1_), channel_id=1, source_target_pairs={{0,16},{16,0},{1,17},{17,1},{2,18},{18,2},{3,19},{19,3},{4,20},{20... | collective-permute-start | bytes 3538952 | tf_op jit(solution)/shard_map/ppermute | solution.py:59
  60.2 14.6 %collective-permute-start.12 = (bf16[4,48,1024]{2,1,0:T(8,128)(2,1)}, bf16[4,48,1024]{2,1,0:T(8,128)(2,1)}, u32[]{:S(2)}, u32[]{:S(2)}) collective-permute-start(bf16[4,48,1024]{2,1,0:T(8,128)(2,1)} %get-tuple-element.142), channel_id=1, source_target_pairs={{0,2},{1,3},{2,0},{3,1},{4,6},{5,7},{6,4},{7,5},{8,10},{9,11},{10,... | collective-permute-start | bytes 1179656 | tf_op jit(solution)/shard_map/ppermute | solution.py:59
  60.9 17.2 %collective-permute-start.13 = (bf16[4,48,1024]{2,1,0:T(8,128)(2,1)}, bf16[4,48,1024]{2,1,0:T(8,128)(2,1)}, u32[]{:S(2)}, u32[]{:S(2)}) collective-permute-start(bf16[4,48,1024]{2,1,0:T(8,128)(2,1)} %get-tuple-element.143), channel_id=1, source_target_pairs={{0,1},{1,0},{2,3},{3,2},{4,5},{5,4},{6,7},{7,6},{8,9},{9,8},{10,11... | collective-permute-start | bytes 1179656 | tf_op jit(solution)/shard_map/ppermute | solution.py:59
  75.8 27.7 %collective-permute-start.14 = (bf16[8,48,1024]{2,1,0:T(8,128)(2,1)S(1)}, bf16[8,48,1024]{2,1,0:T(8,128)(2,1)S(1)}, u32[]{:S(2)}, u32[]{:S(2)}) collective-permute-start(bf16[8,48,1024]{2,1,0:T(8,128)(2,1)S(1)} %constant_dynamic-update-slice_fusion.9), channel_id=1, source_target_pairs={{0,1},{1,0},{2,3},{3,2},{4,5},{5,4},{6,7},{7,6},{8,9},{9,8},{10,11... | collective-permute-start | bytes 2359304 | tf_op jit(solution)/shard_map/ppermute | solution.py:59
  79.1 27.8 %collective-permute-start.15 = (bf16[8,48,1024]{2,1,0:T(8,128)(2,1)S(1)}, bf16[8,48,1024]{2,1,0:T(8,128)(2,1)S(1)}, u32[]{:S(2)}, u32[]{:S(2)}) collective-permute-start(bf16[8,48,1024]{2,1,0:T(8,128)(2,1)S(1)} %constant_dynamic-update-slice_fusion.11), channel_id=1, source_target_pairs={{0,2},{1,3},{2,0},{3,1},{4,6},{5,7},{6,4},{7,5},{8,10},{9,11},{10,... | collective-permute-start | bytes 2359304 | tf_op jit(solution)/shard_map/ppermute | solution.py:59
  103.6 6.3 %collective-permute-start.16 = (bf16[16,48,1024]{2,1,0:T(8,128)(2,1)S(1)}, bf16[16,48,1024]{2,1,0:T(8,128)(2,1)}, u32[]{:S(2)}, u32[]{:S(2)}) collective-permute-start(bf16[16,48,1024]{2,1,0:T(8,128)(2,1)S(1)} %constant_dynamic-update-slice_fusion.13.refs_0_), channel_id=1, source_target_pairs={{0,16},{16,0},{1,17},{17,1},{2,18},{18,2},{3,19},{19,3},{4,20},{20... | collective-permute-start | bytes 4718600 | tf_op jit(solution)/shard_map/ppermute | solution.py:59
  106.9 4.3 %collective-permute-start.17 = (bf16[16,48,1024]{2,1,0:T(8,128)(2,1)S(1)}, bf16[16,48,1024]{2,1,0:T(8,128)(2,1)}, u32[]{:S(2)}, u32[]{:S(2)}) collective-permute-start(bf16[16,48,1024]{2,1,0:T(8,128)(2,1)S(1)} %constant_dynamic-update-slice_fusion.15.refs_1_), channel_id=1, source_target_pairs={{0,16},{16,0},{1,17},{17,1},{2,18},{18,2},{3,19},{19,3},{4,20},{20... | collective-permute-start | bytes 4718600 | tf_op jit(solution)/shard_map/ppermute | solution.py:59
  116.8 22.8 %copy-start.3 = (bf16[16,48,768]{2,1,0:T(8,128)(2,1)}, bf16[16,48,768]{2,1,0:T(8,128)(2,1)S(1)}, u32[]{:S(2)}) copy-start(bf16[16,48,768]{2,1,0:T(8,128)(2,1)S(1)} %get-tuple-element.150) | copy-start | bytes 3538948
  139.6 3.8 %collective-permute-start.18 = (bf16[1,8,896]{2,1,0:T(8,128)(2,1)S(1)}, bf16[1,8,896]{2,1,0:T(8,128)(2,1)S(1)}, u32[]{:S(2)}, u32[]{:S(2)}) collective-permute-start(bf16[1,8,896]{2,1,0:T(8,128)(2,1)S(1)} %bitcast.94), channel_id=1, source_target_pairs={{0,1},{1,0},{2,3},{3,2},{4,5},{5,4},{6,7},{7,6},{8,9},{9,8},{10,11... | collective-permute-start | bytes 43016 | tf_op jit(solution)/shard_map/ppermute | solution.py:59
  140.5 3.7 %collective-permute-start.19 = (bf16[1,8,896]{2,1,0:T(8,128)(2,1)S(1)}, bf16[1,8,896]{2,1,0:T(8,128)(2,1)S(1)}, u32[]{:S(2)}, u32[]{:S(2)}) collective-permute-start(bf16[1,8,896]{2,1,0:T(8,128)(2,1)S(1)} %bitcast.95), channel_id=1, source_target_pairs={{0,2},{1,3},{2,0},{3,1},{4,6},{5,7},{6,4},{7,5},{8,10},{9,11},{10,... | collective-permute-start | bytes 43016 | tf_op jit(solution)/shard_map/ppermute | solution.py:59
  141.2 4.6 %collective-permute-start.20 = (bf16[1,8,896]{2,1,0:T(8,128)(2,1)S(1)}, bf16[1,8,896]{2,1,0:T(8,128)(2,1)S(1)}, u32[]{:S(2)}, u32[]{:S(2)}) collective-permute-start(bf16[1,8,896]{2,1,0:T(8,128)(2,1)S(1)} %bitcast.96), channel_id=1, source_target_pairs={{0,3},{1,2},{2,1},{3,0},{4,7},{5,6},{6,5},{7,4},{8,11},{9,10},{10,... | collective-permute-start | bytes 43016 | tf_op jit(solution)/shard_map/ppermute | solution.py:59
  145.8 5.0 %collective-permute-start.21 = (bf16[4,8,896]{2,1,0:T(8,128)(2,1)S(1)}, bf16[4,8,896]{2,1,0:T(8,128)(2,1)S(1)}, u32[]{:S(2)}, u32[]{:S(2)}) collective-permute-start(bf16[4,8,896]{2,1,0:T(8,128)(2,1)S(1)} %pad_maximum_fusion.6), channel_id=1, source_target_pairs={{0,4},{1,5},{2,6},{3,7},{4,0},{5,1},{6,2},{7,3},{8,12},{9,13},{10,... | collective-permute-start | bytes 172040 | tf_op jit(solution)/shard_map/ppermute | solution.py:59
  148.3 5.4 %collective-permute-start.22 = (bf16[4,8,896]{2,1,0:T(8,128)(2,1)S(1)}, bf16[4,8,896]{2,1,0:T(8,128)(2,1)S(1)}, u32[]{:S(2)}, u32[]{:S(2)}) collective-permute-start(bf16[4,8,896]{2,1,0:T(8,128)(2,1)S(1)} %pad_maximum_fusion.6), channel_id=1, source_target_pairs={{0,8},{1,9},{2,10},{3,11},{4,12},{5,13},{6,14},{7,15},{8,0},{9,1},... | collective-permute-start | bytes 172040 | tf_op jit(solution)/shard_map/ppermute | solution.py:59
  148.7 6.1 %collective-permute-start.23 = (bf16[4,8,896]{2,1,0:T(8,128)(2,1)S(1)}, bf16[4,8,896]{2,1,0:T(8,128)(2,1)S(1)}, u32[]{:S(2)}, u32[]{:S(2)}) collective-permute-start(bf16[4,8,896]{2,1,0:T(8,128)(2,1)S(1)} %pad_maximum_fusion.6), channel_id=1, source_target_pairs={{0,12},{1,13},{2,14},{3,15},{4,8},{5,9},{6,10},{7,11},{8,4},{9,5},... | collective-permute-start | bytes 172040 | tf_op jit(solution)/shard_map/ppermute | solution.py:59
  154.8 1.6 collective-permute-start.24
  169.3 4.6 %collective-permute-start.25 = (bf16[3072,384]{1,0:T(8,128)(2,1)S(1)}, bf16[3072,384]{1,0:T(8,128)(2,1)S(1)}, u32[]{:S(2)}, u32[]{:S(2)}) collective-permute-start(bf16[3072,384]{1,0:T(8,128)(2,1)S(1)} %get-tuple-element.164), channel_id=1, source_target_pairs={{0,16},{16,0},{1,17},{17,1},{2,18},{18,2},{3,19},{19,3},{4,20},{20... | collective-permute-start | bytes 7077896 | tf_op jit(solution)/shard_map/ppermute | solution.py:59
  176.8 17.2 %collective-permute-start.26 = (bf16[4,2,96,384]{3,2,1,0:T(8,128)(2,1)}, bf16[4,2,96,384]{3,2,1,0:T(8,128)(2,1)}, u32[]{:S(2)}, u32[]{:S(2)}) collective-permute-start(bf16[4,2,96,384]{3,2,1,0:T(8,128)(2,1)} %get-tuple-element.165), channel_id=1, source_target_pairs={{0,1},{1,0},{2,3},{3,2},{4,5},{5,4},{6,7},{7,6},{8,9},{9,8},{10,11... | collective-permute-start | bytes 1769480 | tf_op jit(solution)/shard_map/ppermute | solution.py:59
  177.7 16.2 %collective-permute-start.27 = (bf16[4,2,96,384]{3,2,1,0:T(8,128)(2,1)}, bf16[4,2,96,384]{3,2,1,0:T(8,128)(2,1)}, u32[]{:S(2)}, u32[]{:S(2)}) collective-permute-start(bf16[4,2,96,384]{3,2,1,0:T(8,128)(2,1)} %get-tuple-element.167), channel_id=1, source_target_pairs={{0,2},{1,3},{2,0},{3,1},{4,6},{5,7},{6,4},{7,5},{8,10},{9,11},{10,... | collective-permute-start | bytes 1769480 | tf_op jit(solution)/shard_map/ppermute | solution.py:59
  197.9 8.8 %collective-permute-start.28 = (bf16[4,96,384]{2,1,0:T(8,128)(2,1)}, bf16[4,96,384]{2,1,0:T(8,128)(2,1)}, u32[]{:S(2)}, u32[]{:S(2)}) collective-permute-start(bf16[4,96,384]{2,1,0:T(8,128)(2,1)} %get-tuple-element.176), channel_id=1, source_target_pairs={{0,2},{1,3},{2,0},{3,1},{4,6},{5,7},{6,4},{7,5},{8,10},{9,11},{10,... | collective-permute-start | bytes 884744 | tf_op jit(solution)/shard_map/ppermute | solution.py:59
  198.7 8.1 %collective-permute-start.29 = (bf16[4,96,384]{2,1,0:T(8,128)(2,1)}, bf16[4,96,384]{2,1,0:T(8,128)(2,1)}, u32[]{:S(2)}, u32[]{:S(2)}) collective-permute-start(bf16[4,96,384]{2,1,0:T(8,128)(2,1)} %get-tuple-element.178), channel_id=1, source_target_pairs={{0,1},{1,0},{2,3},{3,2},{4,5},{5,4},{6,7},{7,6},{8,9},{9,8},{10,11... | collective-permute-start | bytes 884744 | tf_op jit(solution)/shard_map/ppermute | solution.py:59
  206.3 10.9 %collective-permute-start.30 = (bf16[768,1536]{1,0:T(8,128)(2,1)}, bf16[768,1536]{1,0:T(8,128)(2,1)}, u32[]{:S(2)}, u32[]{:S(2)}) collective-permute-start(bf16[768,1536]{1,0:T(8,128)(2,1)} %get-tuple-element.183), channel_id=1, source_target_pairs={{0,16},{16,0},{1,17},{17,1},{2,18},{18,2},{3,19},{19,3},{4,20},{20... | collective-permute-start | bytes 7077896 | tf_op jit(solution)/shard_map/ppermute | solution.py:59
  209.9 7.3 %collective-permute-start.31 = (bf16[768,384]{1,0:T(8,128)(2,1)}, bf16[768,384]{1,0:T(8,128)(2,1)}, u32[]{:S(2)}, u32[]{:S(2)}) collective-permute-start(bf16[768,384]{1,0:T(8,128)(2,1)} %get-tuple-element.194), channel_id=1, source_target_pairs={{0,16},{16,0},{1,17},{17,1},{2,18},{18,2},{3,19},{19,3},{4,20},{20... | collective-permute-start | bytes 1769480 | tf_op jit(solution)/shard_map/ppermute | solution.py:59
  212.8 57.2 %collective-permute-start.50 = (bf16[1,96,768]{2,1,0:T(8,128)(2,1)}, bf16[1,96,768]{2,1,0:T(8,128)(2,1)}, u32[]{:S(2)}, u32[]{:S(2)}) collective-permute-start(bf16[1,96,768]{2,1,0:T(8,128)(2,1)} %get-tuple-element.191), channel_id=1, source_target_pairs={{0,12},{1,13},{2,14},{3,15},{4,8},{5,9},{6,10},{7,11},{8,4},{9,5},... | collective-permute-start | bytes 442376 | tf_op jit(solution)/shard_map/ppermute | solution.py:59
  215.0 55.0 %collective-permute-start.49 = (bf16[1,96,768]{2,1,0:T(8,128)(2,1)}, bf16[1,96,768]{2,1,0:T(8,128)(2,1)}, u32[]{:S(2)}, u32[]{:S(2)}) collective-permute-start(bf16[1,96,768]{2,1,0:T(8,128)(2,1)} %get-tuple-element.190), channel_id=1, source_target_pairs={{0,8},{1,9},{2,10},{3,11},{4,12},{5,13},{6,14},{7,15},{8,0},{9,1},... | collective-permute-start | bytes 442376 | tf_op jit(solution)/shard_map/ppermute | solution.py:59
  215.1 54.9 %collective-permute-start.48 = (bf16[1,96,768]{2,1,0:T(8,128)(2,1)}, bf16[1,96,768]{2,1,0:T(8,128)(2,1)}, u32[]{:S(2)}, u32[]{:S(2)}) collective-permute-start(bf16[1,96,768]{2,1,0:T(8,128)(2,1)} %get-tuple-element.189), channel_id=1, source_target_pairs={{0,4},{1,5},{2,6},{3,7},{4,0},{5,1},{6,2},{7,3},{8,12},{9,13},{10,... | collective-permute-start | bytes 442376 | tf_op jit(solution)/shard_map/ppermute | solution.py:59
  217.2 9.2 %slice-start = ((s8[12582912]{0:T(1024)(128)(4,1)}), s8[4194304]{0:T(1024)(128)(4,1)S(1)}, s32[]{:S(2)}) async-start(s8[12582912]{0:T(1024)(128)(4,1)} %bitcast.98), calls=%async_computation.1 | async-start | bytes 8388608
  217.2 9.2 %slice-start.1 = ((s8[12582912]{0:T(1024)(128)(4,1)}), s8[4194304]{0:T(1024)(128)(4,1)S(1)}, s32[]{:S(2)}) async-start(s8[12582912]{0:T(1024)(128)(4,1)} %bitcast.98), calls=%async_computation.2 | async-start | bytes 8388608
  222.4 31.0 %collective-permute-start.32 = (bf16[4,2,48,1024]{3,2,1,0:T(8,128)(2,1)}, bf16[4,2,48,1024]{3,2,1,0:T(8,128)(2,1)}, u32[]{:S(2)}, u32[]{:S(2)}) collective-permute-start(bf16[4,2,48,1024]{3,2,1,0:T(8,128)(2,1)} %get-tuple-element.195), channel_id=1, source_target_pairs={{0,1},{1,0},{2,3},{3,2},{4,5},{5,4},{6,7},{7,6},{8,9},{9,8},{10,11... | collective-permute-start | bytes 2359304 | tf_op jit(solution)/shard_map/ppermute | solution.py:59
  223.7 29.7 %collective-permute-start.33 = (bf16[4,2,48,896]{3,2,1,0:T(8,128)(2,1)}, bf16[4,2,48,896]{3,2,1,0:T(8,128)(2,1)}, u32[]{:S(2)}, u32[]{:S(2)}) collective-permute-start(bf16[4,2,48,896]{3,2,1,0:T(8,128)(2,1)} %get-tuple-element.197), channel_id=1, source_target_pairs={{0,2},{1,3},{2,0},{3,1},{4,6},{5,7},{6,4},{7,5},{8,10},{9,11},{10,... | collective-permute-start | bytes 2064392 | tf_op jit(solution)/shard_map/ppermute | solution.py:59
  227.6 19.7 %copy-start.5 = (bf16[768,1024]{1,0:T(8,128)(2,1)S(1)}, bf16[768,1024]{1,0:T(8,128)(2,1)}, u32[]{:S(2)}) copy-start(bf16[768,1024]{1,0:T(8,128)(2,1)} %get-tuple-element.156.left_ref) | copy-start | bytes 4718596
  253.4 20.2 %collective-permute-start.34 = (bf16[768,1152]{1,0:T(8,128)(2,1)}, bf16[768,1152]{1,0:T(8,128)(2,1)}, u32[]{:S(2)}, u32[]{:S(2)}) collective-permute-start(bf16[768,1152]{1,0:T(8,128)(2,1)} %get-tuple-element.202), channel_id=1, source_target_pairs={{0,16},{16,0},{1,17},{17,1},{2,18},{18,2},{3,19},{19,3},{4,20},{20... | collective-permute-start | bytes 5308424 | tf_op jit(solution)/shard_map/ppermute | solution.py:59
  257.8 9.8 %copy-start.10 = (bf16[4,48,1024]{2,1,0:T(8,128)(2,1)}, bf16[4,48,1024]{2,1,0:T(8,128)(2,1)S(1)}, u32[]{:S(2)}) copy-start(bf16[4,48,1024]{2,1,0:T(8,128)(2,1)S(1)} %get-tuple-element.204) | copy-start | bytes 1179652
  257.8 9.8 %copy-start.11 = (bf16[4,48,896]{2,1,0:T(8,128)(2,1)}, bf16[4,48,896]{2,1,0:T(8,128)(2,1)S(1)}, u32[]{:S(2)}) copy-start(bf16[4,48,896]{2,1,0:T(8,128)(2,1)S(1)} %get-tuple-element.206) | copy-start | bytes 1032196
  257.8 10.1 %copy-start.35 = (f32[4,48]{1,0:T(4,128)S(1)}, f32[4,48]{1,0:T(4,128)}, u32[]{:S(2)}) copy-start(f32[4,48]{1,0:T(4,128)} %param.32) | copy-start | bytes 2308
  257.9 10.1 %copy-start.33 = (f32[4,48]{1,0:T(4,128)S(1)}, f32[4,48]{1,0:T(4,128)}, u32[]{:S(2)}) copy-start(f32[4,48]{1,0:T(4,128)} %param.31) | copy-start | bytes 2308
  257.9 10.7 %copy-start.36 = (f32[4,48]{1,0:T(4,128)S(1)}, f32[4,48]{1,0:T(4,128)}, u32[]{:S(2)}) copy-start(f32[4,48]{1,0:T(4,128)} %param.33) | copy-start | bytes 2308
  267.6 6.0 %collective-permute-start.35 = (bf16[768,384]{1,0:T(8,128)(2,1)}, bf16[768,384]{1,0:T(8,128)(2,1)S(1)}, u32[]{:S(2)}, u32[]{:S(2)}) collective-permute-start(bf16[768,384]{1,0:T(8,128)(2,1)} %get-tuple-element.217), channel_id=1, source_target_pairs={{0,16},{16,0},{1,17},{17,1},{2,18},{18,2},{3,19},{19,3},{4,20},{20... | collective-permute-start | bytes 1769480 | tf_op jit(solution)/shard_map/ppermute | solution.py:59
  270.0 11.8 %collective-permute-start.36 = (bf16[4,48,1024]{2,1,0:T(8,128)(2,1)}, bf16[4,48,1024]{2,1,0:T(8,128)(2,1)S(1)}, u32[]{:S(2)}, u32[]{:S(2)}) collective-permute-start(bf16[4,48,1024]{2,1,0:T(8,128)(2,1)} %copy-done.10), channel_id=1, source_target_pairs={{0,2},{1,3},{2,0},{3,1},{4,6},{5,7},{6,4},{7,5},{8,10},{9,11},{10,... | collective-permute-start | bytes 1179656 | tf_op jit(solution)/shard_map/ppermute | solution.py:59
  270.9 10.8 %collective-permute-start.37 = (bf16[4,48,896]{2,1,0:T(8,128)(2,1)}, bf16[4,48,896]{2,1,0:T(8,128)(2,1)S(1)}, u32[]{:S(2)}, u32[]{:S(2)}) collective-permute-start(bf16[4,48,896]{2,1,0:T(8,128)(2,1)} %copy-done.11), channel_id=1, source_target_pairs={{0,1},{1,0},{2,3},{3,2},{4,5},{5,4},{6,7},{7,6},{8,9},{9,8},{10,11... | collective-permute-start | bytes 1032200 | tf_op jit(solution)/shard_map/ppermute | solution.py:59
  277.8 16.0 %collective-permute-start.38 = (bf16[4,2,48,768]{3,2,1,0:T(8,128)(2,1)}, bf16[4,2,48,768]{3,2,1,0:T(8,128)(2,1)}, u32[]{:S(2)}, u32[]{:S(2)}) collective-permute-start(bf16[4,2,48,768]{3,2,1,0:T(8,128)(2,1)} %get-tuple-element.218), channel_id=1, source_target_pairs={{0,1},{1,0},{2,3},{3,2},{4,5},{5,4},{6,7},{7,6},{8,9},{9,8},{10,11... | collective-permute-start | bytes 1769480 | tf_op jit(solution)/shard_map/ppermute | solution.py:59
  279.1 15.3 %collective-permute-start.39 = (bf16[4,2,48,768]{3,2,1,0:T(8,128)(2,1)}, bf16[4,2,48,768]{3,2,1,0:T(8,128)(2,1)}, u32[]{:S(2)}, u32[]{:S(2)}) collective-permute-start(bf16[4,2,48,768]{3,2,1,0:T(8,128)(2,1)} %get-tuple-element.220), channel_id=1, source_target_pairs={{0,2},{1,3},{2,0},{3,1},{4,6},{5,7},{6,4},{7,5},{8,10},{9,11},{10,... | collective-permute-start | bytes 1769480 | tf_op jit(solution)/shard_map/ppermute | solution.py:59
  284.6 15.6 %collective-permute-start.47 = (bf16[1,48,1920]{2,1,0:T(8,128)(2,1)S(1)}, bf16[1,48,1920]{2,1,0:T(8,128)(2,1)S(1)}, u32[]{:S(2)}, u32[]{:S(2)}) collective-permute-start(bf16[1,48,1920]{2,1,0:T(8,128)(2,1)S(1)} %get-tuple-element.226), channel_id=1, source_target_pairs={{0,12},{1,13},{2,14},{3,15},{4,8},{5,9},{6,10},{7,11},{8,4},{9,5},... | collective-permute-start | bytes 552968 | tf_op jit(solution)/shard_map/ppermute | solution.py:59
  286.7 15.0 %collective-permute-start.46 = (bf16[1,48,1920]{2,1,0:T(8,128)(2,1)S(1)}, bf16[1,48,1920]{2,1,0:T(8,128)(2,1)S(1)}, u32[]{:S(2)}, u32[]{:S(2)}) collective-permute-start(bf16[1,48,1920]{2,1,0:T(8,128)(2,1)S(1)} %get-tuple-element.225), channel_id=1, source_target_pairs={{0,8},{1,9},{2,10},{3,11},{4,12},{5,13},{6,14},{7,15},{8,0},{9,1},... | collective-permute-start | bytes 552968 | tf_op jit(solution)/shard_map/ppermute | solution.py:59
  286.7 15.0 %collective-permute-start.45 = (bf16[1,48,1920]{2,1,0:T(8,128)(2,1)S(1)}, bf16[1,48,1920]{2,1,0:T(8,128)(2,1)S(1)}, u32[]{:S(2)}, u32[]{:S(2)}) collective-permute-start(bf16[1,48,1920]{2,1,0:T(8,128)(2,1)S(1)} %get-tuple-element.224), channel_id=1, source_target_pairs={{0,4},{1,5},{2,6},{3,7},{4,0},{5,1},{6,2},{7,3},{8,12},{9,13},{10,... | collective-permute-start | bytes 552968 | tf_op jit(solution)/shard_map/ppermute | solution.py:59
  290.1 11.7 %copy-start.19 = (f32[1,48,1920]{2,1,0:T(8,128)S(1)}, f32[1,48,1920]{2,1,0:T(8,128)}, u32[]{:S(2)}) copy-start(f32[1,48,1920]{2,1,0:T(8,128)} %get-tuple-element.223) | copy-start | bytes 1105924
  298.1 7.8 %collective-permute-start.40 = (bf16[4,48,768]{2,1,0:T(8,128)(2,1)S(1)}, bf16[4,48,768]{2,1,0:T(8,128)(2,1)S(1)}, u32[]{:S(2)}, u32[]{:S(2)}) collective-permute-start(bf16[4,48,768]{2,1,0:T(8,128)(2,1)S(1)} %get-tuple-element.230), channel_id=1, source_target_pairs={{0,2},{1,3},{2,0},{3,1},{4,6},{5,7},{6,4},{7,5},{8,10},{9,11},{10,... | collective-permute-start | bytes 884744 | tf_op jit(solution)/shard_map/ppermute | solution.py:59
  299.1 7.6 %collective-permute-start.41 = (bf16[4,48,768]{2,1,0:T(8,128)(2,1)S(1)}, bf16[4,48,768]{2,1,0:T(8,128)(2,1)S(1)}, u32[]{:S(2)}, u32[]{:S(2)}) collective-permute-start(bf16[4,48,768]{2,1,0:T(8,128)(2,1)S(1)} %get-tuple-element.231), channel_id=1, source_target_pairs={{0,1},{1,0},{2,3},{3,2},{4,5},{5,4},{6,7},{7,6},{8,9},{9,8},{10,11... | collective-permute-start | bytes 884744 | tf_op jit(solution)/shard_map/ppermute | solution.py:59
  309.3 5.5 %collective-permute-start.42 = (bf16[1,48,1536]{2,1,0:T(8,128)(2,1)S(1)}, bf16[1,48,1536]{2,1,0:T(8,128)(2,1)S(1)}, u32[]{:S(2)}, u32[]{:S(2)}) collective-permute-start(bf16[1,48,1536]{2,1,0:T(8,128)(2,1)S(1)} %get-tuple-element.233), channel_id=1, source_target_pairs={{0,4},{1,5},{2,6},{3,7},{4,0},{5,1},{6,2},{7,3},{8,12},{9,13},{10,... | collective-permute-start | bytes 442376 | tf_op jit(solution)/shard_map/ppermute | solution.py:59
  310.5 12.3 %collective-permute-start.43 = (bf16[1,48,1536]{2,1,0:T(8,128)(2,1)S(1)}, bf16[1,48,1536]{2,1,0:T(8,128)(2,1)S(1)}, u32[]{:S(2)}, u32[]{:S(2)}) collective-permute-start(bf16[1,48,1536]{2,1,0:T(8,128)(2,1)S(1)} %get-tuple-element.234), channel_id=1, source_target_pairs={{0,8},{1,9},{2,10},{3,11},{4,12},{5,13},{6,14},{7,15},{8,0},{9,1},... | collective-permute-start | bytes 442376 | tf_op jit(solution)/shard_map/ppermute | solution.py:59
  313.2 9.8 %collective-permute-start.44 = (bf16[1,48,1536]{2,1,0:T(8,128)(2,1)S(1)}, bf16[1,48,1536]{2,1,0:T(8,128)(2,1)S(1)}, u32[]{:S(2)}, u32[]{:S(2)}) collective-permute-start(bf16[1,48,1536]{2,1,0:T(8,128)(2,1)S(1)} %get-tuple-element.235), channel_id=1, source_target_pairs={{0,12},{1,13},{2,14},{3,15},{4,8},{5,9},{6,10},{7,11},{8,4},{9,5},... | collective-permute-start | bytes 442376 | tf_op jit(solution)/shard_map/ppermute | solution.py:59
  314.9 8.5 %copy-start.26 = (f32[1,48,1536]{2,1,0:T(8,128)S(1)}, f32[1,48,1536]{2,1,0:T(8,128)}, u32[]{:S(2)}) copy-start(f32[1,48,1536]{2,1,0:T(8,128)} %get-tuple-element.232) | copy-start | bytes 884740
  (32 other events, 139.2 us)
Sparse Core Ops, SparseCore 0:
  28.6 83.6 all-gather.1

commit v2 on v1

--- a/solution.py
+++ b/solution.py
@@ -221,7 +221,7 @@
             num_scalar_prefetch=1, grid=(count,), in_specs=in_specs, out_specs=out_specs
         ),
         out_shape=outs,
-        compiler_params=pltpu.CompilerParams(vmem_limit_bytes=26 << 20),
+        compiler_params=pltpu.CompilerParams(vmem_limit_bytes=20 << 20),
         cost_estimate=LONG_COST if long else COST,
     )(at, *ins)
 
@@ -266,7 +266,7 @@
                 ins += piece[:2]
                 in_specs += [piece_spec(piece)] * 2
             shape = (self.count, 2, self.rows[side], self.columns[side])
-            outs += [stacked(*shape, dtype=jnp.bfloat16), far_off(*shape, dtype=jnp.float32)]
+            outs += [stacked(*shape, dtype=jnp.bfloat16), pltpu.VMEM(shape, jnp.float32)]
         return fold_call(self.first_kernel, 1, self.at, ins, in_specs, outs, [whole_block(o) for o in outs])
 
     def first_sent(self, parts):
@@ -286,9 +286,9 @@
     def second(self, arrived):
         ins, outs = [], []
         for side in range(2):
-            ins += [far_away(self.stays[side]), arrived[side]]
+            ins += [near_by(self.stays[side]), arrived[side]]
             shape = (self.count, self.rows[side], self.columns[side])
-            outs += [stacked(*shape, dtype=jnp.bfloat16), far_off(*shape, dtype=jnp.float32)]
+            outs += [stacked(*shape, dtype=jnp.bfloat16), pltpu.VMEM(shape, jnp.float32)]
         return fold_call(
             self.second_kernel, 1, self.at, ins, [whole_block(a) for a in ins], outs,
             [whole_block(out) for out in outs],
@@ -311,19 +311,21 @@
 
     def third(self, arrived, kept):
         radix = min(4, self.count)
-        ins = [far_away(part) for part in kept] + arrived
+        ins = [near_by(part) for part in kept] + arrived
         in_specs = [pl.BlockSpec((radix,) + a.shape[1:], lambda z, at: (z, 0, 0)) for a in ins]
         shape = (self.count // radix, self.rows[0], sum(self.columns))
-        outs = [far_off(*shape, dtype=jnp.float32)] + [stacked(*shape, dtype=jnp.bfloat16)] * (radix - 1)
+        outs = [pltpu.VMEM(shape, jnp.float32)] + [stacked(*shape, dtype=jnp.bfloat16)] * (radix - 1)
         out_specs = [pl.BlockSpec((1,) + o.shape[1:], lambda z, at: (z, 0, 0)) for o in outs]
         return fold_call(
             functools.partial(self.third_kernel, radix), self.count // radix, self.at, ins, in_specs, outs, out_specs, True
         )
 
-    def third_sent(self, out, *earlier):
+    def third_sent(self, out):
+        return [exchanged(part, "batch", 4 * d) for d, part in enumerate(out) if d > 0]
+
+    def total(self, kept, arrived, *earlier):
         radix = min(4, self.count)
-        arrived = [exchanged(part, "batch", 4 * d) for d, part in enumerate(out) if d > 0]
-        terms = [out[0]] + [after(part, *earlier) if earlier else part for part in arrived]
+        terms = [kept] + [after(part, *earlier) if earlier else part for part in arrived]
         total = None
         for term in terms:
             value = received(term, self.wide[1]) if term.dtype == jnp.bfloat16 else term
@@ -413,7 +415,7 @@
             far_off(width, tokens),
             far_off(pairs, 2, 2, rows, rows),
         ],
-        compiler_params=pltpu.CompilerParams(vmem_limit_bytes=24 << 20),
+        compiler_params=pltpu.CompilerParams(vmem_limit_bytes=14 << 20),
         cost_estimate=COST,
     )(at, *[far_away(triples)] * 3)
 
@@ -484,7 +486,7 @@
             ],
         ),
         out_shape=[pltpu.VMEM(triples.shape, jnp.bfloat16), stacked(2, 2, 1, width // 2)],
-        compiler_params=pltpu.CompilerParams(vmem_limit_bytes=24 << 20),
+        compiler_params=pltpu.CompilerParams(vmem_limit_bytes=16 << 20),
         cost_estimate=LONG_COST,
     )(at, *[far_away(triples)] * 3, context, grad, probs)
 
@@ -956,6 +958,52 @@
     return (grad, moment_new, weight_new, average_new)
 
 
+def finish_kernel(kept, first, second, third, out_grad, *refs):
+    states, outs = refs[:9], refs[9:]
+    quarter = out_grad.shape[1]
+    total = kept[...]
+    for part in (first, second, third):
+        total = total + received(part[...], True)
+
+    def write(at, grad, state, results, rate):
+        for result, value in zip(results, renew(grad, *[ref[at] for ref in state], rate), strict=True):
+            result[at] = value
+
+    for k in range(4):
+        grad = total[:, k * quarter : (k + 1) * quarter] if k < 3 else out_grad[...]
+        write((k,), grad, states[:3], outs[:4], RATE)
+    lines = total[:, -LANES:].T
+    write((Ellipsis,), lines[:4], states[3:6], outs[4:8], RATE)
+    write((Ellipsis,), total[:, 3 * quarter : -LANES], states[6:], outs[8:12], POS_RATE)
+    rows = kept.shape[0]
+    row = lax.broadcasted_iota(jnp.int32, (rows, 2 * rows), 0)
+    column = lax.broadcasted_iota(jnp.int32, (rows, 2 * rows), 1)
+    bias = jnp.zeros((8, 2 * rows), jnp.float32)
+    for k in range(2):
+        chosen = jnp.where(column == 2 * row + k, 1.0, 0.0)
+        line = jnp.broadcast_to(lines[4 + k : 5 + k], (8, rows))
+        bias = bias + jnp.dot(
+            line, chosen, precision=lax.Precision.HIGHEST, preferred_element_type=jnp.float32
+        )
+    outs[12][...] = bias[:1]
+
+
+def finished(kept, arrived, out_grad, attn_state, vector_state, pos_state):
+    pos_state = tuple(part.T for part in pos_state)
+    states = attn_state + vector_state + pos_state
+    outs = [stacked(*state[0].shape) for state in (attn_state, vector_state, pos_state) for _ in range(4)]
+    outs.append(stacked(1, 2 * kept.shape[0]))
+    out = pl.pallas_call(
+        finish_kernel,
+        in_specs=[HERE] * (5 + len(states)),
+        out_specs=[HERE] * len(outs),
+        out_shape=outs,
+        compiler_params=pltpu.CompilerParams(vmem_limit_bytes=20 << 20),
+        cost_estimate=COST,
+    )(kept, *arrived, out_grad, *states)
+    return out[:4], out[4:8], [part.T for part in out[8:12]], out[12]
+
+
 def local(
     tokens,
     lengths,
@@ -1095,12 +1143,13 @@
     )
     out_in = exchanged(out_away, "stream", 1)
     down_fold.at = after(at, out_own, *down_second)
-    down_parts = down_fold.third(down_second, down_kept)
+    down_last = down_fold.third(down_second, down_kept)
+    down_third = down_fold.third_sent(down_last)
     third = hidden_half // 3
     up_pair = (blocks(up_own), blocks(up_in))
     out_pair = (blocks(out_own), blocks(out_in))
     middle_fold = Fold(
-        after(at, *down_parts),
+        after(at, *down_last),
         [
             [up_pair + (rows, 0, third, 0, False), up_pair + (rows, 0, third, 1, False)],
             [up_pair + (rows, 0, third, 2, False), out_pair + (rows, 0, quarter, 0, False)],
@@ -1111,13 +1160,12 @@
     dcontext_half = halved(matmul(after(dresid1_half, *middle_parts), out_full, NT))
     dtriples, dsums = attend_back(at, triples, context_half, dcontext_half, probs)
     qkv_own, qkv_away = product(at, entry, dtriples, near=1)
-    down_sum = down_fold.third_sent(down_parts, qkv_away)
     qkv_in = exchanged(qkv_away, "stream", 1)
     middle_fold.at = after(at, qkv_away, *middle_first)
     middle_parts = middle_fold.second(middle_first)
     middle_second, middle_kept = middle_fold.second_sent(middle_parts)
     input_grad, last_own, last_away = left(
-        after(at, qkv_away, *middle_parts), dresid1, dtriples, qkv, dsums, sums1, sums2, dpre_sum
+        after(at, qkv_away, *middle_parts, *down_third), dresid1, dtriples, qkv, dsums, sums1, sums2, dpre_sum
     )
     last_in = exchanged(last_away, "stream", 1)
     qkv_pair = (blocks(qkv_own), blocks(qkv_in))
@@ -1140,26 +1188,40 @@
     middle_parts = middle_fold.third(middle_second, middle_kept)
     entry_fold.at = after(at, *middle_parts)
     entry_parts = entry_fold.second(entry_first)
-    middle_sum = middle_fold.third_sent(middle_parts, *entry_parts)
+    middle_third = middle_fold.third_sent(middle_parts)
+    middle_sum = middle_fold.total(middle_parts[0], middle_third, *entry_parts)
+    down_sum = down_fold.total(down_last[0], down_third, *entry_parts)
     entry_second, entry_kept = entry_fold.second_sent(entry_parts)
-    entry_sum = entry_fold.third_sent(entry_fold.third(entry_second, entry_kept))
+    entry_parts = entry_fold.third(entry_second, entry_kept)
+    vector_moment, vector_average = (
+        after(part, *entry_parts) for part in (vector_moment, vector_average)
+    )
+    entry_third = entry_fold.third_sent(entry_parts)
 
     down_grad = down_sum
     if by_rows:
         down_grad = jnp.concatenate([down_sum[:, :quarter], down_sum[:, quarter:]], axis=0)
-    attn_grad = jnp.stack(
-        [entry_sum[:, k * quarter : (k + 1) * quarter] for k in range(3)]
-        + [middle_sum[:, hidden_half : hidden_half + quarter]]
-    )
-    attn_all = renew(attn_grad, attn_moment, attn_weight, attn_average, RATE)
     up_all = renew(middle_sum[:, :hidden_half], up_moment, up_weight, up_average, RATE)
     down_all = renew(down_grad, down_moment, down_weight, down_average, RATE)
-    vector_grad = entry_sum[:, pos_stop : pos_stop + 4].T
-    vector_all = renew(vector_grad, vector_moment, layer_vectors, vector_average, RATE)
-    bias_grad = entry_sum[:, pos_stop + 4 : pos_stop + 6].reshape(-1)
+    out_grad = middle_sum[:, hidden_half : hidden_half + quarter]
+    attn_state = (attn_moment, attn_weight, attn_average)
+    vector_state = (vector_moment, layer_vectors, vector_average)
+    pos_state = (pos_moment, pos_table, pos_average)
+    if rows % 16 == 0:
+        attn_all, vector_all, pos_all, bias_grad = finished(
+            entry_parts[0][0], [part[0] for part in entry_third], out_grad, attn_state, vector_state, pos_state
+        )
+        bias_grad = bias_grad.reshape(-1)
+    else:
+        entry_sum = entry_fold.total(entry_parts[0], entry_third)
+        attn_grad = jnp.stack(
+            [entry_sum[:, k * quarter : (k + 1) * quarter] for k in range(3)] + [out_grad]
+        )
+        attn_all = renew(attn_grad, *attn_state, RATE)
+        vector_all = renew(entry_sum[:, pos_stop : pos_stop + 4].T, *vector_state, RATE)
+        pos_all = renew(entry_sum[:, triple:pos_stop].T, *pos_state, POS_RATE)
+        bias_grad = entry_sum[:, pos_stop + 4 : pos_stop + 6].reshape(-1)
     bias_all = renew(bias_grad, bias_moment, up_bias, bias_average, RATE)
-    pos_grad = entry_sum[:, triple:pos_stop].T
-    pos_all = renew(pos_grad, pos_moment, pos_table, pos_average, POS_RATE)
     return (
         block_out[None],
         input_grad[None],

time: 337 us -> 321 us (0.953)
  Pallas kernels: 162 us -> 152 us
  local copies, waits for them, and re-layouts: 16.7 us -> 11.4 us
    pallas_call x9, Pallas kernels: 32.6 us -> 22 us  [fold_call(): pl.pallas_call(kernel, grid_spec=pltpu.PrefetchScalarGridSpec(num_scalar_...]
    unnamed x108 -> x84, local copies, waits for them, and re-layouts: 7.73 us -> 3.66 us
  transfers between devices with their start and end apart: 52 -> 52, of which waited for: 28 -> 28; matrix products, arithmetic and copies ran while one was open for 6% -> 5% of each run, Pallas kernels for 33% -> 33%
where the time goes in v2:
time: 321 us; the launch traced here: 320 us
  Pallas kernels  152 us (47%)
  waiting for transfers between devices  75 us (23%)
  starting transfers between devices  54.5 us (17%)
  between operations  14.8 us (5%)
  local copies, waits for them, and re-layouts  11.4 us (4%)
  other arithmetic  10.4 us (3%)
    pallas_call x9, Pallas kernels, kernel_call(): pl.pallas_call(kernel, grid_spec=pltpu.PrefetchScalarGridSpec(num_scalar_...  83.6 us
    ppermute x51, waiting for transfers between devices, exchanged(): lax.ppermute(block, axis, [(place, place ^ mask) for place in range(count)])  74.2 us
    ppermute x51, starting transfers between devices, exchanged(): lax.ppermute(block, axis, [(place, place ^ mask) for place in range(count)])  54.5 us
    pallas_call x9, Pallas kernels, fold_call(): pl.pallas_call(kernel, grid_spec=pltpu.PrefetchScalarGridSpec(num_scalar_...  22 us
    pallas_call x1, Pallas kernels, attend_back(): pl.pallas_call(attend_back_kernel, grid_spec=pltpu.PrefetchScalarGridSpec...  19.7 us
    pallas_call x1, Pallas kernels, attend(): pl.pallas_call(attend_kernel, grid_spec=pltpu.PrefetchScalarGridSpec(num_...  19.1 us
  transfers between devices with their start and end apart: 52, of which 28 were waited for; matrix products, arithmetic and copies ran while one was open for 5% of the time, Pallas kernels for 33%

profile of v2, /device:TPU:0, one launch (start us, length us, event | category | flops | bytes accessed | tf_op | source)
XLA Modules:
  0.0 319.5 jit_solution(297014044212731052)
XLA Ops:
  10.8 5.1 %collective-permute-start.2 = (bf16[1,48,1536]{2,1,0:T(8,128)(2,1)S(1)}, bf16[1,48,1536]{2,1,0:T(8,128)(2,1)S(1)}, u32[]{:S(2)}, u32[]{:S(2)}) collective-permute-start(bf16[1,48,1536]{2,1,0:T(8,128)(2,1)S(1)} %constant_dynamic-update-slice_fusion), channel_id=1, source_target_pairs={{0,12},{1,13},{2,14},{3,15},{4,8},{5,9},{6,10},{7,11},{8,4},{9,5},... | collective-permute-start | bytes 442376 | tf_op jit(solution)/shard_map/ppermute | solution.py:59
  16.5 1.6 convert_element_type.39
  18.2 2.5 collective-permute-done.2
  20.7 7.7 %collective-permute-done.1 = bf16[1,48,1536]{2,1,0:T(8,128)(2,1)S(1)} collective-permute-done((bf16[1,48,1536]{2,1,0:T(8,128)(2,1)S(1)}, bf16[1,48,1536]{2,1,0:T(8,128)(2,1)S(1)}, u32[]{:S(2)}, u32[]{:S(2)}) %collective-permute-start.1) | collective-permute-done | bytes 147488 | tf_op jit(solution)/shard_map/ppermute | solution.py:59
  28.6 1.6 collective-permute-start.4
  30.2 1.5 collective-permute-start.3
  31.7 5.0 %collective-permute-done.4 = bf16[4,48,768]{2,1,0:T(8,128)(2,1)S(1)} collective-permute-done((bf16[4,48,768]{2,1,0:T(8,128)(2,1)S(1)}, bf16[4,48,768]{2,1,0:T(8,128)(2,1)S(1)}, u32[]{:S(2)}, u32[]{:S(2)}) %collective-permute-start.4) | collective-permute-done | bytes 294944 | tf_op jit(solution)/shard_map/ppermute | solution.py:59
  36.8 1.2 collective-permute-done.3
  38.0 2.4 collective-permute-start.7
  40.4 2.1 collective-permute-start.5
  42.5 1.5 collective-permute-start.9
  44.5 3.9 %collective-permute-done.7 = bf16[1,48,2048]{2,1,0:T(8,128)(2,1)S(1)} collective-permute-done((bf16[1,48,2048]{2,1,0:T(8,128)(2,1)S(1)}, bf16[1,48,2048]{2,1,0:T(8,128)(2,1)S(1)}, u32[]{:S(2)}, u32[]{:S(2)}) %collective-permute-start.7) | collective-permute-done | bytes 196640 | tf_op jit(solution)/shard_map/ppermute | solution.py:59
  48.4 9.9 %collective-permute-done.6 = bf16[1,48,2048]{2,1,0:T(8,128)(2,1)S(1)} collective-permute-done((bf16[1,48,2048]{2,1,0:T(8,128)(2,1)S(1)}, bf16[1,48,2048]{2,1,0:T(8,128)(2,1)S(1)}, u32[]{:S(2)}, u32[]{:S(2)}) %collective-permute-start.6) | collective-permute-done | bytes 196640 | tf_op jit(solution)/shard_map/ppermute | solution.py:59
  60.8 1.5 collective-permute-start.12
  63.7 1.7 shard_map.395
  65.4 8.4 %shard_map.396 = (f32[1024,768]{1,0:T(8,128)}, bf16[768,1024]{1,0:T(8,128)(2,1)}, bf16[2,1024,1152]{2,1,0:T(8,128)(2,1)}, f32[8,768]{1,0:T(8,128)S(1)}, f32[4,768]{1,0:T(4,128)S(1)}) custom-call(s32[13]{0:T(128)S(1)} %concatenate.66.at_ref.at, bf16[1024,768]{1,0:T(8,128)(2,1)} %bitcast.100, bf16[768,512]{1,0:T(8,128)(2,1)S(1)} %bitcast.80, ...), custom_call_target="tpu_custom_call" | custom-call | flops 1000 | bytes 1000 | tf_op jit(solution)/shard_map/pallas_call | solution.py:512
  76.8 1.6 collective-permute-start.15
  81.2 19.1 %shard_map.397 = (bf16[1024,768]{1,0:T(8,128)(2,1)}, bf16[768,1024]{1,0:T(8,128)(2,1)}, bf16[6,2,2,512,512]{4,3,2,1,0:T(8,128)(2,1)}) custom-call(s32[13]{0:T(128)S(1)} %concatenate.66.at_ref.at, bf16[2,1024,1152]{2,1,0:T(8,128)(2,1)} %get-tuple-element.156.q_ref.k_ref.v_ref, bf16[2,1024,1152]{2,1,0:T(8,128)(2,1)} %get-tuple-element.156.q_ref.k_ref.v_ref, ...), custom_call_target="tpu_custom_call" | custom-call | flops 1000 | bytes 1000 | tf_op jit(solution)/shard_map/pallas_call | solution.py:396
  100.3 3.8 %collective-permute-done.15 = bf16[8,48,1024]{2,1,0:T(8,128)(2,1)S(1)} collective-permute-done((bf16[8,48,1024]{2,1,0:T(8,128)(2,1)S(1)}, bf16[8,48,1024]{2,1,0:T(8,128)(2,1)S(1)}, u32[]{:S(2)}, u32[]{:S(2)}) %collective-permute-start.15) | collective-permute-done | bytes 786464 | tf_op jit(solution)/shard_map/ppermute | solution.py:59
  104.3 3.3 %collective-permute-done.14 = bf16[8,48,1024]{2,1,0:T(8,128)(2,1)S(1)} collective-permute-done((bf16[8,48,1024]{2,1,0:T(8,128)(2,1)S(1)}, bf16[8,48,1024]{2,1,0:T(8,128)(2,1)S(1)}, u32[]{:S(2)}, u32[]{:S(2)}) %collective-permute-start.14) | collective-permute-done | bytes 786464 | tf_op jit(solution)/shard_map/ppermute | solution.py:59
  107.7 1.2 copy.58
  108.9 1.6 reshape.201
  112.4 4.6 %shard_map.398 = (bf16[2,16,48,1536]{3,2,1,0:T(8,128)(2,1)S(1)}, bf16[16,48,768]{2,1,0:T(8,128)(2,1)S(1)}, bf16[3072,768]{1,0:T(8,128)(2,1)S(1)}) custom-call(s32[13]{0:T(128)S(1)} %concatenate.66.at_ref.at, bf16[16,48,1024]{2,1,0:T(8,128)(2,1)S(1)} %constant_dynamic-update-slice_fusion.13.refs_0_, ...), custom_call_target="tpu_custom_call" | custom-call | flops 1000 | bytes 1000 | tf_op jit(solution)/shard_map/pallas_call | solution.py:166
  117.0 22.1 %shard_map.399 = (bf16[768,1024]{1,0:T(8,128)(2,1)}, bf16[1024,768]{1,0:T(8,128)(2,1)}, f32[1024,1]{1,0:T(8,128)S(1)}, bf16[3072,1024]{1,0:T(8,128)(2,1)S(1)}, b...) custom-call(s32[13]{0:T(128)S(1)} %concatenate.66.at_ref.at, ...), custom_call_target="tpu_custom_call" | custom-call | flops 1000 | bytes 1000 | tf_op jit(solution)/shard_map/pallas_call | solution.py:512
  141.0 1.6 collective-permute-start.18
  142.6 1.1 collective-permute-done.20
  144.7 1.6 collective-permute-start.23
  147.3 1.9 collective-permute-start.21
  149.2 2.3 collective-permute-done.21
  152.5 1.5 collective-permute-done.24.others
  153.9 6.3 %shard_map.400 = (f32[1024,768]{1,0:T(8,128)}, bf16[1024,768]{1,0:T(8,128)(2,1)S(1)}, f32[3,768]{1,0:T(4,128)S(1)}) custom-call(s32[13]{0:T(128)S(1)} %concatenate.66.at_ref.at, bf16[128,896]{1,0:T(8,128)(2,1)S(1)} %bitcast.85, bf16[128,896]{1,0:T(8,128)(2,1)S(1)} %collective-permute-done.24.others, f32[8,768]{1,0:T(8,128)S(1)} %get-tuple-element.174.pooled, ...), custom_call_target="tpu_custom_call" | custom-call | flops 1000 | bytes 1000 | tf_op jit(solution)/shard_map/pallas_call | solution.py:512
  160.2 6.8 %shard_map.401 = (bf16[3072,384]{1,0:T(8,128)(2,1)S(1)}, bf16[3072,384]{1,0:T(8,128)(2,1)S(1)}) custom-call(s32[13]{0:T(128)S(1)} %concatenate.66.at_ref.at, bf16[3072,1024]{1,0:T(8,128)(2,1)S(1)} %get-tuple-element.172.left_ref, bf16[1024,768]{1,0:T(8,128)(2,1)S(1)} %get-tuple-element.177.right_ref.dresid2_half), custom_call_target="tpu_custom_call" | custom-call | flops 999999995904 | bytes 1000000000 | tf_op jit(solution)/shard_map/pallas_call | solution.py:512
  167.2 4.4 %collective-permute-done.25 = bf16[3072,384]{1,0:T(8,128)(2,1)S(1)} collective-permute-done((bf16[3072,384]{1,0:T(8,128)(2,1)S(1)}, bf16[3072,384]{1,0:T(8,128)(2,1)S(1)}, u32[]{:S(2)}, u32[]{:S(2)}) %collective-permute-start.25) | collective-permute-done | bytes 2359328 | tf_op jit(solution)/shard_map/ppermute | solution.py:59
  171.6 2.4 shard_map.402
  174.1 1.5 collective-permute-start.26
  176.5 14.5 %shard_map.403 = (bf16[1024,3072]{1,0:T(8,128)(2,1)S(1)}, f32[1,3072]{1,0:T(1,128)S(1)}, f32[1024,768]{1,0:T(8,128)}, bf16[1024,768]{1,0:T(8,128)(2,1)S(1)}, f32[3,768]{1,0:T(4,128)S(1)}) custom-call(s32[13]{0:T(128)S(1)} %concatenate.66.at_ref.at, f32[1024,768]{1,0:T(8,128)} %get-tuple-element.185.dresid2, ...), custom_call_target="tpu_custom_call" | custom-call | flops 999999995904 | bytes 1000000000 | tf_op jit(solution)/shard_map/pallas_call | solution.py:512
  191.0 3.3 %shard_map.404 = (bf16[4,96,384]{2,1,0:T(8,128)(2,1)}, f32[4,96,384]{2,1,0:T(8,128)S(1)}, bf16[4,96,384]{2,1,0:T(8,128)(2,1)}, f32[4,96,384]{2,1,0:T(8,128)S(1)}) custom-call(s32[13]{0:T(128)S(1)} %concatenate.66.at_ref.at, f32[4,2,96,384]{3,2,1,0:T(8,128)S(1)} %get-tuple-element.181.refs_0_, bf16[4,2,96,384]{3,2,1,0:T(8,128)(2,1)} %collective-permute-done.26.refs_1_, ...), custom_call_target="tpu_custom_call" | custom-call | flops 1000 | bytes 1000 | tf_op jit(solution)/shard_map/pallas_call | solution.py:218
  196.0 6.8 %shard_map.405 = (bf16[768,1536]{1,0:T(8,128)(2,1)S(1)}, bf16[768,1536]{1,0:T(8,128)(2,1)}) custom-call(s32[13]{0:T(128)S(1)} %concatenate.66.at_ref.at, bf16[768,1024]{1,0:T(8,128)(2,1)S(1)} %copy-done.16, bf16[1024,3072]{1,0:T(8,128)(2,1)S(1)} %get-tuple-element.197.right_ref), custom_call_target="tpu_custom_call" | custom-call | flops 999999995904 | bytes 1000000000 | tf_op jit(solution)/shard_map/pallas_call | solution.py:512
  203.9 3.1 shard_map.406
  207.0 2.4 shard_map.407
  209.4 1.2 collective-permute-start.34
  210.6 1.2 collective-permute-start.35
  211.8 2.0 collective-permute-start.36
  213.8 4.3 %shard_map.408 = (bf16[4,2,48,1024]{3,2,1,0:T(8,128)(2,1)}, f32[4,2,48,1024]{3,2,1,0:T(8,128)S(1)}, bf16[4,2,48,896]{3,2,1,0:T(8,128)(2,1)}, f32[4,2,48,896]{3,2,1,0:T(8,128)S(1)}) custom-call(s32[13]{0:T(128)S(1)} %concatenate.66.at_ref.at, bf16[4,2,2,48,1536]{4,3,2,1,0:T(8,128)(2,1)S(1)} %bitcast.60, ...), custom_call_target="tpu_custom_call" | custom-call | flops 1000 | bytes 1000 | tf_op jit(solution)/shard_map/pallas_call | solution.py:218
  220.0 1.4 convolution_convert_fusion.grad_ref
  221.4 1.2 slice-done.2
  222.7 19.7 %shard_map.409 = (bf16[2,1024,1152]{2,1,0:T(8,128)(2,1)S(1)}, f32[2,2,1,384]{3,2,1,0:T(1,128)S(1)}) custom-call(s32[13]{0:T(128)S(1)} %concatenate.66.at_ref.at, bf16[2,1024,1152]{2,1,0:T(8,128)(2,1)} %get-tuple-element.156.q_ref.k_ref.v_ref, bf16[2,1024,1152]{2,1,0:T(8,128)(2,1)} %get-tuple-element.156.q_ref.k_ref.v_ref, ...), custom_call_target="tpu_custom_call" | custom-call | flops 999999995904 | bytes 1000000000 | tf_op jit(solution)/shard_map/pallas_call | solution.py:470
  242.4 6.0 %shard_map.410 = (bf16[768,1152]{1,0:T(8,128)(2,1)S(1)}, bf16[768,1152]{1,0:T(8,128)(2,1)}) custom-call(s32[13]{0:T(128)S(1)} %concatenate.66.at_ref.at, bf16[768,1024]{1,0:T(8,128)(2,1)S(1)} %copy-done.14, bf16[2,1024,1152]{2,1,0:T(8,128)(2,1)S(1)} %get-tuple-element.216.right_ref.dtriples), custom_call_target="tpu_custom_call" | custom-call | flops 999999995904 | bytes 1000000000 | tf_op jit(solution)/shard_map/pallas_call | solution.py:512
  248.4 2.4 shard_map.411
  250.9 9.5 %shard_map.412 = (f32[1024,768]{1,0:T(8,128)}, f32[768,384]{1,0:T(8,128)S(1)}, bf16[768,384]{1,0:T(8,128)(2,1)S(1)}) custom-call(s32[13]{0:T(128)S(1)} %concatenate.66.at_ref.at, f32[1024,768]{1,0:T(8,128)} %get-tuple-element.224.dresid1, bf16[2,1024,1152]{2,1,0:T(8,128)(2,1)S(1)} %get-tuple-element.216.right_ref.dtriples, ...), custom_call_target="tpu_custom_call" | custom-call | flops 999999995904 | bytes 1000000000 | tf_op jit(solution)/shard_map/pallas_call | solution.py:512
  262.9 3.6 %shard_map.413 = (bf16[4,2,48,768]{3,2,1,0:T(8,128)(2,1)}, f32[4,2,48,768]{3,2,1,0:T(8,128)S(1)}, bf16[4,2,48,768]{3,2,1,0:T(8,128)(2,1)}, f32[4,2,48,768]{3,2,1,0:T(8,128)S(1)}) custom-call(s32[13]{0:T(128)S(1)} %concatenate.66.at_ref.at, bf16[4,2,2,48,1152]{4,3,2,1,0:T(8,128)(2,1)S(1)} %bitcast.63, ...), custom_call_target="tpu_custom_call" | custom-call | flops 1000 | bytes 1000 | tf_op jit(solution)/shard_map/pallas_call | solution.py:218
  268.3 4.4 %collective-permute-done.40.in1 = bf16[4,48,896]{2,1,0:T(8,128)(2,1)S(1)} collective-permute-done((bf16[4,48,896]{2,1,0:T(8,128)(2,1)S(1)}, bf16[4,48,896]{2,1,0:T(8,128)(2,1)S(1)}, u32[]{:S(2)}, u32[]{:S(2)}) %collective-permute-start.40) | collective-permute-done | bytes 344096 | tf_op jit(solution)/shard_map/ppermute | solution.py:59
  273.4 1.9 collective-permute-start.50
  275.3 2.6 collective-permute-start.48
  277.9 6.6 %collective-permute-done.41.refs_1_ = bf16[4,2,48,768]{3,2,1,0:T(8,128)(2,1)} collective-permute-done((bf16[4,2,48,768]{3,2,1,0:T(8,128)(2,1)}, bf16[4,2,48,768]{3,2,1,0:T(8,128)(2,1)}, u32[]{:S(2)}, u32[]{:S(2)}) %collective-permute-start.41) | collective-permute-done | bytes 589856 | tf_op jit(solution)/shard_map/ppermute | solution.py:59
  284.7 2.1 shard_map.415
  286.8 1.2 collective-permute-start.43
  289.1 1.3 collective-permute-done.49
  293.5 1.8 collective-permute-done.43.in0
  297.4 2.1 collective-permute-start.46
  299.4 2.0 collective-permute-start.47
  302.9 7.1 %collective-permute-done.46 = bf16[1,48,1536]{2,1,0:T(8,128)(2,1)S(1)} collective-permute-done((bf16[1,48,1536]{2,1,0:T(8,128)(2,1)S(1)}, bf16[1,48,1536]{2,1,0:T(8,128)(2,1)S(1)}, u32[]{:S(2)}, u32[]{:S(2)}) %collective-permute-start.46) | collective-permute-done | bytes 147488 | tf_op jit(solution)/shard_map/ppermute | solution.py:59
  310.1 1.3 shard_map.417
  311.5 1.2 add_multiply_fusion.2
  (190 shorter events, 40.3 us)
Async XLA Ops:
  7.2 21.3 %copy-start.19 = (f32[48,1536]{1,0:T(8,128)S(1)}, f32[48,1536]{1,0:T(8,128)}, u32[]{:S(2)}) copy-start(f32[48,1536]{1,0:T(8,128)} %param.25) | copy-start | bytes 884740
  7.2 105.2 %all-gather.2.cloned.1.call-start = ((), (), s32[]{:S(2)}) async-start(), calls=%async_computation | async-start | bytes 4866048 | tf_op jit(solution)/shard_map/all_gather | solution.py:1051
  10.8 9.9 %collective-permute-start.2 = (bf16[1,48,1536]{2,1,0:T(8,128)(2,1)S(1)}, bf16[1,48,1536]{2,1,0:T(8,128)(2,1)S(1)}, u32[]{:S(2)}, u32[]{:S(2)}) collective-permute-start(bf16[1,48,1536]{2,1,0:T(8,128)(2,1)S(1)} %constant_dynamic-update-slice_fusion), channel_id=1, source_target_pairs={{0,12},{1,13},{2,14},{3,15},{4,8},{5,9},{6,10},{7,11},{8,4},{9,5},... | collective-permute-start | bytes 442376 | tf_op jit(solution)/shard_map/ppermute | solution.py:59
  15.9 12.5 %collective-permute-start.1 = (bf16[1,48,1536]{2,1,0:T(8,128)(2,1)S(1)}, bf16[1,48,1536]{2,1,0:T(8,128)(2,1)S(1)}, u32[]{:S(2)}, u32[]{:S(2)}) collective-permute-start(bf16[1,48,1536]{2,1,0:T(8,128)(2,1)S(1)} %constant_dynamic-update-slice_fusion), channel_id=1, source_target_pairs={{0,8},{1,9},{2,10},{3,11},{4,12},{5,13},{6,14},{7,15},{8,0},{9,1},... | collective-permute-start | bytes 442376 | tf_op jit(solution)/shard_map/ppermute | solution.py:59
  15.9 12.5 %collective-permute-start = (bf16[1,48,1536]{2,1,0:T(8,128)(2,1)S(1)}, bf16[1,48,1536]{2,1,0:T(8,128)(2,1)S(1)}, u32[]{:S(2)}, u32[]{:S(2)}) collective-permute-start(bf16[1,48,1536]{2,1,0:T(8,128)(2,1)S(1)} %constant_dynamic-update-slice_fusion), channel_id=1, source_target_pairs={{0,4},{1,5},{2,6},{3,7},{4,0},{5,1},{6,2},{7,3},{8,12},{9,13},{10,... | collective-permute-start | bytes 442376 | tf_op jit(solution)/shard_map/ppermute | solution.py:59
  28.6 8.1 %collective-permute-start.4 = (bf16[4,48,768]{2,1,0:T(8,128)(2,1)S(1)}, bf16[4,48,768]{2,1,0:T(8,128)(2,1)S(1)}, u32[]{:S(2)}, u32[]{:S(2)}) collective-permute-start(bf16[4,48,768]{2,1,0:T(8,128)(2,1)S(1)} %get-tuple-element.285), channel_id=1, source_target_pairs={{0,1},{1,0},{2,3},{3,2},{4,5},{5,4},{6,7},{7,6},{8,9},{9,8},{10,11... | collective-permute-start | bytes 884744 | tf_op jit(solution)/shard_map/ppermute | solution.py:59
  30.2 7.8 %collective-permute-start.3 = (bf16[4,48,768]{2,1,0:T(8,128)(2,1)S(1)}, bf16[4,48,768]{2,1,0:T(8,128)(2,1)S(1)}, u32[]{:S(2)}, u32[]{:S(2)}) collective-permute-start(bf16[4,48,768]{2,1,0:T(8,128)(2,1)S(1)} %get-tuple-element.286), channel_id=1, source_target_pairs={{0,2},{1,3},{2,0},{3,1},{4,6},{5,7},{6,4},{7,5},{8,10},{9,11},{10,... | collective-permute-start | bytes 884744 | tf_op jit(solution)/shard_map/ppermute | solution.py:59
  38.0 10.4 %collective-permute-start.7 = (bf16[1,48,2048]{2,1,0:T(8,128)(2,1)S(1)}, bf16[1,48,2048]{2,1,0:T(8,128)(2,1)S(1)}, u32[]{:S(2)}, u32[]{:S(2)}) collective-permute-start(bf16[1,48,2048]{2,1,0:T(8,128)(2,1)S(1)} %bitcast.101), channel_id=1, source_target_pairs={{0,12},{1,13},{2,14},{3,15},{4,8},{5,9},{6,10},{7,11},{8,4},{9,5},... | collective-permute-start | bytes 589832 | tf_op jit(solution)/shard_map/ppermute | solution.py:59
  40.4 17.9 %collective-permute-start.6 = (bf16[1,48,2048]{2,1,0:T(8,128)(2,1)S(1)}, bf16[1,48,2048]{2,1,0:T(8,128)(2,1)S(1)}, u32[]{:S(2)}, u32[]{:S(2)}) collective-permute-start(bf16[1,48,2048]{2,1,0:T(8,128)(2,1)S(1)} %bitcast.102), channel_id=1, source_target_pairs={{0,8},{1,9},{2,10},{3,11},{4,12},{5,13},{6,14},{7,15},{8,0},{9,1},... | collective-permute-start | bytes 589832 | tf_op jit(solution)/shard_map/ppermute | solution.py:59
  40.4 17.9 %collective-permute-start.5 = (bf16[1,48,2048]{2,1,0:T(8,128)(2,1)S(1)}, bf16[1,48,2048]{2,1,0:T(8,128)(2,1)S(1)}, u32[]{:S(2)}, u32[]{:S(2)}) collective-permute-start(bf16[1,48,2048]{2,1,0:T(8,128)(2,1)S(1)} %bitcast.103), channel_id=1, source_target_pairs={{0,4},{1,5},{2,6},{3,7},{4,0},{5,1},{6,2},{7,3},{8,12},{9,13},{10,... | collective-permute-start | bytes 589832 | tf_op jit(solution)/shard_map/ppermute | solution.py:59
  42.5 16.1 %collective-permute-start.9 = (bf16[8,48,768]{2,1,0:T(8,128)(2,1)S(1)}, bf16[8,48,768]{2,1,0:T(8,128)(2,1)S(1)}, u32[]{:S(2)}, u32[]{:S(2)}) collective-permute-start(bf16[8,48,768]{2,1,0:T(8,128)(2,1)S(1)} %pad_maximum_fusion.3), channel_id=1, source_target_pairs={{0,2},{1,3},{2,0},{3,1},{4,6},{5,7},{6,4},{7,5},{8,10},{9,11},{10,... | collective-permute-start | bytes 1769480 | tf_op jit(solution)/shard_map/ppermute | solution.py:59
  44.0 14.7 %collective-permute-start.8 = (bf16[8,48,768]{2,1,0:T(8,128)(2,1)S(1)}, bf16[8,48,768]{2,1,0:T(8,128)(2,1)S(1)}, u32[]{:S(2)}, u32[]{:S(2)}) collective-permute-start(bf16[8,48,768]{2,1,0:T(8,128)(2,1)S(1)} %pad_maximum_fusion.2), channel_id=1, source_target_pairs={{0,1},{1,0},{2,3},{3,2},{4,5},{5,4},{6,7},{7,6},{8,9},{9,8},{10,11... | collective-permute-start | bytes 1769480 | tf_op jit(solution)/shard_map/ppermute | solution.py:59
  58.6 5.1 %collective-permute-start.11 = (bf16[16,48,768]{2,1,0:T(8,128)(2,1)S(1)}, bf16[16,48,768]{2,1,0:T(8,128)(2,1)S(1)}, u32[]{:S(2)}, u32[]{:S(2)}) collective-permute-start(bf16[16,48,768]{2,1,0:T(8,128)(2,1)S(1)} %constant_dynamic-update-slice_fusion.7.refs_1_), channel_id=1, source_target_pairs={{0,16},{16,0},{1,17},{17,1},{2,18},{18,2},{3,19},{19,3},{4,20},{20... | collective-permute-start | bytes 3538952 | tf_op jit(solution)/shard_map/ppermute | solution.py:59
  58.7 5.0 %collective-permute-start.10 = (bf16[16,48,768]{2,1,0:T(8,128)(2,1)S(1)}, bf16[16,48,768]{2,1,0:T(8,128)(2,1)}, u32[]{:S(2)}, u32[]{:S(2)}) collective-permute-start(bf16[16,48,768]{2,1,0:T(8,128)(2,1)S(1)} %constant_dynamic-update-slice_fusion.5.refs_0_), channel_id=1, source_target_pairs={{0,16},{16,0},{1,17},{17,1},{2,18},{18,2},{3,19},{19,3},{4,20},{20... | collective-permute-start | bytes 3538952 | tf_op jit(solution)/shard_map/ppermute | solution.py:59
  60.2 15.6 %collective-permute-start.13 = (bf16[4,48,1024]{2,1,0:T(8,128)(2,1)}, bf16[4,48,1024]{2,1,0:T(8,128)(2,1)}, u32[]{:S(2)}, u32[]{:S(2)}) collective-permute-start(bf16[4,48,1024]{2,1,0:T(8,128)(2,1)} %get-tuple-element.158), channel_id=1, source_target_pairs={{0,1},{1,0},{2,3},{3,2},{4,5},{5,4},{6,7},{7,6},{8,9},{9,8},{10,11... | collective-permute-start | bytes 1179656 | tf_op jit(solution)/shard_map/ppermute | solution.py:59
  60.8 18.6 %collective-permute-start.12 = (bf16[4,48,1024]{2,1,0:T(8,128)(2,1)}, bf16[4,48,1024]{2,1,0:T(8,128)(2,1)}, u32[]{:S(2)}, u32[]{:S(2)}) collective-permute-start(bf16[4,48,1024]{2,1,0:T(8,128)(2,1)} %get-tuple-element.157), channel_id=1, source_target_pairs={{0,2},{1,3},{2,0},{3,1},{4,6},{5,7},{6,4},{7,5},{8,10},{9,11},{10,... | collective-permute-start | bytes 1179656 | tf_op jit(solution)/shard_map/ppermute | solution.py:59
  76.8 27.4 %collective-permute-start.15 = (bf16[8,48,1024]{2,1,0:T(8,128)(2,1)S(1)}, bf16[8,48,1024]{2,1,0:T(8,128)(2,1)S(1)}, u32[]{:S(2)}, u32[]{:S(2)}) collective-permute-start(bf16[8,48,1024]{2,1,0:T(8,128)(2,1)S(1)} %constant_dynamic-update-slice_fusion.11), channel_id=1, source_target_pairs={{0,2},{1,3},{2,0},{3,1},{4,6},{5,7},{6,4},{7,5},{8,10},{9,11},{10,... | collective-permute-start | bytes 2359304 | tf_op jit(solution)/shard_map/ppermute | solution.py:59
  80.5 27.1 %collective-permute-start.14 = (bf16[8,48,1024]{2,1,0:T(8,128)(2,1)S(1)}, bf16[8,48,1024]{2,1,0:T(8,128)(2,1)S(1)}, u32[]{:S(2)}, u32[]{:S(2)}) collective-permute-start(bf16[8,48,1024]{2,1,0:T(8,128)(2,1)S(1)} %constant_dynamic-update-slice_fusion.9), channel_id=1, source_target_pairs={{0,1},{1,0},{2,3},{3,2},{4,5},{5,4},{6,7},{7,6},{8,9},{9,8},{10,11... | collective-permute-start | bytes 2359304 | tf_op jit(solution)/shard_map/ppermute | solution.py:59
  104.2 6.3 %collective-permute-start.17 = (bf16[16,48,1024]{2,1,0:T(8,128)(2,1)S(1)}, bf16[16,48,1024]{2,1,0:T(8,128)(2,1)}, u32[]{:S(2)}, u32[]{:S(2)}) collective-permute-start(bf16[16,48,1024]{2,1,0:T(8,128)(2,1)S(1)} %constant_dynamic-update-slice_fusion.15.refs_1_), channel_id=1, source_target_pairs={{0,16},{16,0},{1,17},{17,1},{2,18},{18,2},{3,19},{19,3},{4,20},{20... | collective-permute-start | bytes 4718600 | tf_op jit(solution)/shard_map/ppermute | solution.py:59
  107.6 4.0 %collective-permute-start.16 = (bf16[16,48,1024]{2,1,0:T(8,128)(2,1)S(1)}, bf16[16,48,1024]{2,1,0:T(8,128)(2,1)}, u32[]{:S(2)}, u32[]{:S(2)}) collective-permute-start(bf16[16,48,1024]{2,1,0:T(8,128)(2,1)S(1)} %constant_dynamic-update-slice_fusion.13.refs_0_), channel_id=1, source_target_pairs={{0,16},{16,0},{1,17},{17,1},{2,18},{18,2},{3,19},{19,3},{4,20},{20... | collective-permute-start | bytes 4718600 | tf_op jit(solution)/shard_map/ppermute | solution.py:59
  117.0 22.1 %copy-start.3 = (bf16[16,48,768]{2,1,0:T(8,128)(2,1)}, bf16[16,48,768]{2,1,0:T(8,128)(2,1)S(1)}, u32[]{:S(2)}) copy-start(bf16[16,48,768]{2,1,0:T(8,128)(2,1)S(1)} %get-tuple-element.165) | copy-start | bytes 3538948
  139.1 4.7 %collective-permute-start.20 = (bf16[1,8,896]{2,1,0:T(8,128)(2,1)S(1)}, bf16[1,8,896]{2,1,0:T(8,128)(2,1)S(1)}, u32[]{:S(2)}, u32[]{:S(2)}) collective-permute-start(bf16[1,8,896]{2,1,0:T(8,128)(2,1)S(1)} %bitcast.90), channel_id=1, source_target_pairs={{0,3},{1,2},{2,1},{3,0},{4,7},{5,6},{6,5},{7,4},{8,11},{9,10},{10,... | collective-permute-start | bytes 43016 | tf_op jit(solution)/shard_map/ppermute | solution.py:59
  140.0 3.9 %collective-permute-start.19 = (bf16[1,8,896]{2,1,0:T(8,128)(2,1)S(1)}, bf16[1,8,896]{2,1,0:T(8,128)(2,1)S(1)}, u32[]{:S(2)}, u32[]{:S(2)}) collective-permute-start(bf16[1,8,896]{2,1,0:T(8,128)(2,1)S(1)} %bitcast.91), channel_id=1, source_target_pairs={{0,2},{1,3},{2,0},{3,1},{4,6},{5,7},{6,4},{7,5},{8,10},{9,11},{10,... | collective-permute-start | bytes 43016 | tf_op jit(solution)/shard_map/ppermute | solution.py:59
  141.0 3.7 %collective-permute-start.18 = (bf16[1,8,896]{2,1,0:T(8,128)(2,1)S(1)}, bf16[1,8,896]{2,1,0:T(8,128)(2,1)S(1)}, u32[]{:S(2)}, u32[]{:S(2)}) collective-permute-start(bf16[1,8,896]{2,1,0:T(8,128)(2,1)S(1)} %bitcast.92), channel_id=1, source_target_pairs={{0,1},{1,0},{2,3},{3,2},{4,5},{5,4},{6,7},{7,6},{8,9},{9,8},{10,11... | collective-permute-start | bytes 43016 | tf_op jit(solution)/shard_map/ppermute | solution.py:59
  144.7 7.6 %collective-permute-start.23 = (bf16[4,8,896]{2,1,0:T(8,128)(2,1)S(1)}, bf16[4,8,896]{2,1,0:T(8,128)(2,1)S(1)}, u32[]{:S(2)}, u32[]{:S(2)}) collective-permute-start(bf16[4,8,896]{2,1,0:T(8,128)(2,1)S(1)} %pad_maximum_fusion.5), channel_id=1, source_target_pairs={{0,12},{1,13},{2,14},{3,15},{4,8},{5,9},{6,10},{7,11},{8,4},{9,5},... | collective-permute-start | bytes 172040 | tf_op jit(solution)/shard_map/ppermute | solution.py:59
  146.4 6.0 %collective-permute-start.22 = (bf16[4,8,896]{2,1,0:T(8,128)(2,1)S(1)}, bf16[4,8,896]{2,1,0:T(8,128)(2,1)S(1)}, u32[]{:S(2)}, u32[]{:S(2)}) collective-permute-start(bf16[4,8,896]{2,1,0:T(8,128)(2,1)S(1)} %pad_maximum_fusion.5), channel_id=1, source_target_pairs={{0,8},{1,9},{2,10},{3,11},{4,12},{5,13},{6,14},{7,15},{8,0},{9,1},... | collective-permute-start | bytes 172040 | tf_op jit(solution)/shard_map/ppermute | solution.py:59
  147.3 4.2 %collective-permute-start.21 = (bf16[4,8,896]{2,1,0:T(8,128)(2,1)S(1)}, bf16[4,8,896]{2,1,0:T(8,128)(2,1)S(1)}, u32[]{:S(2)}, u32[]{:S(2)}) collective-permute-start(bf16[4,8,896]{2,1,0:T(8,128)(2,1)S(1)} %pad_maximum_fusion.5), channel_id=1, source_target_pairs={{0,4},{1,5},{2,6},{3,7},{4,0},{5,1},{6,2},{7,3},{8,12},{9,13},{10,... | collective-permute-start | bytes 172040 | tf_op jit(solution)/shard_map/ppermute | solution.py:59
  152.4 1.6 collective-permute-start.24
  167.0 4.6 %collective-permute-start.25 = (bf16[3072,384]{1,0:T(8,128)(2,1)S(1)}, bf16[3072,384]{1,0:T(8,128)(2,1)S(1)}, u32[]{:S(2)}, u32[]{:S(2)}) collective-permute-start(bf16[3072,384]{1,0:T(8,128)(2,1)S(1)} %get-tuple-element.179), channel_id=1, source_target_pairs={{0,16},{16,0},{1,17},{17,1},{2,18},{18,2},{3,19},{19,3},{4,20},{20... | collective-permute-start | bytes 7077896 | tf_op jit(solution)/shard_map/ppermute | solution.py:59
  174.1 16.9 %collective-permute-start.26 = (bf16[4,2,96,384]{3,2,1,0:T(8,128)(2,1)}, bf16[4,2,96,384]{3,2,1,0:T(8,128)(2,1)}, u32[]{:S(2)}, u32[]{:S(2)}) collective-permute-start(bf16[4,2,96,384]{3,2,1,0:T(8,128)(2,1)} %get-tuple-element.180), channel_id=1, source_target_pairs={{0,1},{1,0},{2,3},{3,2},{4,5},{5,4},{6,7},{7,6},{8,9},{9,8},{10,11... | collective-permute-start | bytes 1769480 | tf_op jit(solution)/shard_map/ppermute | solution.py:59
  175.5 15.5 %collective-permute-start.27 = (bf16[4,2,96,384]{3,2,1,0:T(8,128)(2,1)}, bf16[4,2,96,384]{3,2,1,0:T(8,128)(2,1)}, u32[]{:S(2)}, u32[]{:S(2)}) collective-permute-start(bf16[4,2,96,384]{3,2,1,0:T(8,128)(2,1)} %get-tuple-element.182), channel_id=1, source_target_pairs={{0,2},{1,3},{2,0},{3,1},{4,6},{5,7},{6,4},{7,5},{8,10},{9,11},{10,... | collective-permute-start | bytes 1769480 | tf_op jit(solution)/shard_map/ppermute | solution.py:59
  194.3 8.8 %collective-permute-start.28 = (bf16[4,96,384]{2,1,0:T(8,128)(2,1)}, bf16[4,96,384]{2,1,0:T(8,128)(2,1)}, u32[]{:S(2)}, u32[]{:S(2)}) collective-permute-start(bf16[4,96,384]{2,1,0:T(8,128)(2,1)} %get-tuple-element.191), channel_id=1, source_target_pairs={{0,2},{1,3},{2,0},{3,1},{4,6},{5,7},{6,4},{7,5},{8,10},{9,11},{10,... | collective-permute-start | bytes 884744 | tf_op jit(solution)/shard_map/ppermute | solution.py:59
  195.4 8.5 %collective-permute-start.29 = (bf16[4,96,384]{2,1,0:T(8,128)(2,1)}, bf16[4,96,384]{2,1,0:T(8,128)(2,1)}, u32[]{:S(2)}, u32[]{:S(2)}) collective-permute-start(bf16[4,96,384]{2,1,0:T(8,128)(2,1)} %get-tuple-element.193), channel_id=1, source_target_pairs={{0,1},{1,0},{2,3},{3,2},{4,5},{5,4},{6,7},{7,6},{8,9},{9,8},{10,11... | collective-permute-start | bytes 884744 | tf_op jit(solution)/shard_map/ppermute | solution.py:59
  202.8 11.0 %collective-permute-start.30 = (bf16[768,1536]{1,0:T(8,128)(2,1)}, bf16[768,1536]{1,0:T(8,128)(2,1)}, u32[]{:S(2)}, u32[]{:S(2)}) collective-permute-start(bf16[768,1536]{1,0:T(8,128)(2,1)} %get-tuple-element.198), channel_id=1, source_target_pairs={{0,16},{16,0},{1,17},{17,1},{2,18},{18,2},{3,19},{19,3},{4,20},{20... | collective-permute-start | bytes 7077896 | tf_op jit(solution)/shard_map/ppermute | solution.py:59
  207.0 6.8 %collective-permute-start.31 = (bf16[768,384]{1,0:T(8,128)(2,1)}, bf16[768,384]{1,0:T(8,128)(2,1)}, u32[]{:S(2)}, u32[]{:S(2)}) collective-permute-start(bf16[768,384]{1,0:T(8,128)(2,1)} %get-tuple-element.209), channel_id=1, source_target_pairs={{0,16},{16,0},{1,17},{17,1},{2,18},{18,2},{3,19},{19,3},{4,20},{20... | collective-permute-start | bytes 1769480 | tf_op jit(solution)/shard_map/ppermute | solution.py:59
  209.4 41.5 %collective-permute-start.34 = (bf16[1,96,768]{2,1,0:T(8,128)(2,1)}, bf16[1,96,768]{2,1,0:T(8,128)(2,1)}, u32[]{:S(2)}, u32[]{:S(2)}) collective-permute-start(bf16[1,96,768]{2,1,0:T(8,128)(2,1)} %get-tuple-element.204), channel_id=1, source_target_pairs={{0,4},{1,5},{2,6},{3,7},{4,0},{5,1},{6,2},{7,3},{8,12},{9,13},{10,... | collective-permute-start | bytes 442376 | tf_op jit(solution)/shard_map/ppermute | solution.py:59
  210.6 40.3 %collective-permute-start.35 = (bf16[1,96,768]{2,1,0:T(8,128)(2,1)}, bf16[1,96,768]{2,1,0:T(8,128)(2,1)}, u32[]{:S(2)}, u32[]{:S(2)}) collective-permute-start(bf16[1,96,768]{2,1,0:T(8,128)(2,1)} %get-tuple-element.205), channel_id=1, source_target_pairs={{0,8},{1,9},{2,10},{3,11},{4,12},{5,13},{6,14},{7,15},{8,0},{9,1},... | collective-permute-start | bytes 442376 | tf_op jit(solution)/shard_map/ppermute | solution.py:59
  211.8 39.1 %collective-permute-start.36 = (bf16[1,96,768]{2,1,0:T(8,128)(2,1)}, bf16[1,96,768]{2,1,0:T(8,128)(2,1)}, u32[]{:S(2)}, u32[]{:S(2)}) collective-permute-start(bf16[1,96,768]{2,1,0:T(8,128)(2,1)} %get-tuple-element.206), channel_id=1, source_target_pairs={{0,12},{1,13},{2,14},{3,15},{4,8},{5,9},{6,10},{7,11},{8,4},{9,5},... | collective-permute-start | bytes 442376 | tf_op jit(solution)/shard_map/ppermute | solution.py:59
  218.2 30.3 %collective-permute-start.33 = (bf16[4,2,48,896]{3,2,1,0:T(8,128)(2,1)}, bf16[4,2,48,896]{3,2,1,0:T(8,128)(2,1)}, u32[]{:S(2)}, u32[]{:S(2)}) collective-permute-start(bf16[4,2,48,896]{3,2,1,0:T(8,128)(2,1)} %get-tuple-element.212), channel_id=1, source_target_pairs={{0,2},{1,3},{2,0},{3,1},{4,6},{5,7},{6,4},{7,5},{8,10},{9,11},{10,... | collective-permute-start | bytes 2064392 | tf_op jit(solution)/shard_map/ppermute | solution.py:59
  219.1 29.3 %collective-permute-start.32 = (bf16[4,2,48,1024]{3,2,1,0:T(8,128)(2,1)}, bf16[4,2,48,1024]{3,2,1,0:T(8,128)(2,1)}, u32[]{:S(2)}, u32[]{:S(2)}) collective-permute-start(bf16[4,2,48,1024]{3,2,1,0:T(8,128)(2,1)} %get-tuple-element.210), channel_id=1, source_target_pairs={{0,1},{1,0},{2,3},{3,2},{4,5},{5,4},{6,7},{7,6},{8,9},{9,8},{10,11... | collective-permute-start | bytes 2359304 | tf_op jit(solution)/shard_map/ppermute | solution.py:59
  222.6 19.7 %copy-start.14 = (bf16[768,1024]{1,0:T(8,128)(2,1)S(1)}, bf16[768,1024]{1,0:T(8,128)(2,1)}, u32[]{:S(2)}) copy-start(bf16[768,1024]{1,0:T(8,128)(2,1)} %get-tuple-element.171.left_ref) | copy-start | bytes 4718596
  248.4 14.5 %collective-permute-start.37 = (bf16[768,1152]{1,0:T(8,128)(2,1)}, bf16[768,1152]{1,0:T(8,128)(2,1)}, u32[]{:S(2)}, u32[]{:S(2)}) collective-permute-start(bf16[768,1152]{1,0:T(8,128)(2,1)} %get-tuple-element.217), channel_id=1, source_target_pairs={{0,16},{16,0},{1,17},{17,1},{2,18},{18,2},{3,19},{19,3},{4,20},{20... | collective-permute-start | bytes 5308424 | tf_op jit(solution)/shard_map/ppermute | solution.py:59
  260.5 2.5 collective-permute-start.38
  260.7 12.0 %collective-permute-start.39 = (bf16[4,48,1024]{2,1,0:T(8,128)(2,1)S(1)}, bf16[4,48,1024]{2,1,0:T(8,128)(2,1)S(1)}, u32[]{:S(2)}, u32[]{:S(2)}) collective-permute-start(bf16[4,48,1024]{2,1,0:T(8,128)(2,1)S(1)} %get-tuple-element.219), channel_id=1, source_target_pairs={{0,2},{1,3},{2,0},{3,1},{4,6},{5,7},{6,4},{7,5},{8,10},{9,11},{10,... | collective-permute-start | bytes 1179656 | tf_op jit(solution)/shard_map/ppermute | solution.py:59
  261.8 10.9 %collective-permute-start.40 = (bf16[4,48,896]{2,1,0:T(8,128)(2,1)S(1)}, bf16[4,48,896]{2,1,0:T(8,128)(2,1)S(1)}, u32[]{:S(2)}, u32[]{:S(2)}) collective-permute-start(bf16[4,48,896]{2,1,0:T(8,128)(2,1)S(1)} %get-tuple-element.221), channel_id=1, source_target_pairs={{0,1},{1,0},{2,3},{3,2},{4,5},{5,4},{6,7},{7,6},{8,9},{9,8},{10,11... | collective-permute-start | bytes 1032200 | tf_op jit(solution)/shard_map/ppermute | solution.py:59
  266.5 18.0 %collective-permute-start.41 = (bf16[4,2,48,768]{3,2,1,0:T(8,128)(2,1)}, bf16[4,2,48,768]{3,2,1,0:T(8,128)(2,1)}, u32[]{:S(2)}, u32[]{:S(2)}) collective-permute-start(bf16[4,2,48,768]{3,2,1,0:T(8,128)(2,1)} %get-tuple-element.233), channel_id=1, source_target_pairs={{0,1},{1,0},{2,3},{3,2},{4,5},{5,4},{6,7},{7,6},{8,9},{9,8},{10,11... | collective-permute-start | bytes 1769480 | tf_op jit(solution)/shard_map/ppermute | solution.py:59
  267.4 17.3 %collective-permute-start.42 = (bf16[4,2,48,768]{3,2,1,0:T(8,128)(2,1)}, bf16[4,2,48,768]{3,2,1,0:T(8,128)(2,1)}, u32[]{:S(2)}, u32[]{:S(2)}) collective-permute-start(bf16[4,2,48,768]{3,2,1,0:T(8,128)(2,1)} %get-tuple-element.235), channel_id=1, source_target_pairs={{0,2},{1,3},{2,0},{3,1},{4,6},{5,7},{6,4},{7,5},{8,10},{9,11},{10,... | collective-permute-start | bytes 1769480 | tf_op jit(solution)/shard_map/ppermute | solution.py:59
  273.4 15.7 %collective-permute-start.50 = (bf16[1,48,1920]{2,1,0:T(8,128)(2,1)S(1)}, bf16[1,48,1920]{2,1,0:T(8,128)(2,1)S(1)}, u32[]{:S(2)}, u32[]{:S(2)}) collective-permute-start(bf16[1,48,1920]{2,1,0:T(8,128)(2,1)S(1)} %get-tuple-element.241), channel_id=1, source_target_pairs={{0,12},{1,13},{2,14},{3,15},{4,8},{5,9},{6,10},{7,11},{8,4},{9,5},... | collective-permute-start | bytes 552968 | tf_op jit(solution)/shard_map/ppermute | solution.py:59
  275.3 15.2 %collective-permute-start.49 = (bf16[1,48,1920]{2,1,0:T(8,128)(2,1)S(1)}, bf16[1,48,1920]{2,1,0:T(8,128)(2,1)S(1)}, u32[]{:S(2)}, u32[]{:S(2)}) collective-permute-start(bf16[1,48,1920]{2,1,0:T(8,128)(2,1)S(1)} %get-tuple-element.240), channel_id=1, source_target_pairs={{0,8},{1,9},{2,10},{3,11},{4,12},{5,13},{6,14},{7,15},{8,0},{9,1},... | collective-permute-start | bytes 552968 | tf_op jit(solution)/shard_map/ppermute | solution.py:59
  275.3 15.2 %collective-permute-start.48 = (bf16[1,48,1920]{2,1,0:T(8,128)(2,1)S(1)}, bf16[1,48,1920]{2,1,0:T(8,128)(2,1)S(1)}, u32[]{:S(2)}, u32[]{:S(2)}) collective-permute-start(bf16[1,48,1920]{2,1,0:T(8,128)(2,1)S(1)} %get-tuple-element.239), channel_id=1, source_target_pairs={{0,4},{1,5},{2,6},{3,7},{4,0},{5,1},{6,2},{7,3},{8,12},{9,13},{10,... | collective-permute-start | bytes 552968 | tf_op jit(solution)/shard_map/ppermute | solution.py:59
  286.8 8.5 %collective-permute-start.43 = (bf16[4,48,768]{2,1,0:T(8,128)(2,1)S(1)}, bf16[4,48,768]{2,1,0:T(8,128)(2,1)S(1)}, u32[]{:S(2)}, u32[]{:S(2)}) collective-permute-start(bf16[4,48,768]{2,1,0:T(8,128)(2,1)S(1)} %get-tuple-element.245), channel_id=1, source_target_pairs={{0,2},{1,3},{2,0},{3,1},{4,6},{5,7},{6,4},{7,5},{8,10},{9,11},{10,... | collective-permute-start | bytes 884744 | tf_op jit(solution)/shard_map/ppermute | solution.py:59
  288.0 8.1 %collective-permute-start.44 = (bf16[4,48,768]{2,1,0:T(8,128)(2,1)S(1)}, bf16[4,48,768]{2,1,0:T(8,128)(2,1)S(1)}, u32[]{:S(2)}, u32[]{:S(2)}) collective-permute-start(bf16[4,48,768]{2,1,0:T(8,128)(2,1)S(1)} %get-tuple-element.246), channel_id=1, source_target_pairs={{0,1},{1,0},{2,3},{3,2},{4,5},{5,4},{6,7},{7,6},{8,9},{9,8},{10,11... | collective-permute-start | bytes 884744 | tf_op jit(solution)/shard_map/ppermute | solution.py:59
  296.9 13.1 %copy-start.5 = (f32[4,48,384]{2,1,0:T(8,128)S(1)}, f32[4,48,384]{2,1,0:T(8,128)}, u32[]{:S(2)}) copy-start(f32[4,48,384]{2,1,0:T(8,128)} %refs_1_.1) | copy-start | bytes 884740
  296.9 13.1 %copy-start.6 = (f32[4,48,384]{2,1,0:T(8,128)S(1)}, f32[4,48,384]{2,1,0:T(8,128)}, u32[]{:S(2)}) copy-start(f32[4,48,384]{2,1,0:T(8,128)} %refs_0_.1) | copy-start | bytes 884740
  296.9 13.1 %copy-start.7 = (f32[4,48,384]{2,1,0:T(8,128)S(1)}, f32[4,48,384]{2,1,0:T(8,128)}, u32[]{:S(2)}) copy-start(f32[4,48,384]{2,1,0:T(8,128)} %refs_2_.1) | copy-start | bytes 884740
  296.9 13.1 %copy-start.8 = (f32[256,48]{0,1:T(8,128)S(1)}, f32[256,48]{0,1:T(8,128)}, u32[]{:S(2)}) copy-start(f32[256,48]{0,1:T(8,128)} %param.37) | copy-start | bytes 147460
  297.0 13.1 %copy-start.9 = (f32[256,48]{0,1:T(8,128)S(1)}, f32[256,48]{0,1:T(8,128)}, u32[]{:S(2)}) copy-start(f32[256,48]{0,1:T(8,128)} %param.38) | copy-start | bytes 147460
  297.0 13.1 %copy-start.10 = (f32[256,48]{0,1:T(8,128)S(1)}, f32[256,48]{0,1:T(8,128)}, u32[]{:S(2)}) copy-start(f32[256,48]{0,1:T(8,128)} %param.39) | copy-start | bytes 147460
  297.0 13.1 %copy-start.11 = (f32[4,48]{1,0:T(4,128)S(1)}, f32[4,48]{1,0:T(4,128)}, u32[]{:S(2)}) copy-start(f32[4,48]{1,0:T(4,128)} %refs_4_.1) | copy-start | bytes 2308
  297.0 13.1 %copy-start.12 = (f32[4,48]{1,0:T(4,128)S(1)}, f32[4,48]{1,0:T(4,128)}, u32[]{:S(2)}) copy-start(f32[4,48]{1,0:T(4,128)} %refs_3_) | copy-start | bytes 2308
  297.0 13.1 %copy-start.13 = (f32[4,48]{1,0:T(4,128)S(1)}, f32[4,48]{1,0:T(4,128)}, u32[]{:S(2)}) copy-start(f32[4,48]{1,0:T(4,128)} %refs_5_) | copy-start | bytes 2308
  297.0 5.9 %collective-permute-start.45 = (bf16[1,48,1536]{2,1,0:T(8,128)(2,1)S(1)}, bf16[1,48,1536]{2,1,0:T(8,128)(2,1)S(1)}, u32[]{:S(2)}, u32[]{:S(2)}) collective-permute-start(bf16[1,48,1536]{2,1,0:T(8,128)(2,1)S(1)} %get-tuple-element.248), channel_id=1, source_target_pairs={{0,4},{1,5},{2,6},{3,7},{4,0},{5,1},{6,2},{7,3},{8,12},{9,13},{10,... | collective-permute-start | bytes 442376 | tf_op jit(solution)/shard_map/ppermute | solution.py:59
  297.4 12.7 %collective-permute-start.46 = (bf16[1,48,1536]{2,1,0:T(8,128)(2,1)S(1)}, bf16[1,48,1536]{2,1,0:T(8,128)(2,1)S(1)}, u32[]{:S(2)}, u32[]{:S(2)}) collective-permute-start(bf16[1,48,1536]{2,1,0:T(8,128)(2,1)S(1)} %get-tuple-element.249), channel_id=1, source_target_pairs={{0,8},{1,9},{2,10},{3,11},{4,12},{5,13},{6,14},{7,15},{8,0},{9,1},... | collective-permute-start | bytes 442376 | tf_op jit(solution)/shard_map/ppermute | solution.py:59
  299.4 10.6 %collective-permute-start.47 = (bf16[1,48,1536]{2,1,0:T(8,128)(2,1)S(1)}, bf16[1,48,1536]{2,1,0:T(8,128)(2,1)S(1)}, u32[]{:S(2)}, u32[]{:S(2)}) collective-permute-start(bf16[1,48,1536]{2,1,0:T(8,128)(2,1)S(1)} %get-tuple-element.250), channel_id=1, source_target_pairs={{0,12},{1,13},{2,14},{3,15},{4,8},{5,9},{6,10},{7,11},{8,4},{9,5},... | collective-permute-start | bytes 442376 | tf_op jit(solution)/shard_map/ppermute | solution.py:59
  (23 other events, 166.8 us)
Sparse Core Ops, SparseCore 0:
  28.6 83.7 all-gather.1

commit v3 on v2

--- a/solution.py
+++ b/solution.py
@@ -28,7 +28,7 @@
 LONG_COST = pl.CostEstimate(flops=10**12, bytes_accessed=10**9, transcendentals=0)
 ANYWHERE = pl.BlockSpec(memory_space=pl.ANY)
 HERE = pl.BlockSpec(memory_space=pltpu.VMEM)
-FORWARD_VMEM, BACKWARD_VMEM, PRODUCT_VMEM, OTHER_VMEM = 22, 20, 14, 20
+FORWARD_VMEM, BACKWARD_VMEM, PRODUCT_VMEM, OTHER_VMEM = 22, 17, 12, 20
 NN = (((1,), (0,)), ((), ()))
 NT = (((1,), (1,)), ((), ()))
 TN = (((0,), (0,)), ((), ()))
@@ -221,7 +221,7 @@
             num_scalar_prefetch=1, grid=(count,), in_specs=in_specs, out_specs=out_specs
         ),
         out_shape=outs,
-        compiler_params=pltpu.CompilerParams(vmem_limit_bytes=20 << 20),
+        compiler_params=pltpu.CompilerParams(vmem_limit_bytes=17 << 20),
         cost_estimate=LONG_COST if long else COST,
     )(at, *ins)
 
@@ -674,7 +674,7 @@
         stacked(token_count, 1),
         pltpu.VMEM((hidden, token_count), jnp.bfloat16),
         pltpu.VMEM((token_count, hidden), jnp.bfloat16),
-        far_off(token_count, width),
+        pltpu.VMEM((token_count, width), jnp.bfloat16),
         stacked(token_count, 1),
         far_off(token_count, width),
         stacked(slots, width),
@@ -770,10 +770,10 @@
 def loss_back(at, units, others, pooled, normed2, inverse2, vectors):
     token_count, width = normed2.shape
     half = functools.partial(stacked, dtype=jnp.bfloat16)
-    ins = [units, others, pooled, far_away(normed2), inverse2, vectors]
+    ins = [units, others, pooled, near_by(normed2), inverse2, vectors]
     outs = [
-        far_off(token_count, width, dtype=jnp.float32),
-        half(token_count, width),
+        pltpu.VMEM((token_count, width), jnp.float32),
+        pltpu.VMEM((token_count, width), jnp.bfloat16),
         stacked(3, width),
     ]
     return kernel_call(
@@ -785,6 +785,7 @@
         outs,
         tiles(*outs[:2]) + [whole_block(outs[2])],
         [pltpu.VMEM(pooled.shape, jnp.float32)],
+        vmem=12,
     )
 
 
@@ -834,7 +835,7 @@
         backward_kernel,
         (token_count // CHUNK,),
         at,
-        [far_away(dresid2), dresid2_half, near_by(slope), near_by(up), near_by(down), far_away(normed1), inverse1, vectors],
+        [near_by(dresid2), near_by(dresid2_half), near_by(slope), near_by(up), near_by(down), far_away(normed1), inverse1, vectors],
         tiles(dresid2, dresid2_half, slope) + [HERE, HERE] + tiles(normed1, inverse1)
         + [held(vectors)],
         outs,
@@ -942,8 +943,8 @@
         functools.partial(product_kernel, natural_order),
         (rows // tile,),
         at,
-        [near_by(left_array) if near == 0 else left_array, near_by(right_array) if near == 1 else right_array],
-        [pl.BlockSpec((tile, depth), lambda i, at: (i, 0)), HERE if near == 1 else held(right_array)],
+        [near_by(left_array) if near in (0, 2) else left_array, near_by(right_array) if near in (1, 2) else right_array],
+        [pl.BlockSpec((tile, depth), lambda i, at: (i, 0)), HERE if near in (1, 2) else held(right_array)],
         outs,
         [pl.BlockSpec((tile, columns), lambda i, at: (i, 0))] * 2,
         long=True,
@@ -1116,7 +1117,7 @@
     def blocks(values):
         return values.reshape(devices // 4, 2, 2, values.shape[0] // devices, values.shape[1])
 
-    down_own, down_away = product(at, active, dresid2_half, True, near=0)
+    down_own, down_away = product(at, active, dresid2_half, True, near=2)
     down_in = exchanged(down_away, "stream", 1)
     by_rows = down_weight.shape[0] % 32 == 0
     half_rows = down_weight.shape[0] // 2

time: 321 us -> 318 us (level)
  no operation moved by 1% of the time
where the time goes in v3:
time: 318 us; the launch traced here: 317 us
  Pallas kernels  149 us (47%)
  waiting for transfers between devices  75 us (24%)
  starting transfers between devices  54.6 us (17%)
  between operations  14.8 us (5%)
  local copies, waits for them, and re-layouts  11.4 us (4%)
  other arithmetic  10.4 us (3%)
    pallas_call x9, Pallas kernels, kernel_call(): pl.pallas_call(kernel, grid_spec=pltpu.PrefetchScalarGridSpec(num_scalar_...  80.8 us
    ppermute x51, waiting for transfers between devices, exchanged(): lax.ppermute(block, axis, [(place, place ^ mask) for place in range(count)])  74.2 us
    ppermute x51, starting transfers between devices, exchanged(): lax.ppermute(block, axis, [(place, place ^ mask) for place in range(count)])  54.5 us
    pallas_call x9, Pallas kernels, fold_call(): pl.pallas_call(kernel, grid_spec=pltpu.PrefetchScalarGridSpec(num_scalar_...  22 us
    pallas_call x1, Pallas kernels, attend_back(): pl.pallas_call(attend_back_kernel, grid_spec=pltpu.PrefetchScalarGridSpec...  19.7 us
    pallas_call x1, Pallas kernels, attend(): pl.pallas_call(attend_kernel, grid_spec=pltpu.PrefetchScalarGridSpec(num_...  19 us
  transfers between devices with their start and end apart: 52, of which 28 were waited for; matrix products, arithmetic and copies ran while one was open for 5% of the time, Pallas kernels for 33%

profile of v3, /device:TPU:0, one launch (start us, length us, event | category | flops | bytes accessed | tf_op | source)
XLA Modules:
  0.0 316.8 jit_solution(11402914185684349132)
XLA Ops:
  10.8 5.1 %collective-permute-start.2 = (bf16[1,48,1536]{2,1,0:T(8,128)(2,1)S(1)}, bf16[1,48,1536]{2,1,0:T(8,128)(2,1)S(1)}, u32[]{:S(2)}, u32[]{:S(2)}) collective-permute-start(bf16[1,48,1536]{2,1,0:T(8,128)(2,1)S(1)} %constant_dynamic-update-slice_fusion), channel_id=1, source_target_pairs={{0,12},{1,13},{2,14},{3,15},{4,8},{5,9},{6,10},{7,11},{8,4},{9,5},... | collective-permute-start | bytes 442376 | tf_op jit(solution)/shard_map/ppermute | solution.py:59
  16.5 1.6 convert_element_type.39
  18.2 2.5 collective-permute-done.2
  20.7 7.7 %collective-permute-done.1 = bf16[1,48,1536]{2,1,0:T(8,128)(2,1)S(1)} collective-permute-done((bf16[1,48,1536]{2,1,0:T(8,128)(2,1)S(1)}, bf16[1,48,1536]{2,1,0:T(8,128)(2,1)S(1)}, u32[]{:S(2)}, u32[]{:S(2)}) %collective-permute-start.1) | collective-permute-done | bytes 147488 | tf_op jit(solution)/shard_map/ppermute | solution.py:59
  28.6 1.6 collective-permute-start.4
  30.2 1.5 collective-permute-start.3
  31.7 5.0 %collective-permute-done.4 = bf16[4,48,768]{2,1,0:T(8,128)(2,1)S(1)} collective-permute-done((bf16[4,48,768]{2,1,0:T(8,128)(2,1)S(1)}, bf16[4,48,768]{2,1,0:T(8,128)(2,1)S(1)}, u32[]{:S(2)}, u32[]{:S(2)}) %collective-permute-start.4) | collective-permute-done | bytes 294944 | tf_op jit(solution)/shard_map/ppermute | solution.py:59
  36.8 1.2 collective-permute-done.3
  38.0 2.4 collective-permute-start.7
  40.4 2.1 collective-permute-start.5
  42.5 1.5 collective-permute-start.9
  44.5 3.9 %collective-permute-done.7 = bf16[1,48,2048]{2,1,0:T(8,128)(2,1)S(1)} collective-permute-done((bf16[1,48,2048]{2,1,0:T(8,128)(2,1)S(1)}, bf16[1,48,2048]{2,1,0:T(8,128)(2,1)S(1)}, u32[]{:S(2)}, u32[]{:S(2)}) %collective-permute-start.7) | collective-permute-done | bytes 196640 | tf_op jit(solution)/shard_map/ppermute | solution.py:59
  48.4 9.9 %collective-permute-done.6 = bf16[1,48,2048]{2,1,0:T(8,128)(2,1)S(1)} collective-permute-done((bf16[1,48,2048]{2,1,0:T(8,128)(2,1)S(1)}, bf16[1,48,2048]{2,1,0:T(8,128)(2,1)S(1)}, u32[]{:S(2)}, u32[]{:S(2)}) %collective-permute-start.6) | collective-permute-done | bytes 196640 | tf_op jit(solution)/shard_map/ppermute | solution.py:59
  60.9 1.5 collective-permute-start.12
  63.7 1.7 shard_map.395
  65.4 8.4 %shard_map.396 = (f32[1024,768]{1,0:T(8,128)}, bf16[768,1024]{1,0:T(8,128)(2,1)}, bf16[2,1024,1152]{2,1,0:T(8,128)(2,1)}, f32[8,768]{1,0:T(8,128)S(1)}, f32[4,768]{1,0:T(4,128)S(1)}) custom-call(s32[13]{0:T(128)S(1)} %concatenate.66.at_ref.at, bf16[1024,768]{1,0:T(8,128)(2,1)} %bitcast.100, bf16[768,512]{1,0:T(8,128)(2,1)S(1)} %bitcast.80, ...), custom_call_target="tpu_custom_call" | custom-call | flops 1000 | bytes 1000 | tf_op jit(solution)/shard_map/pallas_call | solution.py:512
  76.8 1.6 collective-permute-start.15
  81.2 19.0 %shard_map.397 = (bf16[1024,768]{1,0:T(8,128)(2,1)}, bf16[768,1024]{1,0:T(8,128)(2,1)}, bf16[6,2,2,512,512]{4,3,2,1,0:T(8,128)(2,1)}) custom-call(s32[13]{0:T(128)S(1)} %concatenate.66.at_ref.at, bf16[2,1024,1152]{2,1,0:T(8,128)(2,1)} %get-tuple-element.156.q_ref.k_ref.v_ref, bf16[2,1024,1152]{2,1,0:T(8,128)(2,1)} %get-tuple-element.156.q_ref.k_ref.v_ref, ...), custom_call_target="tpu_custom_call" | custom-call | flops 1000 | bytes 1000 | tf_op jit(solution)/shard_map/pallas_call | solution.py:396
  100.3 3.9 %collective-permute-done.15 = bf16[8,48,1024]{2,1,0:T(8,128)(2,1)S(1)} collective-permute-done((bf16[8,48,1024]{2,1,0:T(8,128)(2,1)S(1)}, bf16[8,48,1024]{2,1,0:T(8,128)(2,1)S(1)}, u32[]{:S(2)}, u32[]{:S(2)}) %collective-permute-start.15) | collective-permute-done | bytes 786464 | tf_op jit(solution)/shard_map/ppermute | solution.py:59
  104.3 3.3 %collective-permute-done.14 = bf16[8,48,1024]{2,1,0:T(8,128)(2,1)S(1)} collective-permute-done((bf16[8,48,1024]{2,1,0:T(8,128)(2,1)S(1)}, bf16[8,48,1024]{2,1,0:T(8,128)(2,1)S(1)}, u32[]{:S(2)}, u32[]{:S(2)}) %collective-permute-start.14) | collective-permute-done | bytes 786464 | tf_op jit(solution)/shard_map/ppermute | solution.py:59
  107.8 1.2 copy.58
  108.9 1.6 reshape.201
  112.4 4.6 %shard_map.398 = (bf16[2,16,48,1536]{3,2,1,0:T(8,128)(2,1)S(1)}, bf16[16,48,768]{2,1,0:T(8,128)(2,1)S(1)}, bf16[3072,768]{1,0:T(8,128)(2,1)S(1)}) custom-call(s32[13]{0:T(128)S(1)} %concatenate.66.at_ref.at, bf16[16,48,1024]{2,1,0:T(8,128)(2,1)S(1)} %constant_dynamic-update-slice_fusion.13.refs_0_, ...), custom_call_target="tpu_custom_call" | custom-call | flops 1000 | bytes 1000 | tf_op jit(solution)/shard_map/pallas_call | solution.py:166
  117.0 21.9 %shard_map.399 = (bf16[768,1024]{1,0:T(8,128)(2,1)}, bf16[1024,768]{1,0:T(8,128)(2,1)}, f32[1024,1]{1,0:T(8,128)S(1)}, bf16[3072,1024]{1,0:T(8,128)(2,1)S(1)}, b...) custom-call(s32[13]{0:T(128)S(1)} %concatenate.66.at_ref.at, ...), custom_call_target="tpu_custom_call" | custom-call | flops 1000 | bytes 1000 | tf_op jit(solution)/shard_map/pallas_call | solution.py:512
  140.9 1.6 collective-permute-start.18
  142.5 1.1 collective-permute-done.20
  144.6 1.6 collective-permute-start.23
  147.2 1.9 collective-permute-start.21
  149.1 2.3 collective-permute-done.21
  152.3 1.5 collective-permute-done.24.others
  153.8 3.7 %shard_map.400 = (f32[1024,768]{1,0:T(8,128)S(1)}, bf16[1024,768]{1,0:T(8,128)(2,1)S(1)}, f32[3,768]{1,0:T(4,128)S(1)}) custom-call(s32[13]{0:T(128)S(1)} %concatenate.66.at_ref.at, bf16[128,896]{1,0:T(8,128)(2,1)S(1)} %bitcast.85, bf16[128,896]{1,0:T(8,128)(2,1)S(1)} %collective-permute-done.24.others, f32[8,768]{1,0:T(8,128)S(1)} %get-tuple-element.174.pooled, ...), custom_call_target="tpu_custom_call" | custom-call | flops 1000 | bytes 1000 | tf_op jit(solution)/shard_map/pallas_call | solution.py:512
  157.6 6.8 %shard_map.401 = (bf16[3072,384]{1,0:T(8,128)(2,1)S(1)}, bf16[3072,384]{1,0:T(8,128)(2,1)S(1)}) custom-call(s32[13]{0:T(128)S(1)} %concatenate.66.at_ref.at, bf16[3072,1024]{1,0:T(8,128)(2,1)S(1)} %get-tuple-element.172.left_ref, bf16[1024,768]{1,0:T(8,128)(2,1)S(1)} %get-tuple-element.177.right_ref.dresid2_half), custom_call_target="tpu_custom_call" | custom-call | flops 999999995904 | bytes 1000000000 | tf_op jit(solution)/shard_map/pallas_call | solution.py:512
  164.6 4.4 %collective-permute-done.25 = bf16[3072,384]{1,0:T(8,128)(2,1)S(1)} collective-permute-done((bf16[3072,384]{1,0:T(8,128)(2,1)S(1)}, bf16[3072,384]{1,0:T(8,128)(2,1)S(1)}, u32[]{:S(2)}, u32[]{:S(2)}) %collective-permute-start.25) | collective-permute-done | bytes 2359328 | tf_op jit(solution)/shard_map/ppermute | solution.py:59
  169.0 2.5 shard_map.402
  171.4 1.5 collective-permute-start.26
  173.9 14.4 %shard_map.403 = (bf16[1024,3072]{1,0:T(8,128)(2,1)S(1)}, f32[1,3072]{1,0:T(1,128)S(1)}, f32[1024,768]{1,0:T(8,128)}, bf16[1024,768]{1,0:T(8,128)(2,1)S(1)}, f32[3,768]{1,0:T(4,128)S(1)}) custom-call(s32[13]{0:T(128)S(1)} %concatenate.66.at_ref.at, f32[1024,768]{1,0:T(8,128)S(1)} %get-tuple-element.185.dresid2, ...), custom_call_target="tpu_custom_call" | custom-call | flops 999999995904 | bytes 1000000000 | tf_op jit(solution)/shard_map/pallas_call | solution.py:512
  188.3 3.3 %shard_map.404 = (bf16[4,96,384]{2,1,0:T(8,128)(2,1)}, f32[4,96,384]{2,1,0:T(8,128)S(1)}, bf16[4,96,384]{2,1,0:T(8,128)(2,1)}, f32[4,96,384]{2,1,0:T(8,128)S(1)}) custom-call(s32[13]{0:T(128)S(1)} %concatenate.66.at_ref.at, f32[4,2,96,384]{3,2,1,0:T(8,128)S(1)} %get-tuple-element.181.refs_0_, bf16[4,2,96,384]{3,2,1,0:T(8,128)(2,1)} %collective-permute-done.26.refs_1_, ...), custom_call_target="tpu_custom_call" | custom-call | flops 1000 | bytes 1000 | tf_op jit(solution)/shard_map/pallas_call | solution.py:218
  193.2 6.9 %shard_map.405 = (bf16[768,1536]{1,0:T(8,128)(2,1)S(1)}, bf16[768,1536]{1,0:T(8,128)(2,1)}) custom-call(s32[13]{0:T(128)S(1)} %concatenate.66.at_ref.at, bf16[768,1024]{1,0:T(8,128)(2,1)S(1)} %copy-done.16, bf16[1024,3072]{1,0:T(8,128)(2,1)S(1)} %get-tuple-element.197.right_ref), custom_call_target="tpu_custom_call" | custom-call | flops 999999995904 | bytes 1000000000 | tf_op jit(solution)/shard_map/pallas_call | solution.py:512
  201.2 3.1 shard_map.406
  204.3 2.4 shard_map.407
  206.7 1.2 collective-permute-start.34
  207.9 1.2 collective-permute-start.35
  209.0 2.1 collective-permute-start.36
  211.1 4.3 %shard_map.408 = (bf16[4,2,48,1024]{3,2,1,0:T(8,128)(2,1)}, f32[4,2,48,1024]{3,2,1,0:T(8,128)S(1)}, bf16[4,2,48,896]{3,2,1,0:T(8,128)(2,1)}, f32[4,2,48,896]{3,2,1,0:T(8,128)S(1)}) custom-call(s32[13]{0:T(128)S(1)} %concatenate.66.at_ref.at, bf16[4,2,2,48,1536]{4,3,2,1,0:T(8,128)(2,1)S(1)} %bitcast.60, ...), custom_call_target="tpu_custom_call" | custom-call | flops 1000 | bytes 1000 | tf_op jit(solution)/shard_map/pallas_call | solution.py:218
  217.3 1.4 convolution_convert_fusion.grad_ref
  218.8 1.2 slice-done.2
  220.0 19.7 %shard_map.409 = (bf16[2,1024,1152]{2,1,0:T(8,128)(2,1)S(1)}, f32[2,2,1,384]{3,2,1,0:T(1,128)S(1)}) custom-call(s32[13]{0:T(128)S(1)} %concatenate.66.at_ref.at, bf16[2,1024,1152]{2,1,0:T(8,128)(2,1)} %get-tuple-element.156.q_ref.k_ref.v_ref, bf16[2,1024,1152]{2,1,0:T(8,128)(2,1)} %get-tuple-element.156.q_ref.k_ref.v_ref, ...), custom_call_target="tpu_custom_call" | custom-call | flops 999999995904 | bytes 1000000000 | tf_op jit(solution)/shard_map/pallas_call | solution.py:470
  239.7 6.0 %shard_map.410 = (bf16[768,1152]{1,0:T(8,128)(2,1)S(1)}, bf16[768,1152]{1,0:T(8,128)(2,1)}) custom-call(s32[13]{0:T(128)S(1)} %concatenate.66.at_ref.at, bf16[768,1024]{1,0:T(8,128)(2,1)S(1)} %copy-done.14, bf16[2,1024,1152]{2,1,0:T(8,128)(2,1)S(1)} %get-tuple-element.216.right_ref.dtriples), custom_call_target="tpu_custom_call" | custom-call | flops 999999995904 | bytes 1000000000 | tf_op jit(solution)/shard_map/pallas_call | solution.py:512
  245.8 2.4 shard_map.411
  248.3 9.5 %shard_map.412 = (f32[1024,768]{1,0:T(8,128)}, f32[768,384]{1,0:T(8,128)S(1)}, bf16[768,384]{1,0:T(8,128)(2,1)S(1)}) custom-call(s32[13]{0:T(128)S(1)} %concatenate.66.at_ref.at, f32[1024,768]{1,0:T(8,128)} %get-tuple-element.224.dresid1, bf16[2,1024,1152]{2,1,0:T(8,128)(2,1)S(1)} %get-tuple-element.216.right_ref.dtriples, ...), custom_call_target="tpu_custom_call" | custom-call | flops 999999995904 | bytes 1000000000 | tf_op jit(solution)/shard_map/pallas_call | solution.py:512
  260.2 3.6 %shard_map.413 = (bf16[4,2,48,768]{3,2,1,0:T(8,128)(2,1)}, f32[4,2,48,768]{3,2,1,0:T(8,128)S(1)}, bf16[4,2,48,768]{3,2,1,0:T(8,128)(2,1)}, f32[4,2,48,768]{3,2,1,0:T(8,128)S(1)}) custom-call(s32[13]{0:T(128)S(1)} %concatenate.66.at_ref.at, bf16[4,2,2,48,1152]{4,3,2,1,0:T(8,128)(2,1)S(1)} %bitcast.63, ...), custom_call_target="tpu_custom_call" | custom-call | flops 1000 | bytes 1000 | tf_op jit(solution)/shard_map/pallas_call | solution.py:218
  265.7 4.4 %collective-permute-done.40.in1 = bf16[4,48,896]{2,1,0:T(8,128)(2,1)S(1)} collective-permute-done((bf16[4,48,896]{2,1,0:T(8,128)(2,1)S(1)}, bf16[4,48,896]{2,1,0:T(8,128)(2,1)S(1)}, u32[]{:S(2)}, u32[]{:S(2)}) %collective-permute-start.40) | collective-permute-done | bytes 344096 | tf_op jit(solution)/shard_map/ppermute | solution.py:59
  270.7 1.8 collective-permute-start.50
  272.6 2.6 collective-permute-start.48
  275.2 6.6 %collective-permute-done.41.refs_1_ = bf16[4,2,48,768]{3,2,1,0:T(8,128)(2,1)} collective-permute-done((bf16[4,2,48,768]{3,2,1,0:T(8,128)(2,1)}, bf16[4,2,48,768]{3,2,1,0:T(8,128)(2,1)}, u32[]{:S(2)}, u32[]{:S(2)}) %collective-permute-start.41) | collective-permute-done | bytes 589856 | tf_op jit(solution)/shard_map/ppermute | solution.py:59
  282.1 2.1 shard_map.415
  284.2 1.1 collective-permute-start.43
  286.4 1.4 collective-permute-done.49
  290.9 1.8 collective-permute-done.43.in0
  294.6 2.1 collective-permute-start.46
  296.7 2.0 collective-permute-start.47
  300.2 7.1 %collective-permute-done.46 = bf16[1,48,1536]{2,1,0:T(8,128)(2,1)S(1)} collective-permute-done((bf16[1,48,1536]{2,1,0:T(8,128)(2,1)S(1)}, bf16[1,48,1536]{2,1,0:T(8,128)(2,1)S(1)}, u32[]{:S(2)}, u32[]{:S(2)}) %collective-permute-start.46) | collective-permute-done | bytes 147488 | tf_op jit(solution)/shard_map/ppermute | solution.py:59
  307.4 1.3 shard_map.417
  308.8 1.2 add_multiply_fusion.2
  (194 shorter events, 40.3 us)
Async XLA Ops:
  7.2 21.3 %copy-start.21 = (f32[48,1536]{1,0:T(8,128)S(1)}, f32[48,1536]{1,0:T(8,128)}, u32[]{:S(2)}) copy-start(f32[48,1536]{1,0:T(8,128)} %param.25) | copy-start | bytes 884740
  7.2 105.2 %all-gather.2.cloned.1.call-start = ((), (), s32[]{:S(2)}) async-start(), calls=%async_computation | async-start | bytes 4866048 | tf_op jit(solution)/shard_map/all_gather | solution.py:1052
  10.8 9.9 %collective-permute-start.2 = (bf16[1,48,1536]{2,1,0:T(8,128)(2,1)S(1)}, bf16[1,48,1536]{2,1,0:T(8,128)(2,1)S(1)}, u32[]{:S(2)}, u32[]{:S(2)}) collective-permute-start(bf16[1,48,1536]{2,1,0:T(8,128)(2,1)S(1)} %constant_dynamic-update-slice_fusion), channel_id=1, source_target_pairs={{0,12},{1,13},{2,14},{3,15},{4,8},{5,9},{6,10},{7,11},{8,4},{9,5},... | collective-permute-start | bytes 442376 | tf_op jit(solution)/shard_map/ppermute | solution.py:59
  15.9 12.5 %collective-permute-start.1 = (bf16[1,48,1536]{2,1,0:T(8,128)(2,1)S(1)}, bf16[1,48,1536]{2,1,0:T(8,128)(2,1)S(1)}, u32[]{:S(2)}, u32[]{:S(2)}) collective-permute-start(bf16[1,48,1536]{2,1,0:T(8,128)(2,1)S(1)} %constant_dynamic-update-slice_fusion), channel_id=1, source_target_pairs={{0,8},{1,9},{2,10},{3,11},{4,12},{5,13},{6,14},{7,15},{8,0},{9,1},... | collective-permute-start | bytes 442376 | tf_op jit(solution)/shard_map/ppermute | solution.py:59
  15.9 12.5 %collective-permute-start = (bf16[1,48,1536]{2,1,0:T(8,128)(2,1)S(1)}, bf16[1,48,1536]{2,1,0:T(8,128)(2,1)S(1)}, u32[]{:S(2)}, u32[]{:S(2)}) collective-permute-start(bf16[1,48,1536]{2,1,0:T(8,128)(2,1)S(1)} %constant_dynamic-update-slice_fusion), channel_id=1, source_target_pairs={{0,4},{1,5},{2,6},{3,7},{4,0},{5,1},{6,2},{7,3},{8,12},{9,13},{10,... | collective-permute-start | bytes 442376 | tf_op jit(solution)/shard_map/ppermute | solution.py:59
  28.6 8.1 %collective-permute-start.4 = (bf16[4,48,768]{2,1,0:T(8,128)(2,1)S(1)}, bf16[4,48,768]{2,1,0:T(8,128)(2,1)S(1)}, u32[]{:S(2)}, u32[]{:S(2)}) collective-permute-start(bf16[4,48,768]{2,1,0:T(8,128)(2,1)S(1)} %get-tuple-element.285), channel_id=1, source_target_pairs={{0,1},{1,0},{2,3},{3,2},{4,5},{5,4},{6,7},{7,6},{8,9},{9,8},{10,11... | collective-permute-start | bytes 884744 | tf_op jit(solution)/shard_map/ppermute | solution.py:59
  30.2 7.8 %collective-permute-start.3 = (bf16[4,48,768]{2,1,0:T(8,128)(2,1)S(1)}, bf16[4,48,768]{2,1,0:T(8,128)(2,1)S(1)}, u32[]{:S(2)}, u32[]{:S(2)}) collective-permute-start(bf16[4,48,768]{2,1,0:T(8,128)(2,1)S(1)} %get-tuple-element.286), channel_id=1, source_target_pairs={{0,2},{1,3},{2,0},{3,1},{4,6},{5,7},{6,4},{7,5},{8,10},{9,11},{10,... | collective-permute-start | bytes 884744 | tf_op jit(solution)/shard_map/ppermute | solution.py:59
  38.0 10.4 %collective-permute-start.7 = (bf16[1,48,2048]{2,1,0:T(8,128)(2,1)S(1)}, bf16[1,48,2048]{2,1,0:T(8,128)(2,1)S(1)}, u32[]{:S(2)}, u32[]{:S(2)}) collective-permute-start(bf16[1,48,2048]{2,1,0:T(8,128)(2,1)S(1)} %bitcast.101), channel_id=1, source_target_pairs={{0,12},{1,13},{2,14},{3,15},{4,8},{5,9},{6,10},{7,11},{8,4},{9,5},... | collective-permute-start | bytes 589832 | tf_op jit(solution)/shard_map/ppermute | solution.py:59
  40.4 17.9 %collective-permute-start.6 = (bf16[1,48,2048]{2,1,0:T(8,128)(2,1)S(1)}, bf16[1,48,2048]{2,1,0:T(8,128)(2,1)S(1)}, u32[]{:S(2)}, u32[]{:S(2)}) collective-permute-start(bf16[1,48,2048]{2,1,0:T(8,128)(2,1)S(1)} %bitcast.102), channel_id=1, source_target_pairs={{0,8},{1,9},{2,10},{3,11},{4,12},{5,13},{6,14},{7,15},{8,0},{9,1},... | collective-permute-start | bytes 589832 | tf_op jit(solution)/shard_map/ppermute | solution.py:59
  40.4 17.9 %collective-permute-start.5 = (bf16[1,48,2048]{2,1,0:T(8,128)(2,1)S(1)}, bf16[1,48,2048]{2,1,0:T(8,128)(2,1)S(1)}, u32[]{:S(2)}, u32[]{:S(2)}) collective-permute-start(bf16[1,48,2048]{2,1,0:T(8,128)(2,1)S(1)} %bitcast.103), channel_id=1, source_target_pairs={{0,4},{1,5},{2,6},{3,7},{4,0},{5,1},{6,2},{7,3},{8,12},{9,13},{10,... | collective-permute-start | bytes 589832 | tf_op jit(solution)/shard_map/ppermute | solution.py:59
  42.5 16.1 %collective-permute-start.9 = (bf16[8,48,768]{2,1,0:T(8,128)(2,1)S(1)}, bf16[8,48,768]{2,1,0:T(8,128)(2,1)S(1)}, u32[]{:S(2)}, u32[]{:S(2)}) collective-permute-start(bf16[8,48,768]{2,1,0:T(8,128)(2,1)S(1)} %pad_maximum_fusion.3), channel_id=1, source_target_pairs={{0,2},{1,3},{2,0},{3,1},{4,6},{5,7},{6,4},{7,5},{8,10},{9,11},{10,... | collective-permute-start | bytes 1769480 | tf_op jit(solution)/shard_map/ppermute | solution.py:59
  44.0 14.7 %collective-permute-start.8 = (bf16[8,48,768]{2,1,0:T(8,128)(2,1)S(1)}, bf16[8,48,768]{2,1,0:T(8,128)(2,1)S(1)}, u32[]{:S(2)}, u32[]{:S(2)}) collective-permute-start(bf16[8,48,768]{2,1,0:T(8,128)(2,1)S(1)} %pad_maximum_fusion.2), channel_id=1, source_target_pairs={{0,1},{1,0},{2,3},{3,2},{4,5},{5,4},{6,7},{7,6},{8,9},{9,8},{10,11... | collective-permute-start | bytes 1769480 | tf_op jit(solution)/shard_map/ppermute | solution.py:59
  58.6 5.2 %collective-permute-start.11 = (bf16[16,48,768]{2,1,0:T(8,128)(2,1)S(1)}, bf16[16,48,768]{2,1,0:T(8,128)(2,1)S(1)}, u32[]{:S(2)}, u32[]{:S(2)}) collective-permute-start(bf16[16,48,768]{2,1,0:T(8,128)(2,1)S(1)} %constant_dynamic-update-slice_fusion.7.refs_1_), channel_id=1, source_target_pairs={{0,16},{16,0},{1,17},{17,1},{2,18},{18,2},{3,19},{19,3},{4,20},{20... | collective-permute-start | bytes 3538952 | tf_op jit(solution)/shard_map/ppermute | solution.py:59
  58.7 5.0 %collective-permute-start.10 = (bf16[16,48,768]{2,1,0:T(8,128)(2,1)S(1)}, bf16[16,48,768]{2,1,0:T(8,128)(2,1)}, u32[]{:S(2)}, u32[]{:S(2)}) collective-permute-start(bf16[16,48,768]{2,1,0:T(8,128)(2,1)S(1)} %constant_dynamic-update-slice_fusion.5.refs_0_), channel_id=1, source_target_pairs={{0,16},{16,0},{1,17},{17,1},{2,18},{18,2},{3,19},{19,3},{4,20},{20... | collective-permute-start | bytes 3538952 | tf_op jit(solution)/shard_map/ppermute | solution.py:59
  60.2 15.6 %collective-permute-start.13 = (bf16[4,48,1024]{2,1,0:T(8,128)(2,1)}, bf16[4,48,1024]{2,1,0:T(8,128)(2,1)}, u32[]{:S(2)}, u32[]{:S(2)}) collective-permute-start(bf16[4,48,1024]{2,1,0:T(8,128)(2,1)} %get-tuple-element.158), channel_id=1, source_target_pairs={{0,1},{1,0},{2,3},{3,2},{4,5},{5,4},{6,7},{7,6},{8,9},{9,8},{10,11... | collective-permute-start | bytes 1179656 | tf_op jit(solution)/shard_map/ppermute | solution.py:59
  60.9 18.6 %collective-permute-start.12 = (bf16[4,48,1024]{2,1,0:T(8,128)(2,1)}, bf16[4,48,1024]{2,1,0:T(8,128)(2,1)}, u32[]{:S(2)}, u32[]{:S(2)}) collective-permute-start(bf16[4,48,1024]{2,1,0:T(8,128)(2,1)} %get-tuple-element.157), channel_id=1, source_target_pairs={{0,2},{1,3},{2,0},{3,1},{4,6},{5,7},{6,4},{7,5},{8,10},{9,11},{10,... | collective-permute-start | bytes 1179656 | tf_op jit(solution)/shard_map/ppermute | solution.py:59
  76.8 27.4 %collective-permute-start.15 = (bf16[8,48,1024]{2,1,0:T(8,128)(2,1)S(1)}, bf16[8,48,1024]{2,1,0:T(8,128)(2,1)S(1)}, u32[]{:S(2)}, u32[]{:S(2)}) collective-permute-start(bf16[8,48,1024]{2,1,0:T(8,128)(2,1)S(1)} %constant_dynamic-update-slice_fusion.11), channel_id=1, source_target_pairs={{0,2},{1,3},{2,0},{3,1},{4,6},{5,7},{6,4},{7,5},{8,10},{9,11},{10,... | collective-permute-start | bytes 2359304 | tf_op jit(solution)/shard_map/ppermute | solution.py:59
  80.5 27.1 %collective-permute-start.14 = (bf16[8,48,1024]{2,1,0:T(8,128)(2,1)S(1)}, bf16[8,48,1024]{2,1,0:T(8,128)(2,1)S(1)}, u32[]{:S(2)}, u32[]{:S(2)}) collective-permute-start(bf16[8,48,1024]{2,1,0:T(8,128)(2,1)S(1)} %constant_dynamic-update-slice_fusion.9), channel_id=1, source_target_pairs={{0,1},{1,0},{2,3},{3,2},{4,5},{5,4},{6,7},{7,6},{8,9},{9,8},{10,11... | collective-permute-start | bytes 2359304 | tf_op jit(solution)/shard_map/ppermute | solution.py:59
  104.2 6.3 %collective-permute-start.17 = (bf16[16,48,1024]{2,1,0:T(8,128)(2,1)S(1)}, bf16[16,48,1024]{2,1,0:T(8,128)(2,1)}, u32[]{:S(2)}, u32[]{:S(2)}) collective-permute-start(bf16[16,48,1024]{2,1,0:T(8,128)(2,1)S(1)} %constant_dynamic-update-slice_fusion.15.refs_1_), channel_id=1, source_target_pairs={{0,16},{16,0},{1,17},{17,1},{2,18},{18,2},{3,19},{19,3},{4,20},{20... | collective-permute-start | bytes 4718600 | tf_op jit(solution)/shard_map/ppermute | solution.py:59
  107.7 4.0 %collective-permute-start.16 = (bf16[16,48,1024]{2,1,0:T(8,128)(2,1)S(1)}, bf16[16,48,1024]{2,1,0:T(8,128)(2,1)}, u32[]{:S(2)}, u32[]{:S(2)}) collective-permute-start(bf16[16,48,1024]{2,1,0:T(8,128)(2,1)S(1)} %constant_dynamic-update-slice_fusion.13.refs_0_), channel_id=1, source_target_pairs={{0,16},{16,0},{1,17},{17,1},{2,18},{18,2},{3,19},{19,3},{4,20},{20... | collective-permute-start | bytes 4718600 | tf_op jit(solution)/shard_map/ppermute | solution.py:59
  117.0 21.9 %copy-start.3 = (bf16[16,48,768]{2,1,0:T(8,128)(2,1)}, bf16[16,48,768]{2,1,0:T(8,128)(2,1)S(1)}, u32[]{:S(2)}) copy-start(bf16[16,48,768]{2,1,0:T(8,128)(2,1)S(1)} %get-tuple-element.165) | copy-start | bytes 3538948
  138.9 18.6 %copy-start.17 = (f32[1024,1]{1,0:T(8,128)}, f32[1024,1]{1,0:T(8,128)S(1)}, u32[]{:S(2)}) copy-start(f32[1024,1]{1,0:T(8,128)S(1)} %get-tuple-element.188.inverse1) | copy-start | bytes 12292
  138.9 4.7 %collective-permute-start.20 = (bf16[1,8,896]{2,1,0:T(8,128)(2,1)S(1)}, bf16[1,8,896]{2,1,0:T(8,128)(2,1)S(1)}, u32[]{:S(2)}, u32[]{:S(2)}) collective-permute-start(bf16[1,8,896]{2,1,0:T(8,128)(2,1)S(1)} %bitcast.90), channel_id=1, source_target_pairs={{0,3},{1,2},{2,1},{3,0},{4,7},{5,6},{6,5},{7,4},{8,11},{9,10},{10,... | collective-permute-start | bytes 43016 | tf_op jit(solution)/shard_map/ppermute | solution.py:59
  139.9 3.8 %collective-permute-start.19 = (bf16[1,8,896]{2,1,0:T(8,128)(2,1)S(1)}, bf16[1,8,896]{2,1,0:T(8,128)(2,1)S(1)}, u32[]{:S(2)}, u32[]{:S(2)}) collective-permute-start(bf16[1,8,896]{2,1,0:T(8,128)(2,1)S(1)} %bitcast.91), channel_id=1, source_target_pairs={{0,2},{1,3},{2,0},{3,1},{4,6},{5,7},{6,4},{7,5},{8,10},{9,11},{10,... | collective-permute-start | bytes 43016 | tf_op jit(solution)/shard_map/ppermute | solution.py:59
  140.9 3.7 %collective-permute-start.18 = (bf16[1,8,896]{2,1,0:T(8,128)(2,1)S(1)}, bf16[1,8,896]{2,1,0:T(8,128)(2,1)S(1)}, u32[]{:S(2)}, u32[]{:S(2)}) collective-permute-start(bf16[1,8,896]{2,1,0:T(8,128)(2,1)S(1)} %bitcast.92), channel_id=1, source_target_pairs={{0,1},{1,0},{2,3},{3,2},{4,5},{5,4},{6,7},{7,6},{8,9},{9,8},{10,11... | collective-permute-start | bytes 43016 | tf_op jit(solution)/shard_map/ppermute | solution.py:59
  144.6 7.6 %collective-permute-start.23 = (bf16[4,8,896]{2,1,0:T(8,128)(2,1)S(1)}, bf16[4,8,896]{2,1,0:T(8,128)(2,1)S(1)}, u32[]{:S(2)}, u32[]{:S(2)}) collective-permute-start(bf16[4,8,896]{2,1,0:T(8,128)(2,1)S(1)} %pad_maximum_fusion.5), channel_id=1, source_target_pairs={{0,12},{1,13},{2,14},{3,15},{4,8},{5,9},{6,10},{7,11},{8,4},{9,5},... | collective-permute-start | bytes 172040 | tf_op jit(solution)/shard_map/ppermute | solution.py:59
  146.3 5.9 %collective-permute-start.22 = (bf16[4,8,896]{2,1,0:T(8,128)(2,1)S(1)}, bf16[4,8,896]{2,1,0:T(8,128)(2,1)S(1)}, u32[]{:S(2)}, u32[]{:S(2)}) collective-permute-start(bf16[4,8,896]{2,1,0:T(8,128)(2,1)S(1)} %pad_maximum_fusion.5), channel_id=1, source_target_pairs={{0,8},{1,9},{2,10},{3,11},{4,12},{5,13},{6,14},{7,15},{8,0},{9,1},... | collective-permute-start | bytes 172040 | tf_op jit(solution)/shard_map/ppermute | solution.py:59
  147.2 4.2 %collective-permute-start.21 = (bf16[4,8,896]{2,1,0:T(8,128)(2,1)S(1)}, bf16[4,8,896]{2,1,0:T(8,128)(2,1)S(1)}, u32[]{:S(2)}, u32[]{:S(2)}) collective-permute-start(bf16[4,8,896]{2,1,0:T(8,128)(2,1)S(1)} %pad_maximum_fusion.5), channel_id=1, source_target_pairs={{0,4},{1,5},{2,6},{3,7},{4,0},{5,1},{6,2},{7,3},{8,12},{9,13},{10,... | collective-permute-start | bytes 172040 | tf_op jit(solution)/shard_map/ppermute | solution.py:59
  152.3 1.6 collective-permute-start.24
  164.4 4.6 %collective-permute-start.25 = (bf16[3072,384]{1,0:T(8,128)(2,1)S(1)}, bf16[3072,384]{1,0:T(8,128)(2,1)S(1)}, u32[]{:S(2)}, u32[]{:S(2)}) collective-permute-start(bf16[3072,384]{1,0:T(8,128)(2,1)S(1)} %get-tuple-element.179), channel_id=1, source_target_pairs={{0,16},{16,0},{1,17},{17,1},{2,18},{18,2},{3,19},{19,3},{4,20},{20... | collective-permute-start | bytes 7077896 | tf_op jit(solution)/shard_map/ppermute | solution.py:59
  171.4 16.9 %collective-permute-start.26 = (bf16[4,2,96,384]{3,2,1,0:T(8,128)(2,1)}, bf16[4,2,96,384]{3,2,1,0:T(8,128)(2,1)}, u32[]{:S(2)}, u32[]{:S(2)}) collective-permute-start(bf16[4,2,96,384]{3,2,1,0:T(8,128)(2,1)} %get-tuple-element.180), channel_id=1, source_target_pairs={{0,1},{1,0},{2,3},{3,2},{4,5},{5,4},{6,7},{7,6},{8,9},{9,8},{10,11... | collective-permute-start | bytes 1769480 | tf_op jit(solution)/shard_map/ppermute | solution.py:59
  172.9 15.4 %collective-permute-start.27 = (bf16[4,2,96,384]{3,2,1,0:T(8,128)(2,1)}, bf16[4,2,96,384]{3,2,1,0:T(8,128)(2,1)}, u32[]{:S(2)}, u32[]{:S(2)}) collective-permute-start(bf16[4,2,96,384]{3,2,1,0:T(8,128)(2,1)} %get-tuple-element.182), channel_id=1, source_target_pairs={{0,2},{1,3},{2,0},{3,1},{4,6},{5,7},{6,4},{7,5},{8,10},{9,11},{10,... | collective-permute-start | bytes 1769480 | tf_op jit(solution)/shard_map/ppermute | solution.py:59
  191.6 8.8 %collective-permute-start.28 = (bf16[4,96,384]{2,1,0:T(8,128)(2,1)}, bf16[4,96,384]{2,1,0:T(8,128)(2,1)}, u32[]{:S(2)}, u32[]{:S(2)}) collective-permute-start(bf16[4,96,384]{2,1,0:T(8,128)(2,1)} %get-tuple-element.191), channel_id=1, source_target_pairs={{0,2},{1,3},{2,0},{3,1},{4,6},{5,7},{6,4},{7,5},{8,10},{9,11},{10,... | collective-permute-start | bytes 884744 | tf_op jit(solution)/shard_map/ppermute | solution.py:59
  192.7 8.5 %collective-permute-start.29 = (bf16[4,96,384]{2,1,0:T(8,128)(2,1)}, bf16[4,96,384]{2,1,0:T(8,128)(2,1)}, u32[]{:S(2)}, u32[]{:S(2)}) collective-permute-start(bf16[4,96,384]{2,1,0:T(8,128)(2,1)} %get-tuple-element.193), channel_id=1, source_target_pairs={{0,1},{1,0},{2,3},{3,2},{4,5},{5,4},{6,7},{7,6},{8,9},{9,8},{10,11... | collective-permute-start | bytes 884744 | tf_op jit(solution)/shard_map/ppermute | solution.py:59
  200.1 11.0 %collective-permute-start.30 = (bf16[768,1536]{1,0:T(8,128)(2,1)}, bf16[768,1536]{1,0:T(8,128)(2,1)}, u32[]{:S(2)}, u32[]{:S(2)}) collective-permute-start(bf16[768,1536]{1,0:T(8,128)(2,1)} %get-tuple-element.198), channel_id=1, source_target_pairs={{0,16},{16,0},{1,17},{17,1},{2,18},{18,2},{3,19},{19,3},{4,20},{20... | collective-permute-start | bytes 7077896 | tf_op jit(solution)/shard_map/ppermute | solution.py:59
  204.3 6.8 %collective-permute-start.31 = (bf16[768,384]{1,0:T(8,128)(2,1)}, bf16[768,384]{1,0:T(8,128)(2,1)}, u32[]{:S(2)}, u32[]{:S(2)}) collective-permute-start(bf16[768,384]{1,0:T(8,128)(2,1)} %get-tuple-element.209), channel_id=1, source_target_pairs={{0,16},{16,0},{1,17},{17,1},{2,18},{18,2},{3,19},{19,3},{4,20},{20... | collective-permute-start | bytes 1769480 | tf_op jit(solution)/shard_map/ppermute | solution.py:59
  206.7 41.5 %collective-permute-start.34 = (bf16[1,96,768]{2,1,0:T(8,128)(2,1)}, bf16[1,96,768]{2,1,0:T(8,128)(2,1)}, u32[]{:S(2)}, u32[]{:S(2)}) collective-permute-start(bf16[1,96,768]{2,1,0:T(8,128)(2,1)} %get-tuple-element.204), channel_id=1, source_target_pairs={{0,4},{1,5},{2,6},{3,7},{4,0},{5,1},{6,2},{7,3},{8,12},{9,13},{10,... | collective-permute-start | bytes 442376 | tf_op jit(solution)/shard_map/ppermute | solution.py:59
  207.9 40.4 %collective-permute-start.35 = (bf16[1,96,768]{2,1,0:T(8,128)(2,1)}, bf16[1,96,768]{2,1,0:T(8,128)(2,1)}, u32[]{:S(2)}, u32[]{:S(2)}) collective-permute-start(bf16[1,96,768]{2,1,0:T(8,128)(2,1)} %get-tuple-element.205), channel_id=1, source_target_pairs={{0,8},{1,9},{2,10},{3,11},{4,12},{5,13},{6,14},{7,15},{8,0},{9,1},... | collective-permute-start | bytes 442376 | tf_op jit(solution)/shard_map/ppermute | solution.py:59
  209.0 39.2 %collective-permute-start.36 = (bf16[1,96,768]{2,1,0:T(8,128)(2,1)}, bf16[1,96,768]{2,1,0:T(8,128)(2,1)}, u32[]{:S(2)}, u32[]{:S(2)}) collective-permute-start(bf16[1,96,768]{2,1,0:T(8,128)(2,1)} %get-tuple-element.206), channel_id=1, source_target_pairs={{0,12},{1,13},{2,14},{3,15},{4,8},{5,9},{6,10},{7,11},{8,4},{9,5},... | collective-permute-start | bytes 442376 | tf_op jit(solution)/shard_map/ppermute | solution.py:59
  215.4 30.4 %collective-permute-start.33 = (bf16[4,2,48,896]{3,2,1,0:T(8,128)(2,1)}, bf16[4,2,48,896]{3,2,1,0:T(8,128)(2,1)}, u32[]{:S(2)}, u32[]{:S(2)}) collective-permute-start(bf16[4,2,48,896]{3,2,1,0:T(8,128)(2,1)} %get-tuple-element.212), channel_id=1, source_target_pairs={{0,2},{1,3},{2,0},{3,1},{4,6},{5,7},{6,4},{7,5},{8,10},{9,11},{10,... | collective-permute-start | bytes 2064392 | tf_op jit(solution)/shard_map/ppermute | solution.py:59
  216.3 29.4 %collective-permute-start.32 = (bf16[4,2,48,1024]{3,2,1,0:T(8,128)(2,1)}, bf16[4,2,48,1024]{3,2,1,0:T(8,128)(2,1)}, u32[]{:S(2)}, u32[]{:S(2)}) collective-permute-start(bf16[4,2,48,1024]{3,2,1,0:T(8,128)(2,1)} %get-tuple-element.210), channel_id=1, source_target_pairs={{0,1},{1,0},{2,3},{3,2},{4,5},{5,4},{6,7},{7,6},{8,9},{9,8},{10,11... | collective-permute-start | bytes 2359304 | tf_op jit(solution)/shard_map/ppermute | solution.py:59
  220.0 19.7 %copy-start.14 = (bf16[768,1024]{1,0:T(8,128)(2,1)S(1)}, bf16[768,1024]{1,0:T(8,128)(2,1)}, u32[]{:S(2)}) copy-start(bf16[768,1024]{1,0:T(8,128)(2,1)} %get-tuple-element.171.left_ref) | copy-start | bytes 4718596
  245.8 14.4 %collective-permute-start.37 = (bf16[768,1152]{1,0:T(8,128)(2,1)}, bf16[768,1152]{1,0:T(8,128)(2,1)}, u32[]{:S(2)}, u32[]{:S(2)}) collective-permute-start(bf16[768,1152]{1,0:T(8,128)(2,1)} %get-tuple-element.217), channel_id=1, source_target_pairs={{0,16},{16,0},{1,17},{17,1},{2,18},{18,2},{3,19},{19,3},{4,20},{20... | collective-permute-start | bytes 5308424 | tf_op jit(solution)/shard_map/ppermute | solution.py:59
  257.8 2.4 collective-permute-start.38
  258.0 12.0 %collective-permute-start.39 = (bf16[4,48,1024]{2,1,0:T(8,128)(2,1)S(1)}, bf16[4,48,1024]{2,1,0:T(8,128)(2,1)S(1)}, u32[]{:S(2)}, u32[]{:S(2)}) collective-permute-start(bf16[4,48,1024]{2,1,0:T(8,128)(2,1)S(1)} %get-tuple-element.219), channel_id=1, source_target_pairs={{0,2},{1,3},{2,0},{3,1},{4,6},{5,7},{6,4},{7,5},{8,10},{9,11},{10,... | collective-permute-start | bytes 1179656 | tf_op jit(solution)/shard_map/ppermute | solution.py:59
  259.1 10.9 %collective-permute-start.40 = (bf16[4,48,896]{2,1,0:T(8,128)(2,1)S(1)}, bf16[4,48,896]{2,1,0:T(8,128)(2,1)S(1)}, u32[]{:S(2)}, u32[]{:S(2)}) collective-permute-start(bf16[4,48,896]{2,1,0:T(8,128)(2,1)S(1)} %get-tuple-element.221), channel_id=1, source_target_pairs={{0,1},{1,0},{2,3},{3,2},{4,5},{5,4},{6,7},{7,6},{8,9},{9,8},{10,11... | collective-permute-start | bytes 1032200 | tf_op jit(solution)/shard_map/ppermute | solution.py:59
  263.8 18.1 %collective-permute-start.41 = (bf16[4,2,48,768]{3,2,1,0:T(8,128)(2,1)}, bf16[4,2,48,768]{3,2,1,0:T(8,128)(2,1)}, u32[]{:S(2)}, u32[]{:S(2)}) collective-permute-start(bf16[4,2,48,768]{3,2,1,0:T(8,128)(2,1)} %get-tuple-element.233), channel_id=1, source_target_pairs={{0,1},{1,0},{2,3},{3,2},{4,5},{5,4},{6,7},{7,6},{8,9},{9,8},{10,11... | collective-permute-start | bytes 1769480 | tf_op jit(solution)/shard_map/ppermute | solution.py:59
  264.7 17.3 %collective-permute-start.42 = (bf16[4,2,48,768]{3,2,1,0:T(8,128)(2,1)}, bf16[4,2,48,768]{3,2,1,0:T(8,128)(2,1)}, u32[]{:S(2)}, u32[]{:S(2)}) collective-permute-start(bf16[4,2,48,768]{3,2,1,0:T(8,128)(2,1)} %get-tuple-element.235), channel_id=1, source_target_pairs={{0,2},{1,3},{2,0},{3,1},{4,6},{5,7},{6,4},{7,5},{8,10},{9,11},{10,... | collective-permute-start | bytes 1769480 | tf_op jit(solution)/shard_map/ppermute | solution.py:59
  270.7 15.6 %collective-permute-start.50 = (bf16[1,48,1920]{2,1,0:T(8,128)(2,1)S(1)}, bf16[1,48,1920]{2,1,0:T(8,128)(2,1)S(1)}, u32[]{:S(2)}, u32[]{:S(2)}) collective-permute-start(bf16[1,48,1920]{2,1,0:T(8,128)(2,1)S(1)} %get-tuple-element.241), channel_id=1, source_target_pairs={{0,12},{1,13},{2,14},{3,15},{4,8},{5,9},{6,10},{7,11},{8,4},{9,5},... | collective-permute-start | bytes 552968 | tf_op jit(solution)/shard_map/ppermute | solution.py:59
  272.6 15.2 %collective-permute-start.49 = (bf16[1,48,1920]{2,1,0:T(8,128)(2,1)S(1)}, bf16[1,48,1920]{2,1,0:T(8,128)(2,1)S(1)}, u32[]{:S(2)}, u32[]{:S(2)}) collective-permute-start(bf16[1,48,1920]{2,1,0:T(8,128)(2,1)S(1)} %get-tuple-element.240), channel_id=1, source_target_pairs={{0,8},{1,9},{2,10},{3,11},{4,12},{5,13},{6,14},{7,15},{8,0},{9,1},... | collective-permute-start | bytes 552968 | tf_op jit(solution)/shard_map/ppermute | solution.py:59
  272.6 15.2 %collective-permute-start.48 = (bf16[1,48,1920]{2,1,0:T(8,128)(2,1)S(1)}, bf16[1,48,1920]{2,1,0:T(8,128)(2,1)S(1)}, u32[]{:S(2)}, u32[]{:S(2)}) collective-permute-start(bf16[1,48,1920]{2,1,0:T(8,128)(2,1)S(1)} %get-tuple-element.239), channel_id=1, source_target_pairs={{0,4},{1,5},{2,6},{3,7},{4,0},{5,1},{6,2},{7,3},{8,12},{9,13},{10,... | collective-permute-start | bytes 552968 | tf_op jit(solution)/shard_map/ppermute | solution.py:59
  284.2 8.5 %collective-permute-start.43 = (bf16[4,48,768]{2,1,0:T(8,128)(2,1)S(1)}, bf16[4,48,768]{2,1,0:T(8,128)(2,1)S(1)}, u32[]{:S(2)}, u32[]{:S(2)}) collective-permute-start(bf16[4,48,768]{2,1,0:T(8,128)(2,1)S(1)} %get-tuple-element.245), channel_id=1, source_target_pairs={{0,2},{1,3},{2,0},{3,1},{4,6},{5,7},{6,4},{7,5},{8,10},{9,11},{10,... | collective-permute-start | bytes 884744 | tf_op jit(solution)/shard_map/ppermute | solution.py:59
  285.3 8.1 %collective-permute-start.44 = (bf16[4,48,768]{2,1,0:T(8,128)(2,1)S(1)}, bf16[4,48,768]{2,1,0:T(8,128)(2,1)S(1)}, u32[]{:S(2)}, u32[]{:S(2)}) collective-permute-start(bf16[4,48,768]{2,1,0:T(8,128)(2,1)S(1)} %get-tuple-element.246), channel_id=1, source_target_pairs={{0,1},{1,0},{2,3},{3,2},{4,5},{5,4},{6,7},{7,6},{8,9},{9,8},{10,11... | collective-permute-start | bytes 884744 | tf_op jit(solution)/shard_map/ppermute | solution.py:59
  294.2 13.1 %copy-start.5 = (f32[4,48,384]{2,1,0:T(8,128)S(1)}, f32[4,48,384]{2,1,0:T(8,128)}, u32[]{:S(2)}) copy-start(f32[4,48,384]{2,1,0:T(8,128)} %refs_1_.1) | copy-start | bytes 884740
  294.2 13.1 %copy-start.6 = (f32[4,48,384]{2,1,0:T(8,128)S(1)}, f32[4,48,384]{2,1,0:T(8,128)}, u32[]{:S(2)}) copy-start(f32[4,48,384]{2,1,0:T(8,128)} %refs_0_.1) | copy-start | bytes 884740
  294.2 13.1 %copy-start.7 = (f32[4,48,384]{2,1,0:T(8,128)S(1)}, f32[4,48,384]{2,1,0:T(8,128)}, u32[]{:S(2)}) copy-start(f32[4,48,384]{2,1,0:T(8,128)} %refs_2_.1) | copy-start | bytes 884740
  294.2 13.1 %copy-start.8 = (f32[256,48]{0,1:T(8,128)S(1)}, f32[256,48]{0,1:T(8,128)}, u32[]{:S(2)}) copy-start(f32[256,48]{0,1:T(8,128)} %param.37) | copy-start | bytes 147460
  294.3 13.1 %copy-start.9 = (f32[256,48]{0,1:T(8,128)S(1)}, f32[256,48]{0,1:T(8,128)}, u32[]{:S(2)}) copy-start(f32[256,48]{0,1:T(8,128)} %param.38) | copy-start | bytes 147460
  294.3 13.1 %copy-start.10 = (f32[256,48]{0,1:T(8,128)S(1)}, f32[256,48]{0,1:T(8,128)}, u32[]{:S(2)}) copy-start(f32[256,48]{0,1:T(8,128)} %param.39) | copy-start | bytes 147460
  294.3 13.1 %copy-start.11 = (f32[4,48]{1,0:T(4,128)S(1)}, f32[4,48]{1,0:T(4,128)}, u32[]{:S(2)}) copy-start(f32[4,48]{1,0:T(4,128)} %refs_4_.1) | copy-start | bytes 2308
  294.3 13.1 %copy-start.12 = (f32[4,48]{1,0:T(4,128)S(1)}, f32[4,48]{1,0:T(4,128)}, u32[]{:S(2)}) copy-start(f32[4,48]{1,0:T(4,128)} %refs_3_) | copy-start | bytes 2308
  294.3 5.9 %collective-permute-start.45 = (bf16[1,48,1536]{2,1,0:T(8,128)(2,1)S(1)}, bf16[1,48,1536]{2,1,0:T(8,128)(2,1)S(1)}, u32[]{:S(2)}, u32[]{:S(2)}) collective-permute-start(bf16[1,48,1536]{2,1,0:T(8,128)(2,1)S(1)} %get-tuple-element.248), channel_id=1, source_target_pairs={{0,4},{1,5},{2,6},{3,7},{4,0},{5,1},{6,2},{7,3},{8,12},{9,13},{10,... | collective-permute-start | bytes 442376 | tf_op jit(solution)/shard_map/ppermute | solution.py:59
  294.6 12.7 %collective-permute-start.46 = (bf16[1,48,1536]{2,1,0:T(8,128)(2,1)S(1)}, bf16[1,48,1536]{2,1,0:T(8,128)(2,1)S(1)}, u32[]{:S(2)}, u32[]{:S(2)}) collective-permute-start(bf16[1,48,1536]{2,1,0:T(8,128)(2,1)S(1)} %get-tuple-element.249), channel_id=1, source_target_pairs={{0,8},{1,9},{2,10},{3,11},{4,12},{5,13},{6,14},{7,15},{8,0},{9,1},... | collective-permute-start | bytes 442376 | tf_op jit(solution)/shard_map/ppermute | solution.py:59
  296.7 10.6 %collective-permute-start.47 = (bf16[1,48,1536]{2,1,0:T(8,128)(2,1)S(1)}, bf16[1,48,1536]{2,1,0:T(8,128)(2,1)S(1)}, u32[]{:S(2)}, u32[]{:S(2)}) collective-permute-start(bf16[1,48,1536]{2,1,0:T(8,128)(2,1)S(1)} %get-tuple-element.250), channel_id=1, source_target_pairs={{0,12},{1,13},{2,14},{3,15},{4,8},{5,9},{6,10},{7,11},{8,4},{9,5},... | collective-permute-start | bytes 442376 | tf_op jit(solution)/shard_map/ppermute | solution.py:59
  (25 other events, 185.1 us)
Sparse Core Ops, SparseCore 0:
  28.6 83.7 all-gather.1

commit v4 on v3

--- a/solution.py
+++ b/solution.py
@@ -559,7 +559,7 @@
     token_count, width = tokens.shape
     triple = qkv.shape[2]
     outs = [
-        far_off(token_count, width, dtype=jnp.float32),
+        pltpu.VMEM((token_count, width), jnp.float32),
         far_off(width, token_count),
         far_off(2, token_count, triple),
         stacked(8, width),
@@ -684,7 +684,7 @@
         forward_kernel,
         (token_count // CHUNK,),
         at,
-        [far_away(hidden0), far_away(context), out_weight, vectors, near_by(up), up_bias, near_by(down)],
+        [near_by(hidden0), far_away(context), out_weight, vectors, near_by(up), up_bias, near_by(down)],
         tiles(hidden0, context)
         + [held(out_weight), held(vectors), HERE, held(up_bias), HERE],
         outs,

time: 318 us -> 323 us (1.016)
  local copies, waits for them, and re-layouts: 11.4 us -> 17 us
    unnamed x88 -> x84, local copies, waits for them, and re-layouts: 3.67 us -> 9.28 us
  transfers between devices with their start and end apart: 52 -> 52, of which waited for: 28 -> 28; matrix products, arithmetic and copies ran while one was open for 5% -> 5% of each run, Pallas kernels for 33% -> 32%
where the time goes in v4:
time: 323 us; the launch traced here: 321 us
  Pallas kernels  149 us (46%)
  waiting for transfers between devices  74.5 us (23%)
  starting transfers between devices  54.5 us (17%)
  local copies, waits for them, and re-layouts  17 us (5%)
  between operations  14.8 us (5%)
  other arithmetic  10.4 us (3%)
    pallas_call x9, Pallas kernels, kernel_call(): pl.pallas_call(kernel, grid_spec=pltpu.PrefetchScalarGridSpec(num_scalar_...  80.7 us
    ppermute x51, waiting for transfers between devices, exchanged(): lax.ppermute(block, axis, [(place, place ^ mask) for place in range(count)])  74.2 us
    ppermute x51, starting transfers between devices, exchanged(): lax.ppermute(block, axis, [(place, place ^ mask) for place in range(count)])  54.5 us
    pallas_call x9, Pallas kernels, fold_call(): pl.pallas_call(kernel, grid_spec=pltpu.PrefetchScalarGridSpec(num_scalar_...  21.5 us
    pallas_call x1, Pallas kernels, attend_back(): pl.pallas_call(attend_back_kernel, grid_spec=pltpu.PrefetchScalarGridSpec...  19.7 us
    pallas_call x1, Pallas kernels, attend(): pl.pallas_call(attend_kernel, grid_spec=pltpu.PrefetchScalarGridSpec(num_...  19 us
    unnamed x84, local copies, waits for them, and re-layouts  9.28 us
  transfers between devices with their start and end apart: 52, of which 28 were waited for; matrix products, arithmetic and copies ran while one was open for 5% of the time, Pallas kernels for 32%

profile of v4, /device:TPU:0, one launch (start us, length us, event | category | flops | bytes accessed | tf_op | source)
XLA Modules:
  0.0 321.3 jit_solution(1998948419313931420)
XLA Ops:
  10.8 5.1 %collective-permute-start.2 = (bf16[1,48,1536]{2,1,0:T(8,128)(2,1)S(1)}, bf16[1,48,1536]{2,1,0:T(8,128)(2,1)S(1)}, u32[]{:S(2)}, u32[]{:S(2)}) collective-permute-start(bf16[1,48,1536]{2,1,0:T(8,128)(2,1)S(1)} %constant_dynamic-update-slice_fusion), channel_id=1, source_target_pairs={{0,12},{1,13},{2,14},{3,15},{4,8},{5,9},{6,10},{7,11},{8,4},{9,5},... | collective-permute-start | bytes 442376 | tf_op jit(solution)/shard_map/ppermute | solution.py:59
  16.5 1.6 convert_element_type.39
  18.2 2.5 collective-permute-done.2
  20.7 7.7 %collective-permute-done.1 = bf16[1,48,1536]{2,1,0:T(8,128)(2,1)S(1)} collective-permute-done((bf16[1,48,1536]{2,1,0:T(8,128)(2,1)S(1)}, bf16[1,48,1536]{2,1,0:T(8,128)(2,1)S(1)}, u32[]{:S(2)}, u32[]{:S(2)}) %collective-permute-start.1) | collective-permute-done | bytes 147488 | tf_op jit(solution)/shard_map/ppermute | solution.py:59
  28.6 1.6 collective-permute-start.4
  30.2 1.5 collective-permute-start.3
  31.7 5.0 %collective-permute-done.4 = bf16[4,48,768]{2,1,0:T(8,128)(2,1)S(1)} collective-permute-done((bf16[4,48,768]{2,1,0:T(8,128)(2,1)S(1)}, bf16[4,48,768]{2,1,0:T(8,128)(2,1)S(1)}, u32[]{:S(2)}, u32[]{:S(2)}) %collective-permute-start.4) | collective-permute-done | bytes 294944 | tf_op jit(solution)/shard_map/ppermute | solution.py:59
  38.0 2.4 collective-permute-start.7
  40.4 2.1 collective-permute-start.5
  42.5 1.5 collective-permute-start.9
  44.5 3.9 %collective-permute-done.7 = bf16[1,48,2048]{2,1,0:T(8,128)(2,1)S(1)} collective-permute-done((bf16[1,48,2048]{2,1,0:T(8,128)(2,1)S(1)}, bf16[1,48,2048]{2,1,0:T(8,128)(2,1)S(1)}, u32[]{:S(2)}, u32[]{:S(2)}) %collective-permute-start.7) | collective-permute-done | bytes 196640 | tf_op jit(solution)/shard_map/ppermute | solution.py:59
  48.4 9.9 %collective-permute-done.6 = bf16[1,48,2048]{2,1,0:T(8,128)(2,1)S(1)} collective-permute-done((bf16[1,48,2048]{2,1,0:T(8,128)(2,1)S(1)}, bf16[1,48,2048]{2,1,0:T(8,128)(2,1)S(1)}, u32[]{:S(2)}, u32[]{:S(2)}) %collective-permute-start.6) | collective-permute-done | bytes 196640 | tf_op jit(solution)/shard_map/ppermute | solution.py:59
  60.9 1.5 collective-permute-start.12
  63.7 1.7 shard_map.395
  65.4 8.5 %shard_map.396 = (f32[1024,768]{1,0:T(8,128)S(1)}, bf16[768,1024]{1,0:T(8,128)(2,1)}, bf16[2,1024,1152]{2,1,0:T(8,128)(2,1)}, f32[8,768]{1,0:T(8,128)S(1)}, f32[4,768]{1,0:T(4,128)S(1)}) custom-call(s32[13]{0:T(128)S(1)} %concatenate.66.at_ref.at, bf16[1024,768]{1,0:T(8,128)(2,1)} %bitcast.100, bf16[768,512]{1,0:T(8,128)(2,1)S(1)} %bitcast.80, ...), custom_call_target="tpu_custom_call" | custom-call | flops 1000 | bytes 1000 | tf_op jit(solution)/shard_map/pallas_call | solution.py:512
  73.9 1.3 constant_dynamic-update-slice_fusion.12
  76.8 1.6 collective-permute-start.15
  81.2 19.0 %shard_map.397 = (bf16[1024,768]{1,0:T(8,128)(2,1)}, bf16[768,1024]{1,0:T(8,128)(2,1)}, bf16[6,2,2,512,512]{4,3,2,1,0:T(8,128)(2,1)}) custom-call(s32[13]{0:T(128)S(1)} %concatenate.66.at_ref.at, bf16[2,1024,1152]{2,1,0:T(8,128)(2,1)} %get-tuple-element.156.q_ref.k_ref.v_ref, bf16[2,1024,1152]{2,1,0:T(8,128)(2,1)} %get-tuple-element.156.q_ref.k_ref.v_ref, ...), custom_call_target="tpu_custom_call" | custom-call | flops 1000 | bytes 1000 | tf_op jit(solution)/shard_map/pallas_call | solution.py:396
  100.3 3.9 %collective-permute-done.15 = bf16[8,48,1024]{2,1,0:T(8,128)(2,1)S(1)} collective-permute-done((bf16[8,48,1024]{2,1,0:T(8,128)(2,1)S(1)}, bf16[8,48,1024]{2,1,0:T(8,128)(2,1)S(1)}, u32[]{:S(2)}, u32[]{:S(2)}) %collective-permute-start.15) | collective-permute-done | bytes 786464 | tf_op jit(solution)/shard_map/ppermute | solution.py:59
  104.3 3.3 %collective-permute-done.14 = bf16[8,48,1024]{2,1,0:T(8,128)(2,1)S(1)} collective-permute-done((bf16[8,48,1024]{2,1,0:T(8,128)(2,1)S(1)}, bf16[8,48,1024]{2,1,0:T(8,128)(2,1)S(1)}, u32[]{:S(2)}, u32[]{:S(2)}) %collective-permute-start.14) | collective-permute-done | bytes 786464 | tf_op jit(solution)/shard_map/ppermute | solution.py:59
  107.8 1.2 copy.58
  109.0 1.6 reshape.201
  110.6 1.3 collective-permute-done.16.refs_2_
  112.2 4.7 %shard_map.398 = (bf16[2,16,48,1536]{3,2,1,0:T(8,128)(2,1)S(1)}, bf16[16,48,768]{2,1,0:T(8,128)(2,1)S(1)}, bf16[3072,768]{1,0:T(8,128)(2,1)S(1)}) custom-call(s32[13]{0:T(128)S(1)} %concatenate.66.at_ref.at, bf16[16,48,1024]{2,1,0:T(8,128)(2,1)S(1)} %constant_dynamic-update-slice_fusion.13.refs_0_, ...), custom_call_target="tpu_custom_call" | custom-call | flops 1000 | bytes 1000 | tf_op jit(solution)/shard_map/pallas_call | solution.py:166
  116.9 21.7 %shard_map.399 = (bf16[768,1024]{1,0:T(8,128)(2,1)}, bf16[1024,768]{1,0:T(8,128)(2,1)}, f32[1024,1]{1,0:T(8,128)S(1)}, bf16[3072,1024]{1,0:T(8,128)(2,1)S(1)}, b...) custom-call(s32[13]{0:T(128)S(1)} %concatenate.66.at_ref.at, ...), custom_call_target="tpu_custom_call" | custom-call | flops 1000 | bytes 1000 | tf_op jit(solution)/shard_map/pallas_call | solution.py:512
  138.7 2.6 copy-done.14
  143.3 1.4 collective-permute-start.18
  147.1 1.8 collective-permute-start.23
  149.7 1.8 collective-permute-start.21
  151.6 2.3 collective-permute-done.21
  154.8 1.5 collective-permute-done.24.others
  156.3 3.7 %shard_map.400 = (f32[1024,768]{1,0:T(8,128)S(1)}, bf16[1024,768]{1,0:T(8,128)(2,1)S(1)}, f32[3,768]{1,0:T(4,128)S(1)}) custom-call(s32[13]{0:T(128)S(1)} %concatenate.66.at_ref.at, bf16[128,896]{1,0:T(8,128)(2,1)S(1)} %bitcast.85, bf16[128,896]{1,0:T(8,128)(2,1)S(1)} %collective-permute-done.24.others, f32[8,768]{1,0:T(8,128)S(1)} %get-tuple-element.174.pooled, ...), custom_call_target="tpu_custom_call" | custom-call | flops 1000 | bytes 1000 | tf_op jit(solution)/shard_map/pallas_call | solution.py:512
  160.0 6.8 %shard_map.401 = (bf16[3072,384]{1,0:T(8,128)(2,1)S(1)}, bf16[3072,384]{1,0:T(8,128)(2,1)S(1)}) custom-call(s32[13]{0:T(128)S(1)} %concatenate.66.at_ref.at, bf16[3072,1024]{1,0:T(8,128)(2,1)S(1)} %get-tuple-element.172.left_ref, bf16[1024,768]{1,0:T(8,128)(2,1)S(1)} %get-tuple-element.177.right_ref.dresid2_half), custom_call_target="tpu_custom_call" | custom-call | flops 999999995904 | bytes 1000000000 | tf_op jit(solution)/shard_map/pallas_call | solution.py:512
  167.0 4.4 %collective-permute-done.25 = bf16[3072,384]{1,0:T(8,128)(2,1)S(1)} collective-permute-done((bf16[3072,384]{1,0:T(8,128)(2,1)S(1)}, bf16[3072,384]{1,0:T(8,128)(2,1)S(1)}, u32[]{:S(2)}, u32[]{:S(2)}) %collective-permute-start.25) | collective-permute-done | bytes 2359328 | tf_op jit(solution)/shard_map/ppermute | solution.py:59
  171.4 2.4 shard_map.402
  173.8 1.4 collective-permute-start.26
  176.3 2.8 copy-done.15
  179.0 14.4 %shard_map.403 = (bf16[1024,3072]{1,0:T(8,128)(2,1)S(1)}, f32[1,3072]{1,0:T(1,128)S(1)}, f32[1024,768]{1,0:T(8,128)}, bf16[1024,768]{1,0:T(8,128)(2,1)S(1)}, f32[3,768]{1,0:T(4,128)S(1)}) custom-call(s32[13]{0:T(128)S(1)} %concatenate.66.at_ref.at, f32[1024,768]{1,0:T(8,128)S(1)} %get-tuple-element.185.dresid2, ...), custom_call_target="tpu_custom_call" | custom-call | flops 999999995904 | bytes 1000000000 | tf_op jit(solution)/shard_map/pallas_call | solution.py:512
  193.4 2.8 shard_map.404
  197.9 6.9 %shard_map.405 = (bf16[768,1536]{1,0:T(8,128)(2,1)S(1)}, bf16[768,1536]{1,0:T(8,128)(2,1)}) custom-call(s32[13]{0:T(128)S(1)} %concatenate.66.at_ref.at, bf16[768,1024]{1,0:T(8,128)(2,1)S(1)} %copy-done.18, bf16[1024,3072]{1,0:T(8,128)(2,1)S(1)} %get-tuple-element.197.right_ref), custom_call_target="tpu_custom_call" | custom-call | flops 999999995904 | bytes 1000000000 | tf_op jit(solution)/shard_map/pallas_call | solution.py:512
  205.8 3.1 shard_map.406
  208.8 2.4 shard_map.407
  212.3 1.4 collective-permute-start.35
  213.7 1.9 collective-permute-start.36
  215.7 4.3 %shard_map.408 = (bf16[4,2,48,1024]{3,2,1,0:T(8,128)(2,1)}, f32[4,2,48,1024]{3,2,1,0:T(8,128)S(1)}, bf16[4,2,48,896]{3,2,1,0:T(8,128)(2,1)}, f32[4,2,48,896]{3,2,1,0:T(8,128)S(1)}) custom-call(s32[13]{0:T(128)S(1)} %concatenate.66.at_ref.at, bf16[4,2,2,48,1536]{4,3,2,1,0:T(8,128)(2,1)S(1)} %bitcast.60, ...), custom_call_target="tpu_custom_call" | custom-call | flops 1000 | bytes 1000 | tf_op jit(solution)/shard_map/pallas_call | solution.py:218
  221.9 1.4 convolution_convert_fusion.grad_ref
  223.4 1.2 slice-done.2
  224.6 19.7 %shard_map.409 = (bf16[2,1024,1152]{2,1,0:T(8,128)(2,1)S(1)}, f32[2,2,1,384]{3,2,1,0:T(1,128)S(1)}) custom-call(s32[13]{0:T(128)S(1)} %concatenate.66.at_ref.at, bf16[2,1024,1152]{2,1,0:T(8,128)(2,1)} %get-tuple-element.156.q_ref.k_ref.v_ref, bf16[2,1024,1152]{2,1,0:T(8,128)(2,1)} %get-tuple-element.156.q_ref.k_ref.v_ref, ...), custom_call_target="tpu_custom_call" | custom-call | flops 999999995904 | bytes 1000000000 | tf_op jit(solution)/shard_map/pallas_call | solution.py:470
  244.4 6.0 %shard_map.410 = (bf16[768,1152]{1,0:T(8,128)(2,1)S(1)}, bf16[768,1152]{1,0:T(8,128)(2,1)}) custom-call(s32[13]{0:T(128)S(1)} %concatenate.66.at_ref.at, bf16[768,1024]{1,0:T(8,128)(2,1)S(1)} %copy-done.16, bf16[2,1024,1152]{2,1,0:T(8,128)(2,1)S(1)} %get-tuple-element.216.right_ref.dtriples), custom_call_target="tpu_custom_call" | custom-call | flops 999999995904 | bytes 1000000000 | tf_op jit(solution)/shard_map/pallas_call | solution.py:512
  250.4 2.4 shard_map.411
  252.9 9.5 %shard_map.412 = (f32[1024,768]{1,0:T(8,128)}, f32[768,384]{1,0:T(8,128)S(1)}, bf16[768,384]{1,0:T(8,128)(2,1)S(1)}) custom-call(s32[13]{0:T(128)S(1)} %concatenate.66.at_ref.at, f32[1024,768]{1,0:T(8,128)} %get-tuple-element.224.dresid1, bf16[2,1024,1152]{2,1,0:T(8,128)(2,1)S(1)} %get-tuple-element.216.right_ref.dtriples, ...), custom_call_target="tpu_custom_call" | custom-call | flops 999999995904 | bytes 1000000000 | tf_op jit(solution)/shard_map/pallas_call | solution.py:512
  264.7 3.6 %shard_map.413 = (bf16[4,2,48,768]{3,2,1,0:T(8,128)(2,1)}, f32[4,2,48,768]{3,2,1,0:T(8,128)S(1)}, bf16[4,2,48,768]{3,2,1,0:T(8,128)(2,1)}, f32[4,2,48,768]{3,2,1,0:T(8,128)S(1)}) custom-call(s32[13]{0:T(128)S(1)} %concatenate.66.at_ref.at, bf16[4,2,2,48,1152]{4,3,2,1,0:T(8,128)(2,1)S(1)} %bitcast.63, ...), custom_call_target="tpu_custom_call" | custom-call | flops 1000 | bytes 1000 | tf_op jit(solution)/shard_map/pallas_call | solution.py:218
  270.3 4.3 %collective-permute-done.40.in1 = bf16[4,48,896]{2,1,0:T(8,128)(2,1)S(1)} collective-permute-done((bf16[4,48,896]{2,1,0:T(8,128)(2,1)S(1)}, bf16[4,48,896]{2,1,0:T(8,128)(2,1)S(1)}, u32[]{:S(2)}, u32[]{:S(2)}) %collective-permute-start.40) | collective-permute-done | bytes 344096 | tf_op jit(solution)/shard_map/ppermute | solution.py:59
  275.3 1.9 collective-permute-start.50
  277.2 2.5 collective-permute-start.48
  279.7 6.6 %collective-permute-done.41.refs_1_ = bf16[4,2,48,768]{3,2,1,0:T(8,128)(2,1)} collective-permute-done((bf16[4,2,48,768]{3,2,1,0:T(8,128)(2,1)}, bf16[4,2,48,768]{3,2,1,0:T(8,128)(2,1)}, u32[]{:S(2)}, u32[]{:S(2)}) %collective-permute-start.41) | collective-permute-done | bytes 589856 | tf_op jit(solution)/shard_map/ppermute | solution.py:59
  286.7 2.1 shard_map.415
  290.9 1.4 collective-permute-done.49
  295.4 1.8 collective-permute-done.43.in0
  299.1 2.3 collective-permute-start.46
  301.4 1.9 collective-permute-start.47
  305.2 6.7 %collective-permute-done.46 = bf16[1,48,1536]{2,1,0:T(8,128)(2,1)S(1)} collective-permute-done((bf16[1,48,1536]{2,1,0:T(8,128)(2,1)S(1)}, bf16[1,48,1536]{2,1,0:T(8,128)(2,1)S(1)}, u32[]{:S(2)}, u32[]{:S(2)}) %collective-permute-start.46) | collective-permute-done | bytes 147488 | tf_op jit(solution)/shard_map/ppermute | solution.py:59
  312.0 1.3 shard_map.417
  313.3 1.2 add_multiply_fusion.2
  (190 shorter events, 42.3 us)
Async XLA Ops:
  7.2 21.3 %copy-start.19 = (f32[48,1536]{1,0:T(8,128)S(1)}, f32[48,1536]{1,0:T(8,128)}, u32[]{:S(2)}) copy-start(f32[48,1536]{1,0:T(8,128)} %param.25) | copy-start | bytes 884740
  7.2 105.0 %all-gather.2.cloned.1.call-start = ((), (), s32[]{:S(2)}) async-start(), calls=%async_computation | async-start | bytes 4866048 | tf_op jit(solution)/shard_map/all_gather | solution.py:1052
  10.8 9.9 %collective-permute-start.2 = (bf16[1,48,1536]{2,1,0:T(8,128)(2,1)S(1)}, bf16[1,48,1536]{2,1,0:T(8,128)(2,1)S(1)}, u32[]{:S(2)}, u32[]{:S(2)}) collective-permute-start(bf16[1,48,1536]{2,1,0:T(8,128)(2,1)S(1)} %constant_dynamic-update-slice_fusion), channel_id=1, source_target_pairs={{0,12},{1,13},{2,14},{3,15},{4,8},{5,9},{6,10},{7,11},{8,4},{9,5},... | collective-permute-start | bytes 442376 | tf_op jit(solution)/shard_map/ppermute | solution.py:59
  15.9 12.5 %collective-permute-start.1 = (bf16[1,48,1536]{2,1,0:T(8,128)(2,1)S(1)}, bf16[1,48,1536]{2,1,0:T(8,128)(2,1)S(1)}, u32[]{:S(2)}, u32[]{:S(2)}) collective-permute-start(bf16[1,48,1536]{2,1,0:T(8,128)(2,1)S(1)} %constant_dynamic-update-slice_fusion), channel_id=1, source_target_pairs={{0,8},{1,9},{2,10},{3,11},{4,12},{5,13},{6,14},{7,15},{8,0},{9,1},... | collective-permute-start | bytes 442376 | tf_op jit(solution)/shard_map/ppermute | solution.py:59
  15.9 12.5 %collective-permute-start = (bf16[1,48,1536]{2,1,0:T(8,128)(2,1)S(1)}, bf16[1,48,1536]{2,1,0:T(8,128)(2,1)S(1)}, u32[]{:S(2)}, u32[]{:S(2)}) collective-permute-start(bf16[1,48,1536]{2,1,0:T(8,128)(2,1)S(1)} %constant_dynamic-update-slice_fusion), channel_id=1, source_target_pairs={{0,4},{1,5},{2,6},{3,7},{4,0},{5,1},{6,2},{7,3},{8,12},{9,13},{10,... | collective-permute-start | bytes 442376 | tf_op jit(solution)/shard_map/ppermute | solution.py:59
  28.6 8.1 %collective-permute-start.4 = (bf16[4,48,768]{2,1,0:T(8,128)(2,1)S(1)}, bf16[4,48,768]{2,1,0:T(8,128)(2,1)S(1)}, u32[]{:S(2)}, u32[]{:S(2)}) collective-permute-start(bf16[4,48,768]{2,1,0:T(8,128)(2,1)S(1)} %get-tuple-element.285), channel_id=1, source_target_pairs={{0,1},{1,0},{2,3},{3,2},{4,5},{5,4},{6,7},{7,6},{8,9},{9,8},{10,11... | collective-permute-start | bytes 884744 | tf_op jit(solution)/shard_map/ppermute | solution.py:59
  30.2 7.8 %collective-permute-start.3 = (bf16[4,48,768]{2,1,0:T(8,128)(2,1)S(1)}, bf16[4,48,768]{2,1,0:T(8,128)(2,1)S(1)}, u32[]{:S(2)}, u32[]{:S(2)}) collective-permute-start(bf16[4,48,768]{2,1,0:T(8,128)(2,1)S(1)} %get-tuple-element.286), channel_id=1, source_target_pairs={{0,2},{1,3},{2,0},{3,1},{4,6},{5,7},{6,4},{7,5},{8,10},{9,11},{10,... | collective-permute-start | bytes 884744 | tf_op jit(solution)/shard_map/ppermute | solution.py:59
  38.0 10.4 %collective-permute-start.7 = (bf16[1,48,2048]{2,1,0:T(8,128)(2,1)S(1)}, bf16[1,48,2048]{2,1,0:T(8,128)(2,1)S(1)}, u32[]{:S(2)}, u32[]{:S(2)}) collective-permute-start(bf16[1,48,2048]{2,1,0:T(8,128)(2,1)S(1)} %bitcast.101), channel_id=1, source_target_pairs={{0,12},{1,13},{2,14},{3,15},{4,8},{5,9},{6,10},{7,11},{8,4},{9,5},... | collective-permute-start | bytes 589832 | tf_op jit(solution)/shard_map/ppermute | solution.py:59
  40.4 17.9 %collective-permute-start.6 = (bf16[1,48,2048]{2,1,0:T(8,128)(2,1)S(1)}, bf16[1,48,2048]{2,1,0:T(8,128)(2,1)S(1)}, u32[]{:S(2)}, u32[]{:S(2)}) collective-permute-start(bf16[1,48,2048]{2,1,0:T(8,128)(2,1)S(1)} %bitcast.102), channel_id=1, source_target_pairs={{0,8},{1,9},{2,10},{3,11},{4,12},{5,13},{6,14},{7,15},{8,0},{9,1},... | collective-permute-start | bytes 589832 | tf_op jit(solution)/shard_map/ppermute | solution.py:59
  40.4 17.9 %collective-permute-start.5 = (bf16[1,48,2048]{2,1,0:T(8,128)(2,1)S(1)}, bf16[1,48,2048]{2,1,0:T(8,128)(2,1)S(1)}, u32[]{:S(2)}, u32[]{:S(2)}) collective-permute-start(bf16[1,48,2048]{2,1,0:T(8,128)(2,1)S(1)} %bitcast.103), channel_id=1, source_target_pairs={{0,4},{1,5},{2,6},{3,7},{4,0},{5,1},{6,2},{7,3},{8,12},{9,13},{10,... | collective-permute-start | bytes 589832 | tf_op jit(solution)/shard_map/ppermute | solution.py:59
  42.5 16.1 %collective-permute-start.9 = (bf16[8,48,768]{2,1,0:T(8,128)(2,1)S(1)}, bf16[8,48,768]{2,1,0:T(8,128)(2,1)S(1)}, u32[]{:S(2)}, u32[]{:S(2)}) collective-permute-start(bf16[8,48,768]{2,1,0:T(8,128)(2,1)S(1)} %pad_maximum_fusion.3), channel_id=1, source_target_pairs={{0,2},{1,3},{2,0},{3,1},{4,6},{5,7},{6,4},{7,5},{8,10},{9,11},{10,... | collective-permute-start | bytes 1769480 | tf_op jit(solution)/shard_map/ppermute | solution.py:59
  44.0 14.7 %collective-permute-start.8 = (bf16[8,48,768]{2,1,0:T(8,128)(2,1)S(1)}, bf16[8,48,768]{2,1,0:T(8,128)(2,1)S(1)}, u32[]{:S(2)}, u32[]{:S(2)}) collective-permute-start(bf16[8,48,768]{2,1,0:T(8,128)(2,1)S(1)} %pad_maximum_fusion.2), channel_id=1, source_target_pairs={{0,1},{1,0},{2,3},{3,2},{4,5},{5,4},{6,7},{7,6},{8,9},{9,8},{10,11... | collective-permute-start | bytes 1769480 | tf_op jit(solution)/shard_map/ppermute | solution.py:59
  58.6 5.2 %collective-permute-start.11 = (bf16[16,48,768]{2,1,0:T(8,128)(2,1)S(1)}, bf16[16,48,768]{2,1,0:T(8,128)(2,1)S(1)}, u32[]{:S(2)}, u32[]{:S(2)}) collective-permute-start(bf16[16,48,768]{2,1,0:T(8,128)(2,1)S(1)} %constant_dynamic-update-slice_fusion.7.refs_1_), channel_id=1, source_target_pairs={{0,16},{16,0},{1,17},{17,1},{2,18},{18,2},{3,19},{19,3},{4,20},{20... | collective-permute-start | bytes 3538952 | tf_op jit(solution)/shard_map/ppermute | solution.py:59
  58.7 5.0 %collective-permute-start.10 = (bf16[16,48,768]{2,1,0:T(8,128)(2,1)S(1)}, bf16[16,48,768]{2,1,0:T(8,128)(2,1)}, u32[]{:S(2)}, u32[]{:S(2)}) collective-permute-start(bf16[16,48,768]{2,1,0:T(8,128)(2,1)S(1)} %constant_dynamic-update-slice_fusion.5.refs_0_), channel_id=1, source_target_pairs={{0,16},{16,0},{1,17},{17,1},{2,18},{18,2},{3,19},{19,3},{4,20},{20... | collective-permute-start | bytes 3538952 | tf_op jit(solution)/shard_map/ppermute | solution.py:59
  60.2 15.6 %collective-permute-start.13 = (bf16[4,48,1024]{2,1,0:T(8,128)(2,1)}, bf16[4,48,1024]{2,1,0:T(8,128)(2,1)}, u32[]{:S(2)}, u32[]{:S(2)}) collective-permute-start(bf16[4,48,1024]{2,1,0:T(8,128)(2,1)} %get-tuple-element.158), channel_id=1, source_target_pairs={{0,1},{1,0},{2,3},{3,2},{4,5},{5,4},{6,7},{7,6},{8,9},{9,8},{10,11... | collective-permute-start | bytes 1179656 | tf_op jit(solution)/shard_map/ppermute | solution.py:59
  60.9 18.6 %collective-permute-start.12 = (bf16[4,48,1024]{2,1,0:T(8,128)(2,1)}, bf16[4,48,1024]{2,1,0:T(8,128)(2,1)}, u32[]{:S(2)}, u32[]{:S(2)}) collective-permute-start(bf16[4,48,1024]{2,1,0:T(8,128)(2,1)} %get-tuple-element.157), channel_id=1, source_target_pairs={{0,2},{1,3},{2,0},{3,1},{4,6},{5,7},{6,4},{7,5},{8,10},{9,11},{10,... | collective-permute-start | bytes 1179656 | tf_op jit(solution)/shard_map/ppermute | solution.py:59
  76.8 27.4 %collective-permute-start.15 = (bf16[8,48,1024]{2,1,0:T(8,128)(2,1)S(1)}, bf16[8,48,1024]{2,1,0:T(8,128)(2,1)S(1)}, u32[]{:S(2)}, u32[]{:S(2)}) collective-permute-start(bf16[8,48,1024]{2,1,0:T(8,128)(2,1)S(1)} %constant_dynamic-update-slice_fusion.11), channel_id=1, source_target_pairs={{0,2},{1,3},{2,0},{3,1},{4,6},{5,7},{6,4},{7,5},{8,10},{9,11},{10,... | collective-permute-start | bytes 2359304 | tf_op jit(solution)/shard_map/ppermute | solution.py:59
  80.5 27.1 %collective-permute-start.14 = (bf16[8,48,1024]{2,1,0:T(8,128)(2,1)S(1)}, bf16[8,48,1024]{2,1,0:T(8,128)(2,1)S(1)}, u32[]{:S(2)}, u32[]{:S(2)}) collective-permute-start(bf16[8,48,1024]{2,1,0:T(8,128)(2,1)S(1)} %constant_dynamic-update-slice_fusion.9), channel_id=1, source_target_pairs={{0,1},{1,0},{2,3},{3,2},{4,5},{5,4},{6,7},{7,6},{8,9},{9,8},{10,11... | collective-permute-start | bytes 2359304 | tf_op jit(solution)/shard_map/ppermute | solution.py:59
  104.2 6.3 %collective-permute-start.17 = (bf16[16,48,1024]{2,1,0:T(8,128)(2,1)S(1)}, bf16[16,48,1024]{2,1,0:T(8,128)(2,1)}, u32[]{:S(2)}, u32[]{:S(2)}) collective-permute-start(bf16[16,48,1024]{2,1,0:T(8,128)(2,1)S(1)} %constant_dynamic-update-slice_fusion.15.refs_1_), channel_id=1, source_target_pairs={{0,16},{16,0},{1,17},{17,1},{2,18},{18,2},{3,19},{19,3},{4,20},{20... | collective-permute-start | bytes 4718600 | tf_op jit(solution)/shard_map/ppermute | solution.py:59
  107.7 4.2 %collective-permute-start.16 = (bf16[16,48,1024]{2,1,0:T(8,128)(2,1)S(1)}, bf16[16,48,1024]{2,1,0:T(8,128)(2,1)}, u32[]{:S(2)}, u32[]{:S(2)}) collective-permute-start(bf16[16,48,1024]{2,1,0:T(8,128)(2,1)S(1)} %constant_dynamic-update-slice_fusion.13.refs_0_), channel_id=1, source_target_pairs={{0,16},{16,0},{1,17},{17,1},{2,18},{18,2},{3,19},{19,3},{4,20},{20... | collective-permute-start | bytes 4718600 | tf_op jit(solution)/shard_map/ppermute | solution.py:59
  141.2 4.6 %collective-permute-start.20 = (bf16[1,8,896]{2,1,0:T(8,128)(2,1)S(1)}, bf16[1,8,896]{2,1,0:T(8,128)(2,1)S(1)}, u32[]{:S(2)}, u32[]{:S(2)}) collective-permute-start(bf16[1,8,896]{2,1,0:T(8,128)(2,1)S(1)} %bitcast.90), channel_id=1, source_target_pairs={{0,3},{1,2},{2,1},{3,0},{4,7},{5,6},{6,5},{7,4},{8,11},{9,10},{10,... | collective-permute-start | bytes 43016 | tf_op jit(solution)/shard_map/ppermute | solution.py:59
  142.3 3.7 %collective-permute-start.19 = (bf16[1,8,896]{2,1,0:T(8,128)(2,1)S(1)}, bf16[1,8,896]{2,1,0:T(8,128)(2,1)S(1)}, u32[]{:S(2)}, u32[]{:S(2)}) collective-permute-start(bf16[1,8,896]{2,1,0:T(8,128)(2,1)S(1)} %bitcast.91), channel_id=1, source_target_pairs={{0,2},{1,3},{2,0},{3,1},{4,6},{5,7},{6,4},{7,5},{8,10},{9,11},{10,... | collective-permute-start | bytes 43016 | tf_op jit(solution)/shard_map/ppermute | solution.py:59
  143.3 3.7 %collective-permute-start.18 = (bf16[1,8,896]{2,1,0:T(8,128)(2,1)S(1)}, bf16[1,8,896]{2,1,0:T(8,128)(2,1)S(1)}, u32[]{:S(2)}, u32[]{:S(2)}) collective-permute-start(bf16[1,8,896]{2,1,0:T(8,128)(2,1)S(1)} %bitcast.92), channel_id=1, source_target_pairs={{0,1},{1,0},{2,3},{3,2},{4,5},{5,4},{6,7},{7,6},{8,9},{9,8},{10,11... | collective-permute-start | bytes 43016 | tf_op jit(solution)/shard_map/ppermute | solution.py:59
  147.1 7.6 %collective-permute-start.23 = (bf16[4,8,896]{2,1,0:T(8,128)(2,1)S(1)}, bf16[4,8,896]{2,1,0:T(8,128)(2,1)S(1)}, u32[]{:S(2)}, u32[]{:S(2)}) collective-permute-start(bf16[4,8,896]{2,1,0:T(8,128)(2,1)S(1)} %pad_maximum_fusion.5), channel_id=1, source_target_pairs={{0,12},{1,13},{2,14},{3,15},{4,8},{5,9},{6,10},{7,11},{8,4},{9,5},... | collective-permute-start | bytes 172040 | tf_op jit(solution)/shard_map/ppermute | solution.py:59
  148.9 5.8 %collective-permute-start.22 = (bf16[4,8,896]{2,1,0:T(8,128)(2,1)S(1)}, bf16[4,8,896]{2,1,0:T(8,128)(2,1)S(1)}, u32[]{:S(2)}, u32[]{:S(2)}) collective-permute-start(bf16[4,8,896]{2,1,0:T(8,128)(2,1)S(1)} %pad_maximum_fusion.5), channel_id=1, source_target_pairs={{0,8},{1,9},{2,10},{3,11},{4,12},{5,13},{6,14},{7,15},{8,0},{9,1},... | collective-permute-start | bytes 172040 | tf_op jit(solution)/shard_map/ppermute | solution.py:59
  149.7 4.2 %collective-permute-start.21 = (bf16[4,8,896]{2,1,0:T(8,128)(2,1)S(1)}, bf16[4,8,896]{2,1,0:T(8,128)(2,1)S(1)}, u32[]{:S(2)}, u32[]{:S(2)}) collective-permute-start(bf16[4,8,896]{2,1,0:T(8,128)(2,1)S(1)} %pad_maximum_fusion.5), channel_id=1, source_target_pairs={{0,4},{1,5},{2,6},{3,7},{4,0},{5,1},{6,2},{7,3},{8,12},{9,13},{10,... | collective-permute-start | bytes 172040 | tf_op jit(solution)/shard_map/ppermute | solution.py:59
  154.7 1.6 collective-permute-start.24
  166.8 4.6 %collective-permute-start.25 = (bf16[3072,384]{1,0:T(8,128)(2,1)S(1)}, bf16[3072,384]{1,0:T(8,128)(2,1)S(1)}, u32[]{:S(2)}, u32[]{:S(2)}) collective-permute-start(bf16[3072,384]{1,0:T(8,128)(2,1)S(1)} %get-tuple-element.179), channel_id=1, source_target_pairs={{0,16},{16,0},{1,17},{17,1},{2,18},{18,2},{3,19},{19,3},{4,20},{20... | collective-permute-start | bytes 7077896 | tf_op jit(solution)/shard_map/ppermute | solution.py:59
  173.8 19.6 %collective-permute-start.26 = (bf16[4,2,96,384]{3,2,1,0:T(8,128)(2,1)}, bf16[4,2,96,384]{3,2,1,0:T(8,128)(2,1)}, u32[]{:S(2)}, u32[]{:S(2)}) collective-permute-start(bf16[4,2,96,384]{3,2,1,0:T(8,128)(2,1)} %get-tuple-element.180), channel_id=1, source_target_pairs={{0,1},{1,0},{2,3},{3,2},{4,5},{5,4},{6,7},{7,6},{8,9},{9,8},{10,11... | collective-permute-start | bytes 1769480 | tf_op jit(solution)/shard_map/ppermute | solution.py:59
  175.2 18.2 %collective-permute-start.27 = (bf16[4,2,96,384]{3,2,1,0:T(8,128)(2,1)}, bf16[4,2,96,384]{3,2,1,0:T(8,128)(2,1)}, u32[]{:S(2)}, u32[]{:S(2)}) collective-permute-start(bf16[4,2,96,384]{3,2,1,0:T(8,128)(2,1)} %get-tuple-element.182), channel_id=1, source_target_pairs={{0,2},{1,3},{2,0},{3,1},{4,6},{5,7},{6,4},{7,5},{8,10},{9,11},{10,... | collective-permute-start | bytes 1769480 | tf_op jit(solution)/shard_map/ppermute | solution.py:59
  196.2 8.8 %collective-permute-start.28 = (bf16[4,96,384]{2,1,0:T(8,128)(2,1)}, bf16[4,96,384]{2,1,0:T(8,128)(2,1)}, u32[]{:S(2)}, u32[]{:S(2)}) collective-permute-start(bf16[4,96,384]{2,1,0:T(8,128)(2,1)} %get-tuple-element.191), channel_id=1, source_target_pairs={{0,2},{1,3},{2,0},{3,1},{4,6},{5,7},{6,4},{7,5},{8,10},{9,11},{10,... | collective-permute-start | bytes 884744 | tf_op jit(solution)/shard_map/ppermute | solution.py:59
  197.2 8.5 %collective-permute-start.29 = (bf16[4,96,384]{2,1,0:T(8,128)(2,1)}, bf16[4,96,384]{2,1,0:T(8,128)(2,1)}, u32[]{:S(2)}, u32[]{:S(2)}) collective-permute-start(bf16[4,96,384]{2,1,0:T(8,128)(2,1)} %get-tuple-element.193), channel_id=1, source_target_pairs={{0,1},{1,0},{2,3},{3,2},{4,5},{5,4},{6,7},{7,6},{8,9},{9,8},{10,11... | collective-permute-start | bytes 884744 | tf_op jit(solution)/shard_map/ppermute | solution.py:59
  204.8 10.9 %collective-permute-start.30 = (bf16[768,1536]{1,0:T(8,128)(2,1)}, bf16[768,1536]{1,0:T(8,128)(2,1)}, u32[]{:S(2)}, u32[]{:S(2)}) collective-permute-start(bf16[768,1536]{1,0:T(8,128)(2,1)} %get-tuple-element.198), channel_id=1, source_target_pairs={{0,16},{16,0},{1,17},{17,1},{2,18},{18,2},{3,19},{19,3},{4,20},{20... | collective-permute-start | bytes 7077896 | tf_op jit(solution)/shard_map/ppermute | solution.py:59
  208.8 6.8 %collective-permute-start.31 = (bf16[768,384]{1,0:T(8,128)(2,1)}, bf16[768,384]{1,0:T(8,128)(2,1)}, u32[]{:S(2)}, u32[]{:S(2)}) collective-permute-start(bf16[768,384]{1,0:T(8,128)(2,1)} %get-tuple-element.209), channel_id=1, source_target_pairs={{0,16},{16,0},{1,17},{17,1},{2,18},{18,2},{3,19},{19,3},{4,20},{20... | collective-permute-start | bytes 1769480 | tf_op jit(solution)/shard_map/ppermute | solution.py:59
  211.2 41.6 %collective-permute-start.34 = (bf16[1,96,768]{2,1,0:T(8,128)(2,1)}, bf16[1,96,768]{2,1,0:T(8,128)(2,1)}, u32[]{:S(2)}, u32[]{:S(2)}) collective-permute-start(bf16[1,96,768]{2,1,0:T(8,128)(2,1)} %get-tuple-element.204), channel_id=1, source_target_pairs={{0,4},{1,5},{2,6},{3,7},{4,0},{5,1},{6,2},{7,3},{8,12},{9,13},{10,... | collective-permute-start | bytes 442376 | tf_op jit(solution)/shard_map/ppermute | solution.py:59
  212.3 40.6 %collective-permute-start.35 = (bf16[1,96,768]{2,1,0:T(8,128)(2,1)}, bf16[1,96,768]{2,1,0:T(8,128)(2,1)}, u32[]{:S(2)}, u32[]{:S(2)}) collective-permute-start(bf16[1,96,768]{2,1,0:T(8,128)(2,1)} %get-tuple-element.205), channel_id=1, source_target_pairs={{0,8},{1,9},{2,10},{3,11},{4,12},{5,13},{6,14},{7,15},{8,0},{9,1},... | collective-permute-start | bytes 442376 | tf_op jit(solution)/shard_map/ppermute | solution.py:59
  213.7 39.2 %collective-permute-start.36 = (bf16[1,96,768]{2,1,0:T(8,128)(2,1)}, bf16[1,96,768]{2,1,0:T(8,128)(2,1)}, u32[]{:S(2)}, u32[]{:S(2)}) collective-permute-start(bf16[1,96,768]{2,1,0:T(8,128)(2,1)} %get-tuple-element.206), channel_id=1, source_target_pairs={{0,12},{1,13},{2,14},{3,15},{4,8},{5,9},{6,10},{7,11},{8,4},{9,5},... | collective-permute-start | bytes 442376 | tf_op jit(solution)/shard_map/ppermute | solution.py:59
  220.0 30.4 %collective-permute-start.33 = (bf16[4,2,48,896]{3,2,1,0:T(8,128)(2,1)}, bf16[4,2,48,896]{3,2,1,0:T(8,128)(2,1)}, u32[]{:S(2)}, u32[]{:S(2)}) collective-permute-start(bf16[4,2,48,896]{3,2,1,0:T(8,128)(2,1)} %get-tuple-element.212), channel_id=1, source_target_pairs={{0,2},{1,3},{2,0},{3,1},{4,6},{5,7},{6,4},{7,5},{8,10},{9,11},{10,... | collective-permute-start | bytes 2064392 | tf_op jit(solution)/shard_map/ppermute | solution.py:59
  221.0 29.4 %collective-permute-start.32 = (bf16[4,2,48,1024]{3,2,1,0:T(8,128)(2,1)}, bf16[4,2,48,1024]{3,2,1,0:T(8,128)(2,1)}, u32[]{:S(2)}, u32[]{:S(2)}) collective-permute-start(bf16[4,2,48,1024]{3,2,1,0:T(8,128)(2,1)} %get-tuple-element.210), channel_id=1, source_target_pairs={{0,1},{1,0},{2,3},{3,2},{4,5},{5,4},{6,7},{7,6},{8,9},{9,8},{10,11... | collective-permute-start | bytes 2359304 | tf_op jit(solution)/shard_map/ppermute | solution.py:59
  224.6 19.7 %copy-start.16 = (bf16[768,1024]{1,0:T(8,128)(2,1)S(1)}, bf16[768,1024]{1,0:T(8,128)(2,1)}, u32[]{:S(2)}) copy-start(bf16[768,1024]{1,0:T(8,128)(2,1)} %get-tuple-element.171.left_ref) | copy-start | bytes 4718596
  250.4 14.3 %collective-permute-start.37 = (bf16[768,1152]{1,0:T(8,128)(2,1)}, bf16[768,1152]{1,0:T(8,128)(2,1)}, u32[]{:S(2)}, u32[]{:S(2)}) collective-permute-start(bf16[768,1152]{1,0:T(8,128)(2,1)} %get-tuple-element.217), channel_id=1, source_target_pairs={{0,16},{16,0},{1,17},{17,1},{2,18},{18,2},{3,19},{19,3},{4,20},{20... | collective-permute-start | bytes 5308424 | tf_op jit(solution)/shard_map/ppermute | solution.py:59
  262.4 2.3 collective-permute-start.38
  262.6 11.9 %collective-permute-start.39 = (bf16[4,48,1024]{2,1,0:T(8,128)(2,1)S(1)}, bf16[4,48,1024]{2,1,0:T(8,128)(2,1)S(1)}, u32[]{:S(2)}, u32[]{:S(2)}) collective-permute-start(bf16[4,48,1024]{2,1,0:T(8,128)(2,1)S(1)} %get-tuple-element.219), channel_id=1, source_target_pairs={{0,2},{1,3},{2,0},{3,1},{4,6},{5,7},{6,4},{7,5},{8,10},{9,11},{10,... | collective-permute-start | bytes 1179656 | tf_op jit(solution)/shard_map/ppermute | solution.py:59
  263.6 10.9 %collective-permute-start.40 = (bf16[4,48,896]{2,1,0:T(8,128)(2,1)S(1)}, bf16[4,48,896]{2,1,0:T(8,128)(2,1)S(1)}, u32[]{:S(2)}, u32[]{:S(2)}) collective-permute-start(bf16[4,48,896]{2,1,0:T(8,128)(2,1)S(1)} %get-tuple-element.221), channel_id=1, source_target_pairs={{0,1},{1,0},{2,3},{3,2},{4,5},{5,4},{6,7},{7,6},{8,9},{9,8},{10,11... | collective-permute-start | bytes 1032200 | tf_op jit(solution)/shard_map/ppermute | solution.py:59
  268.3 18.0 %collective-permute-start.41 = (bf16[4,2,48,768]{3,2,1,0:T(8,128)(2,1)}, bf16[4,2,48,768]{3,2,1,0:T(8,128)(2,1)}, u32[]{:S(2)}, u32[]{:S(2)}) collective-permute-start(bf16[4,2,48,768]{3,2,1,0:T(8,128)(2,1)} %get-tuple-element.233), channel_id=1, source_target_pairs={{0,1},{1,0},{2,3},{3,2},{4,5},{5,4},{6,7},{7,6},{8,9},{9,8},{10,11... | collective-permute-start | bytes 1769480 | tf_op jit(solution)/shard_map/ppermute | solution.py:59
  269.2 17.4 %collective-permute-start.42 = (bf16[4,2,48,768]{3,2,1,0:T(8,128)(2,1)}, bf16[4,2,48,768]{3,2,1,0:T(8,128)(2,1)}, u32[]{:S(2)}, u32[]{:S(2)}) collective-permute-start(bf16[4,2,48,768]{3,2,1,0:T(8,128)(2,1)} %get-tuple-element.235), channel_id=1, source_target_pairs={{0,2},{1,3},{2,0},{3,1},{4,6},{5,7},{6,4},{7,5},{8,10},{9,11},{10,... | collective-permute-start | bytes 1769480 | tf_op jit(solution)/shard_map/ppermute | solution.py:59
  275.3 15.6 %collective-permute-start.50 = (bf16[1,48,1920]{2,1,0:T(8,128)(2,1)S(1)}, bf16[1,48,1920]{2,1,0:T(8,128)(2,1)S(1)}, u32[]{:S(2)}, u32[]{:S(2)}) collective-permute-start(bf16[1,48,1920]{2,1,0:T(8,128)(2,1)S(1)} %get-tuple-element.241), channel_id=1, source_target_pairs={{0,12},{1,13},{2,14},{3,15},{4,8},{5,9},{6,10},{7,11},{8,4},{9,5},... | collective-permute-start | bytes 552968 | tf_op jit(solution)/shard_map/ppermute | solution.py:59
  277.2 15.1 %collective-permute-start.49 = (bf16[1,48,1920]{2,1,0:T(8,128)(2,1)S(1)}, bf16[1,48,1920]{2,1,0:T(8,128)(2,1)S(1)}, u32[]{:S(2)}, u32[]{:S(2)}) collective-permute-start(bf16[1,48,1920]{2,1,0:T(8,128)(2,1)S(1)} %get-tuple-element.240), channel_id=1, source_target_pairs={{0,8},{1,9},{2,10},{3,11},{4,12},{5,13},{6,14},{7,15},{8,0},{9,1},... | collective-permute-start | bytes 552968 | tf_op jit(solution)/shard_map/ppermute | solution.py:59
  277.2 15.1 %collective-permute-start.48 = (bf16[1,48,1920]{2,1,0:T(8,128)(2,1)S(1)}, bf16[1,48,1920]{2,1,0:T(8,128)(2,1)S(1)}, u32[]{:S(2)}, u32[]{:S(2)}) collective-permute-start(bf16[1,48,1920]{2,1,0:T(8,128)(2,1)S(1)} %get-tuple-element.239), channel_id=1, source_target_pairs={{0,4},{1,5},{2,6},{3,7},{4,0},{5,1},{6,2},{7,3},{8,12},{9,13},{10,... | collective-permute-start | bytes 552968 | tf_op jit(solution)/shard_map/ppermute | solution.py:59
  279.7 12.7 %copy-start.25 = (f32[48,1536]{1,0:T(8,128)S(1)}, f32[48,1536]{1,0:T(8,128)}, u32[]{:S(2)}) copy-start(f32[48,1536]{1,0:T(8,128)} %param.26) | copy-start | bytes 884740
  288.8 8.5 %collective-permute-start.43 = (bf16[4,48,768]{2,1,0:T(8,128)(2,1)S(1)}, bf16[4,48,768]{2,1,0:T(8,128)(2,1)S(1)}, u32[]{:S(2)}, u32[]{:S(2)}) collective-permute-start(bf16[4,48,768]{2,1,0:T(8,128)(2,1)S(1)} %get-tuple-element.245), channel_id=1, source_target_pairs={{0,2},{1,3},{2,0},{3,1},{4,6},{5,7},{6,4},{7,5},{8,10},{9,11},{10,... | collective-permute-start | bytes 884744 | tf_op jit(solution)/shard_map/ppermute | solution.py:59
  289.8 8.1 %collective-permute-start.44 = (bf16[4,48,768]{2,1,0:T(8,128)(2,1)S(1)}, bf16[4,48,768]{2,1,0:T(8,128)(2,1)S(1)}, u32[]{:S(2)}, u32[]{:S(2)}) collective-permute-start(bf16[4,48,768]{2,1,0:T(8,128)(2,1)S(1)} %get-tuple-element.246), channel_id=1, source_target_pairs={{0,1},{1,0},{2,3},{3,2},{4,5},{5,4},{6,7},{7,6},{8,9},{9,8},{10,11... | collective-permute-start | bytes 884744 | tf_op jit(solution)/shard_map/ppermute | solution.py:59
  298.7 13.1 %copy-start.5 = (f32[4,48,384]{2,1,0:T(8,128)S(1)}, f32[4,48,384]{2,1,0:T(8,128)}, u32[]{:S(2)}) copy-start(f32[4,48,384]{2,1,0:T(8,128)} %refs_1_.1) | copy-start | bytes 884740
  298.8 13.1 %copy-start.6 = (f32[4,48,384]{2,1,0:T(8,128)S(1)}, f32[4,48,384]{2,1,0:T(8,128)}, u32[]{:S(2)}) copy-start(f32[4,48,384]{2,1,0:T(8,128)} %refs_0_.1) | copy-start | bytes 884740
  298.8 13.1 %copy-start.7 = (f32[4,48,384]{2,1,0:T(8,128)S(1)}, f32[4,48,384]{2,1,0:T(8,128)}, u32[]{:S(2)}) copy-start(f32[4,48,384]{2,1,0:T(8,128)} %refs_2_.1) | copy-start | bytes 884740
  298.8 13.1 %copy-start.8 = (f32[256,48]{0,1:T(8,128)S(1)}, f32[256,48]{0,1:T(8,128)}, u32[]{:S(2)}) copy-start(f32[256,48]{0,1:T(8,128)} %param.37) | copy-start | bytes 147460
  298.8 13.1 %copy-start.9 = (f32[256,48]{0,1:T(8,128)S(1)}, f32[256,48]{0,1:T(8,128)}, u32[]{:S(2)}) copy-start(f32[256,48]{0,1:T(8,128)} %param.38) | copy-start | bytes 147460
  298.8 13.1 %copy-start.10 = (f32[256,48]{0,1:T(8,128)S(1)}, f32[256,48]{0,1:T(8,128)}, u32[]{:S(2)}) copy-start(f32[256,48]{0,1:T(8,128)} %param.39) | copy-start | bytes 147460
  298.8 13.1 %copy-start.11 = (f32[4,48]{1,0:T(4,128)S(1)}, f32[4,48]{1,0:T(4,128)}, u32[]{:S(2)}) copy-start(f32[4,48]{1,0:T(4,128)} %refs_4_.1) | copy-start | bytes 2308
  298.8 13.1 %copy-start.12 = (f32[4,48]{1,0:T(4,128)S(1)}, f32[4,48]{1,0:T(4,128)}, u32[]{:S(2)}) copy-start(f32[4,48]{1,0:T(4,128)} %refs_3_) | copy-start | bytes 2308
  298.8 13.1 %copy-start.13 = (f32[4,48]{1,0:T(4,128)S(1)}, f32[4,48]{1,0:T(4,128)}, u32[]{:S(2)}) copy-start(f32[4,48]{1,0:T(4,128)} %refs_5_) | copy-start | bytes 2308
  298.8 6.3 %collective-permute-start.45 = (bf16[1,48,1536]{2,1,0:T(8,128)(2,1)S(1)}, bf16[1,48,1536]{2,1,0:T(8,128)(2,1)S(1)}, u32[]{:S(2)}, u32[]{:S(2)}) collective-permute-start(bf16[1,48,1536]{2,1,0:T(8,128)(2,1)S(1)} %get-tuple-element.248), channel_id=1, source_target_pairs={{0,4},{1,5},{2,6},{3,7},{4,0},{5,1},{6,2},{7,3},{8,12},{9,13},{10,... | collective-permute-start | bytes 442376 | tf_op jit(solution)/shard_map/ppermute | solution.py:59
  299.1 12.8 %collective-permute-start.46 = (bf16[1,48,1536]{2,1,0:T(8,128)(2,1)S(1)}, bf16[1,48,1536]{2,1,0:T(8,128)(2,1)S(1)}, u32[]{:S(2)}, u32[]{:S(2)}) collective-permute-start(bf16[1,48,1536]{2,1,0:T(8,128)(2,1)S(1)} %get-tuple-element.249), channel_id=1, source_target_pairs={{0,8},{1,9},{2,10},{3,11},{4,12},{5,13},{6,14},{7,15},{8,0},{9,1},... | collective-permute-start | bytes 442376 | tf_op jit(solution)/shard_map/ppermute | solution.py:59
  301.4 10.5 %collective-permute-start.47 = (bf16[1,48,1536]{2,1,0:T(8,128)(2,1)S(1)}, bf16[1,48,1536]{2,1,0:T(8,128)(2,1)S(1)}, u32[]{:S(2)}, u32[]{:S(2)}) collective-permute-start(bf16[1,48,1536]{2,1,0:T(8,128)(2,1)S(1)} %get-tuple-element.250), channel_id=1, source_target_pairs={{0,12},{1,13},{2,14},{3,15},{4,8},{5,9},{6,10},{7,11},{8,4},{9,5},... | collective-permute-start | bytes 442376 | tf_op jit(solution)/shard_map/ppermute | solution.py:59
  (23 other events, 145.4 us)
Sparse Core Ops, SparseCore 0:
  28.6 83.5 all-gather.1
